TPU v7x, 128 devices: a whole 4x4x4 slice. The times are simulated.
128 devices in a mesh: gx: 8 (over x, core), gy: 4 (over y), gz: 4 (over z).
Axes of the slice: x: 4, y: 4, z: 4, core: 2. Of those that a mesh axis runs over, the one named last changes fastest.
Arguments:
- tokens: bfloat16 [16384, 7168], P(('gx', 'gz'), 'gy'), may hold values from -6 to 6
- grad_out: bfloat16 [16384, 7168], P(('gx', 'gz'), 'gy'), may hold values from -6 to 6
- slot_token: int32 [32, 8, 32], P(('gx', 'gz')), may hold values from 0 to 511, as said below
- slot_count: int32 [32, 8], P(('gx', 'gz')), may hold values from 0 to 32, as said below
- slot_score: bfloat16 [32, 8, 32], P(('gx', 'gz')), may hold values from 0.099609375 to 1
- gate_weight: bfloat16 [8, 7168, 2048], P('gx', 'gy', 'gz'), may hold values from -0.0625 to 0.0625
- up_weight: bfloat16 [8, 7168, 2048], P('gx', 'gy', 'gz'), may hold values from -0.0625 to 0.0625
- down_weight: bfloat16 [8, 2048, 7168], P('gx', 'gz', 'gy'), may hold values from -0.125 to 0.125
Outputs:
- input_grad: bfloat16 [16384, 7168], P(('gx', 'gz'), 'gy')
- score_grad: float32 [32, 8, 32], P(('gx', 'gz'))
- gate_grad: bfloat16 [8, 7168, 2048], P('gx', 'gy', 'gz')
- up_grad: bfloat16 [8, 7168, 2048], P('gx', 'gy', 'gz')
- down_grad: bfloat16 [8, 2048, 7168], P('gx', 'gz', 'gy')
Inputs may be any that keep to these rules, and one draw needn't show every extreme that they name: `slot_token`: for each group and expert the 32 indices are distinct. `slot_count`: slots at or beyond the count are not used; their indices and weights play no part.
All inputs are finite; a program needn't handle non-finite values.
Results may differ from a plain program's by a relative error of at most 0.0075.
Values may be sent and summed in bfloat16 or wider, within the bound.
No kernel may reach another device: no remote copies, remote signals or barrier semaphores. Data moves between devices by JAX's collectives and lax.ppermute only.
A program may use at most 128 MiB of HBM per device.

v0:
```python
import jax
import jax.numpy as jnp
from jax import lax
from jax.sharding import PartitionSpec as P


def widen(array, copies):
    shaped = jnp.broadcast_to(array[:, None], (array.shape[0], copies) + array.shape[1:])
    return shaped.reshape((array.shape[0] * copies,) + array.shape[1:])


def activate(gate_value, up_value, pulled, s_rows):
    sigmoid_gate = jax.nn.sigmoid(gate_value)
    activated = gate_value * sigmoid_gate
    hidden = (activated * up_value).astype(jnp.bfloat16)
    score_part = jnp.sum(hidden.astype(jnp.float32) * pulled, axis=1)
    hidden_grad = s_rows[:, None] * pulled
    gate_rows = (
        hidden_grad * up_value * sigmoid_gate * (1.0 + gate_value * (1.0 - sigmoid_gate))
    ).astype(jnp.bfloat16)
    up_rows = (hidden_grad * activated).astype(jnp.bfloat16)
    return (hidden, score_part, gate_rows, up_rows)


def local(
    tokens, grad_out, slot_token, slot_count, slot_score, gate_weight, up_weight, down_weight
):
    gz_count = lax.axis_size("gz")
    chosen = slot_token[0]
    counts = slot_count[0]
    slots = chosen.shape[1]
    width = tokens.shape[1]
    usable = jnp.arange(slots, dtype=jnp.int32)[None, :] < counts[:, None]
    zero_value = jnp.zeros((), tokens.dtype)
    x_sent = jnp.where(usable[..., None], tokens[chosen], zero_value)
    g_sent = jnp.where(usable[..., None], grad_out[chosen], zero_value)
    s_sent = jnp.where(usable, slot_score[0], jnp.zeros((), slot_score.dtype))
    x_in, g_in, s_in = (
        lax.all_to_all(
            widen(x_sent, gz_count), ("gx", "gz"), split_axis=0, concat_axis=0, tiled=True
        ),
        lax.all_to_all(
            widen(g_sent, gz_count), ("gx", "gz"), split_axis=0, concat_axis=0, tiled=True
        ),
        lax.all_to_all(
            widen(s_sent, gz_count), ("gx", "gz"), split_axis=0, concat_axis=0, tiled=True
        ),
    )
    x_rows = x_in.reshape(-1, width)
    g_rows = g_in.reshape(-1, width)
    s_rows = s_in.reshape(-1).astype(jnp.float32)
    w_gate = gate_weight[0]
    w_up = up_weight[0]
    w_down = down_weight[0]
    contract_last = (((1,), (1,)), ((), ()))
    contract_first = (((0,), (0,)), ((), ()))
    gate_part = jnp.dot(x_rows, w_gate, preferred_element_type=jnp.float32)
    up_part = jnp.dot(x_rows, w_up, preferred_element_type=jnp.float32)
    pulled_part = lax.dot_general(g_rows, w_down, contract_last, preferred_element_type=jnp.float32)
    gate_value, up_value, pulled = lax.psum((gate_part, up_part, pulled_part), "gy")
    hidden, score_part, gate_rows, up_rows = activate(gate_value, up_value, pulled, s_rows)
    scaled = (s_rows[:, None] * g_rows.astype(jnp.float32)).astype(jnp.bfloat16)
    down_grad = lax.dot_general(hidden, scaled, contract_first, preferred_element_type=jnp.float32)
    gate_grad = lax.dot_general(
        x_rows, gate_rows, contract_first, preferred_element_type=jnp.float32
    )
    up_grad = lax.dot_general(x_rows, up_rows, contract_first, preferred_element_type=jnp.float32)
    row_part = lax.dot_general(gate_rows, w_gate, contract_last, preferred_element_type=jnp.float32)
    row_part = row_part + lax.dot_general(
        up_rows, w_up, contract_last, preferred_element_type=jnp.float32
    )
    back_rows, back_score = (
        lax.all_to_all(
            row_part.reshape(-1, slots, width),
            ("gx", "gz"),
            split_axis=0,
            concat_axis=0,
            tiled=True,
        ),
        lax.all_to_all(
            score_part.reshape(-1, slots), ("gx", "gz"), split_axis=0, concat_axis=0, tiled=True
        ),
    )
    back_rows = jnp.sum(back_rows.reshape(-1, gz_count, slots, width), axis=1)
    back_score = jnp.sum(back_score.reshape(-1, gz_count, slots), axis=1)
    total = (
        jnp.zeros((tokens.shape[0], width), jnp.float32)
        .at[chosen.reshape(-1)]
        .add(back_rows.reshape(-1, width))
    )
    input_grad = total.astype(jnp.bfloat16)
    score_grad = back_score[None]
    return (
        input_grad,
        score_grad,
        gate_grad.astype(jnp.bfloat16)[None],
        up_grad.astype(jnp.bfloat16)[None],
        down_grad.astype(jnp.bfloat16)[None],
    )


def solution(mesh):
    in_specs = (
        P(("gx", "gz"), "gy"),
        P(("gx", "gz"), "gy"),
        P(("gx", "gz"), None, None),
        P(("gx", "gz"), None),
        P(("gx", "gz"), None, None),
        P("gx", "gy", "gz"),
        P("gx", "gy", "gz"),
        P("gx", "gz", "gy"),
    )
    out_specs = (
        P(("gx", "gz"), "gy"),
        P(("gx", "gz"), None, None),
        P("gx", "gy", "gz"),
        P("gx", "gy", "gz"),
        P("gx", "gz", "gy"),
    )
    return jax.shard_map(local, mesh=mesh, in_specs=in_specs, out_specs=out_specs, check_vma=False)
```

profile of v0, /device:TPU:1, one launch (start us, length us, event | category | flops | bytes accessed | tf_op | source)
XLA Modules:
  0.0 400.3 jit_solution(1573636227464543132)
XLA Ops:
  7.2 0.9 iota_compare_fusion
  8.0 0.7 compare_select_fusion
  8.7 0.1 reshape.173
  8.8 3.9 gather_fusion.1
  12.7 4.8 %gather_fusion = bf16[256,1792]{1,0:T(8,128)(2,1)} fusion(bf16[512,1792]{1,0:T(8,128)(2,1)} %param.9, s32[1024]{0:T(1024)S(1)} %pad_clamp_fusion), kind=kCustom, calls=%fused_computation | custom fusion | bytes 1836032 | tf_op jit(solution)/shard_map/gather | solution.py:36
  17.5 1.4 broadcast_select_fusion.1
  18.9 0.4 broadcast_in_dim.67
  19.3 54.3 %all_to_all.33 = bf16[32,32,1792]{2,1,0:T(8,128)(2,1)} all-to-all(bf16[32,32,1792]{2,1,0:T(8,128)(2,1)S(1)} %bitcast.52), channel_id=1, replica_groups=mesh['gx'=8,'gy'=4,'gz'=4] {'gx','gz'}, dimensions={0} | all-to-all | bytes 7340032 | tf_op jit(solution)/shard_map/all_to_all | solution.py:39
  73.6 2.2 broadcast_in_dim.66
  75.8 5.5 %all-to-all-start.1 = ((bf16[32,32,1792]{2,1,0:T(8,128)(2,1)}), bf16[32,32,1792]{2,1,0:T(8,128)(2,1)}, u32[]{:S(2)}, u32[]{:S(2)}) async-start(bf16[32,32,1792]{2,1,0:T(8,128)(2,1)} %bitcast.51), calls=%async_computation.1 | async-start | bytes 7340032 | tf_op jit(solution)/shard_map/all_to_all | solution.py:42
  81.4 5.6 %fusion.9 = f32[1024,512]{1,0:T(8,128)} fusion(bf16[1024,1792]{1,0:T(8,128)(2,1)} %bitcast.55, bf16[1,1792,512]{2,1,0:T(8,128)(2,1)S(1)} %copy-done), kind=kOutput, calls=%fused_computation.22 | convolution fusion | flops 1879048192 | bytes 7602176 | tf_op jit(solution)/shard_map/dot_general | solution.py:57
  87.0 3.4 fusion.12
  90.4 35.4 %all-to-all-done.1 = bf16[32,32,1792]{2,1,0:T(8,128)(2,1)} async-done(((bf16[32,32,1792]{2,1,0:T(8,128)(2,1)}), bf16[32,32,1792]{2,1,0:T(8,128)(2,1)}, u32[]{:S(2)}, u32[]{:S(2)}) %all-to-all-start.1) | async-done | bytes 3670048 | tf_op jit(solution)/shard_map/all_to_all | solution.py:42
  125.8 6.1 %fusion.14 = f32[1024,512]{1,0:T(8,128)} fusion(bf16[1024,1792]{1,0:T(8,128)(2,1)} %bitcast.7, bf16[1,512,1792]{2,1,0:T(8,128)(2,1)} %param.15), kind=kOutput, calls=%fused_computation.27 | convolution fusion | flops 1879048192 | bytes 7602176 | tf_op jit(solution)/shard_map/dot_general | solution.py:59
  131.9 0.7 copy-done.9
  132.7 14.1 %all_to_all.34 = bf16[32,1,32]{2,1,0:T(2,128)(2,1)S(1)} all-to-all(bf16[32,1,32]{2,1,0:T(2,128)(2,1)S(1)} %copy.17), channel_id=1, replica_groups=mesh['gx'=8,'gy'=4,'gz'=4] {'gx','gz'}, dimensions={0} | all-to-all | bytes 4096 | tf_op jit(solution)/shard_map/all_to_all | solution.py:45
  146.9 113.5 %all-reduce.3.cloned.1.call-done = (f32[1024,512]{1,0:T(8,128)}, f32[1024,512]{1,0:T(8,128)}, f32[1024,512]{1,0:T(8,128)}) async-done(((f32[1024,512]{1,0:T(8,128)}, f32[1024,512]{1,0:T(8,128)}, f32[1024,512]{1,0:T(8,128)}), (f32[1024,512]{1,0:T(8,128)}, f32[1024,512]{1,0:T(8,128)}, f32[1024,512]{1,0:T(8,128)})) %all-reduce.3.cloned.1.call-update) | async-done | bytes 6291472 | tf_op jit(solution)/shard_map/psum | solution.py:60
  260.5 4.6 %multiply_reduce_fusion = (f32[1024]{0:T(1024)S(1)}, bf16[1024,512]{1,0:T(8,128)(2,1)}, bf16[1024,512]{1,0:T(8,128)(2,1)}, bf16[1024,512]{1,0:T(8,128)(2,1)S(1)}) fusion(f32[1024,512]{1,0:T(8,128)} %get-tuple-element.7, f32[1024,512]{1,0:T(8,128)} %get-tuple-element.6, f32[1024,512]{1,0:T(8,128)} %get-tuple-element.5, f32[1024]{0:T(1024)S(1)} %reshape.170), kind=kLoop, calls=%fused_computation.14 | loop fusion | flops 9960448 | bytes 9445376 | tf_op jit(solution)/shard_map/reduce_sum | solution.py:16
  265.1 0.7 all_to_all.26
  265.8 7.7 %all-to-all-start.4 = ((f32[32,1,32]{2,1,0:T(1,128)}), f32[32,1,32]{2,1,0:T(1,128)S(1)}, u32[]{:S(2)}, u32[]{:S(2)}) async-start(f32[32,1,32]{2,1,0:T(1,128)} %all_to_all.26), calls=%async_computation.4 | async-start | bytes 32768 | tf_op jit(solution)/shard_map/all_to_all | solution.py:80
  273.5 3.5 fusion.7
  277.0 5.3 %convolution_add_fusion = f32[1024,1792]{1,0:T(8,128)} fusion(f32[1024,1792]{1,0:T(8,128)S(1)} %fusion.7, bf16[1024,512]{1,0:T(8,128)(2,1)S(1)} %get-tuple-element.11, bf16[1,1792,512]{2,1,0:T(8,128)(2,1)S(1)} %copy-done.5), kind=kOutput, calls=%fused_computation.5 | convolution fusion | flops 1880883200 | bytes 17563648 | tf_op jit(solution)/shard_map/dot_general | solution.py:69
  282.3 7.6 %all-to-all-start.3 = ((f32[32,32,1792]{2,1,0:T(8,128)}), f32[32,32,1792]{2,1,0:T(8,128)}, u32[]{:S(2)}, u32[]{:S(2)}) async-start(f32[32,32,1792]{2,1,0:T(8,128)} %bitcast.50), calls=%async_computation.3 | async-start | bytes 14680064 | tf_op jit(solution)/shard_map/all_to_all | solution.py:73
  289.8 0.1 reshape_squeeze.3
  289.9 5.5 %fusion.4 = bf16[1,1792,512]{2,1,0:T(8,128)(2,1)} fusion(bf16[1024,1792]{1,0:T(8,128)(2,1)} %bitcast.56, bf16[1024,512]{1,0:T(8,128)(2,1)S(1)} %copy-done.7), kind=kOutput, calls=%fused_computation.12 | convolution fusion | flops 1879965696 | bytes 6553600 | tf_op jit(solution)/shard_map/dot_general | solution.py:64
  295.5 3.4 fusion.5
  298.8 5.6 %fusion.3 = bf16[1,512,1792]{2,1,0:T(8,128)(2,1)} fusion(bf16[1024,512]{1,0:T(8,128)(2,1)S(1)} %copy-done.6, bf16[1024,1792]{1,0:T(8,128)(2,1)} %bitcast.7, f32[1024]{0:T(1024)S(1)} %reshape.170), kind=kOutput, calls=%fused_computation.11 | convolution fusion | flops 1885470720 | bytes 6557696 | tf_op jit(solution)/shard_map/dot_general | solution.py:63
  304.4 0.6 reduce_sum.29
  305.0 73.6 %all-to-all-done.3 = f32[32,32,1792]{2,1,0:T(8,128)} async-done(((f32[32,32,1792]{2,1,0:T(8,128)}), f32[32,32,1792]{2,1,0:T(8,128)}, u32[]{:S(2)}, u32[]{:S(2)}) %all-to-all-start.3) | async-done | bytes 7340064 | tf_op jit(solution)/shard_map/all_to_all | solution.py:73
  378.6 5.0 %bitcast_reduce_fusion = f32[8,32,1792]{2,1,0:T(8,128)} fusion(f32[32,32,1792]{2,1,0:T(8,128)} %all-to-all-done.3), kind=kLoop, calls=%fused_computation.3 | loop fusion | flops 1376256 | bytes 9175040 | tf_op jit(solution)/shard_map/reduce_sum | solution.py:84
  383.5 6.5 %scatter_custom_fusion = f32[512,1792]{1,0:T(8,128)} fusion(s32[256]{0:T(256)S(1)} %bitcast.63, f32[256,1792]{1,0:T(8,128)} %bitcast.59, f32[]{:T(128)} %constant.5.clone.1), kind=kCustom, calls=%fused_computation.29 | custom fusion | flops 458752 | bytes 3670528 | tf_op jit(solution)/shard_map/scatter-add | solution.py:89
  390.0 3.4 convert_element_type.44
  (31 shorter events, 0.3 us)
Async XLA Ops:
  7.2 74.2 %copy-start = (bf16[1,1792,512]{2,1,0:T(8,128)(2,1)S(1)}, bf16[1,1792,512]{2,1,0:T(8,128)(2,1)}, u32[]{:S(2)}) copy-start(bf16[1,1792,512]{2,1,0:T(8,128)(2,1)} %param.13) | copy-start | bytes 5505028
  75.8 50.0 %all-to-all-start.1 = ((bf16[32,32,1792]{2,1,0:T(8,128)(2,1)}), bf16[32,32,1792]{2,1,0:T(8,128)(2,1)}, u32[]{:S(2)}, u32[]{:S(2)}) async-start(bf16[32,32,1792]{2,1,0:T(8,128)(2,1)} %bitcast.51), calls=%async_computation.1 | async-start | bytes 7340032 | tf_op jit(solution)/shard_map/all_to_all | solution.py:42
  81.3 179.1 %all-reduce.3.cloned.1.call-start = ((), (), s32[]{:S(2)}) async-start(), calls=%async_computation.5 | async-start | bytes 12582912 | tf_op jit(solution)/shard_map/psum | solution.py:60
  81.4 5.6 %copy-start.2 = (bf16[32,32,1792]{2,1,0:T(8,128)(2,1)S(1)}, bf16[32,32,1792]{2,1,0:T(8,128)(2,1)}, u32[]{:S(2)}) copy-start(bf16[32,32,1792]{2,1,0:T(8,128)(2,1)} %all_to_all.33) | copy-start | bytes 11010052
  81.4 5.6 %copy-start.4 = (bf16[1,1792,512]{2,1,0:T(8,128)(2,1)S(1)}, bf16[1,1792,512]{2,1,0:T(8,128)(2,1)}, u32[]{:S(2)}) copy-start(bf16[1,1792,512]{2,1,0:T(8,128)(2,1)} %param.14) | copy-start | bytes 5505028
  131.9 0.7 copy-start.9
  131.9 0.7 copy-start.10
  265.8 16.5 %all-to-all-start.4 = ((f32[32,1,32]{2,1,0:T(1,128)}), f32[32,1,32]{2,1,0:T(1,128)S(1)}, u32[]{:S(2)}, u32[]{:S(2)}) async-start(f32[32,1,32]{2,1,0:T(1,128)} %all_to_all.26), calls=%async_computation.4 | async-start | bytes 32768 | tf_op jit(solution)/shard_map/all_to_all | solution.py:80
  273.5 3.5 copy-start.5
  282.3 7.6 %copy-start.8 = (s32[1,8,32]{2,1,0:T(8,128)S(1)}, s32[1,8,32]{2,1,0:T(8,128)}, u32[]{:S(2)}) copy-start(s32[1,8,32]{2,1,0:T(8,128)} %param.10) | copy-start | bytes 3076
  282.3 7.7 %copy-start.7 = (bf16[1024,512]{1,0:T(8,128)(2,1)S(1)}, bf16[1024,512]{1,0:T(8,128)(2,1)}, u32[]{:S(2)}) copy-start(bf16[1024,512]{1,0:T(8,128)(2,1)} %get-tuple-element.10) | copy-start | bytes 3145732
  282.3 96.3 %all-to-all-start.3 = ((f32[32,32,1792]{2,1,0:T(8,128)}), f32[32,32,1792]{2,1,0:T(8,128)}, u32[]{:S(2)}, u32[]{:S(2)}) async-start(f32[32,32,1792]{2,1,0:T(8,128)} %bitcast.50), calls=%async_computation.3 | async-start | bytes 14680064 | tf_op jit(solution)/shard_map/all_to_all | solution.py:73
  289.9 5.5 %copy-start.3 = (bf16[32,32,1792]{2,1,0:T(8,128)(2,1)S(1)}, bf16[32,32,1792]{2,1,0:T(8,128)(2,1)}, u32[]{:S(2)}) copy-start(bf16[32,32,1792]{2,1,0:T(8,128)(2,1)} %all_to_all.33) | copy-start | bytes 11010052
  295.5 3.4 copy-start.6
  383.5 9.9 %copy-start.1 = (bf16[1,1792,512]{2,1,0:T(8,128)(2,1)S(1)}, bf16[1,1792,512]{2,1,0:T(8,128)(2,1)}, u32[]{:S(2)}) copy-start(bf16[1,1792,512]{2,1,0:T(8,128)(2,1)} %param.13) | copy-start | bytes 5505028
Sparse Core Ops, SparseCore 0:
  132.0 128.3 all-reduce.2
where the time goes:
time: 405 us; the launch traced here: 400 us
  waiting for transfers between devices  223 us (55%)
  blocking collectives  68.4 us (17%)
  matrix products  38.2 us (9%)
  other arithmetic  23.2 us (6%)
  starting transfers between devices  20.8 us (5%)
  between operations  14.2 us (4%)
  local copies, waits for them, and re-layouts  13 us (3%)
    psum x1, waiting for transfers between devices, local(): lax.psum((gate_part, up_part, pulled_part), 'gy')  114 us
    all_to_all x1, waiting for transfers between devices, local(): lax.all_to_all(row_part.reshape(-1, slots, width), ('gx', 'gz'), split_ax...  73.6 us
    all_to_all x1, blocking collectives, local(): lax.all_to_all(widen(x_sent, gz_count), ('gx', 'gz'), split_axis=0, conca...  54.3 us
    all_to_all x1, waiting for transfers between devices, local(): lax.all_to_all(widen(g_sent, gz_count), ('gx', 'gz'), split_axis=0, conca...  35.4 us
    all_to_all x1, blocking collectives, local(): lax.all_to_all(widen(s_sent, gz_count), ('gx', 'gz'), split_axis=0, conca...  14.1 us
  transfers between devices with their start and end apart: 4, of which 3 were waited for; matrix products, arithmetic and copies ran while one was open for 8% of the time, Pallas kernels for 0%

commit v1 on v0

v1 whole, which is shorter than its diff:
```python
import jax
import jax.numpy as jnp
from jax import lax
from jax.sharding import PartitionSpec as P

CONTRACT_LAST = (((1,), (1,)), ((), ()))
CONTRACT_FIRST = (((0,), (0,)), ((), ()))


def dot(left, right, dims=(((1,), (0,)), ((), ()))):
    return lax.dot_general(left, right, dims, preferred_element_type=jnp.float32)


def shift(array, steps):
    size = lax.axis_size("gz")
    return lax.ppermute(array, "gz", [(i, (i + steps) % size) for i in range(size)])


def ring_gather(own):
    half = own.shape[0] // 2
    before = shift(own, 1)
    after = shift(own, -1)
    far_top = shift(before[:half], 1)
    far_bottom = shift(after[half:], -1)
    return jnp.concatenate([own, before, after, far_top, far_bottom])


def activate(gate_value, up_value, hidden_grad):
    sigmoid_gate = jax.nn.sigmoid(gate_value)
    activated = gate_value * sigmoid_gate
    hidden = (activated * up_value).astype(jnp.bfloat16)
    score_part = jnp.sum(hidden.astype(jnp.float32) * hidden_grad, axis=1)
    gate_rows = (
        hidden_grad * up_value * sigmoid_gate * (1.0 + gate_value * (1.0 - sigmoid_gate))
    ).astype(jnp.bfloat16)
    up_rows = (hidden_grad * activated).astype(jnp.bfloat16)
    return hidden, score_part, gate_rows, up_rows


def local(
    tokens, grad_out, slot_token, slot_count, slot_score, gate_weight, up_weight, down_weight
):
    bf16 = jnp.bfloat16
    chosen = slot_token[0]
    counts = slot_count[0]
    experts, slots = chosen.shape
    group, width = tokens.shape
    usable = jnp.arange(slots, dtype=jnp.int32)[None, :] < counts[:, None]
    score = slot_score[0]
    picked = (
        chosen[:, :, None] == jnp.arange(group, dtype=jnp.int32)[None, None, :]
    ) & usable[:, :, None]
    zero = jnp.zeros((), bf16)
    pick = jnp.where(picked, jnp.ones((), bf16), zero).reshape(experts * slots, group)
    pick_scaled = jnp.where(picked, score[:, :, None], zero).reshape(experts * slots, group)

    w_cat = jnp.concatenate([gate_weight[0], up_weight[0]], axis=1)
    w_down = down_weight[0]
    hidden_units = w_down.shape[0]

    def to_expert(rows):
        return lax.all_to_all(rows, "gx", split_axis=0, concat_axis=0, tiled=True)

    x_own = to_expert(dot(pick, tokens).astype(bf16))
    g_own = to_expert(dot(pick_scaled, grad_out).astype(bf16))
    x_rows = ring_gather(x_own)
    gate_up = lax.psum(dot(x_rows, w_cat).astype(bf16), "gy")
    g_rows = ring_gather(g_own)
    pulled_part = dot(g_rows, w_down, CONTRACT_LAST).astype(bf16)
    gate_up, pulled_part = lax.optimization_barrier((gate_up, pulled_part))
    gate_up = gate_up.astype(jnp.float32)
    pulled = lax.psum(pulled_part, "gy").astype(jnp.float32)
    hidden, score_part, gate_rows, up_rows = activate(
        gate_up[:, :hidden_units], gate_up[:, hidden_units:], pulled
    )
    both_rows = jnp.concatenate([gate_rows, up_rows], axis=1)
    row_part = dot(both_rows, w_cat, CONTRACT_LAST)
    own_rows = x_own.shape[0]

    def piece(k):
        return row_part[k * own_rows : (k + 1) * own_rows]

    f32 = jnp.float32
    total = piece(0)
    total = total + shift(piece(3).astype(bf16), 2).astype(f32)
    total = total + shift(piece(1).astype(bf16), -1).astype(f32)
    total = total + shift(piece(2).astype(bf16), 1).astype(f32)
    back_rows = to_expert(total.astype(bf16))
    input_grad = dot(pick, back_rows, CONTRACT_FIRST).astype(bf16)

    gate_grad = dot(x_rows, gate_rows, CONTRACT_FIRST).astype(bf16)
    up_grad = dot(x_rows, up_rows, CONTRACT_FIRST).astype(bf16)
    down_grad = dot(hidden, g_rows, CONTRACT_FIRST).astype(bf16)

    gz = lax.axis_index("gz")
    gz_count = lax.axis_size("gz")
    relative = score_part.reshape(gz_count, -1)
    place = lax.rem(gz - jnp.arange(gz_count) + gz_count, gz_count)
    order = jnp.array([0, 1, 3, 2], jnp.int32)
    match = place[:, None] == order[None, :]
    absolute = jnp.sum(jnp.where(match[:, :, None], relative[None], 0.0), axis=1)
    absolute = absolute.reshape(gz_count, -1, slots).transpose(1, 0, 2).reshape(-1, slots)
    back_score = lax.all_to_all(absolute, ("gx", "gz"), split_axis=0, concat_axis=0, tiled=True)
    back_score = jnp.sum(back_score.reshape(experts, gz_count, slots), axis=1)
    score_grad = jnp.where(usable, back_score / score.astype(f32), 0.0)[None]
    return input_grad, score_grad, gate_grad[None], up_grad[None], down_grad[None]


def solution(mesh):
    in_specs = (
        P(("gx", "gz"), "gy"),
        P(("gx", "gz"), "gy"),
        P(("gx", "gz"), None, None),
        P(("gx", "gz"), None),
        P(("gx", "gz"), None, None),
        P("gx", "gy", "gz"),
        P("gx", "gy", "gz"),
        P("gx", "gz", "gy"),
    )
    out_specs = (
        P(("gx", "gz"), "gy"),
        P(("gx", "gz"), None, None),
        P("gx", "gy", "gz"),
        P("gx", "gy", "gz"),
        P("gx", "gz", "gy"),
    )
    return jax.shard_map(local, mesh=mesh, in_specs=in_specs, out_specs=out_specs, check_vma=False)
```

time: 405 us -> 295 us (0.73)
  blocking collectives: 68.4 us -> 0 us
  waiting for transfers between devices: 223 us -> 168 us
  starting transfers between devices: 20.8 us -> 40.8 us
  other arithmetic: 23.2 us -> 13.3 us
  local copies, waits for them, and re-layouts: 13 us -> 18.6 us
    all_to_all x3 -> x4, waiting for transfers between devices: 109 us -> 24.3 us  [the longest x3 24.3 us: to_expert(): return lax.all_to_all(rows, 'gx', split_axis=0, concat_axis=0, tiled=True)]
    all_to_all x2 -> x0, blocking collectives: 68.4 us -> none  [the longest x1 54.3 us: local(): lax.all_to_all(widen(x_sent, gz_count), ('gx', 'gz'), split_axis=0, conca...]
    ppermute x0 -> x11, waiting for transfers between devices: none -> 62 us  [shift(): lax.ppermute(array, 'gz', [(i, (i + steps) % size) for i in range(size)])]
    psum x1 -> x2, waiting for transfers between devices: 114 us -> 82.1 us  [the longest x1 43.2 us: local(): pulled = lax.psum(pulled_part, 'gy').astype(jnp.float32)]
    ppermute x0 -> x11, starting transfers between devices: none -> 18.2 us  [shift(): lax.ppermute(array, 'gz', [(i, (i + steps) % size) for i in range(size)])]
    unnamed x22 -> x38, local copies, waits for them, and re-layouts: 0.71 us -> 11.1 us
    gather x2 -> x0, local copies, waits for them, and re-layouts: 8.7 us -> none  [the longest x1 4.81 us: local(): g_sent = jnp.where(usable[..., None], grad_out[chosen], zero_value)]
    scatter-add x1 -> x0, other arithmetic: 6.48 us -> none  [local(): total = jnp.zeros((tokens.shape[0], width), jnp.float32).at[chosen.reshap...]
  transfers between devices with their start and end apart: 4 -> 17, of which waited for: 3 -> 10; matrix products, arithmetic and copies ran while one was open for 8% -> 16% of each run, Pallas kernels for 0% -> 0%
where the time goes in v1:
time: 295 us; the launch traced here: 294 us
  waiting for transfers between devices  168 us (57%)
  starting transfers between devices  40.8 us (14%)
  matrix products  38.9 us (13%)
  local copies, waits for them, and re-layouts  18.6 us (6%)
  between operations  14.3 us (5%)
  other arithmetic  13.3 us (5%)
    ppermute x11, waiting for transfers between devices, shift(): lax.ppermute(array, 'gz', [(i, (i + steps) % size) for i in range(size)])  62 us
    psum x1, waiting for transfers between devices, local(): pulled = lax.psum(pulled_part, 'gy').astype(jnp.float32)  43.2 us
    psum x1, waiting for transfers between devices, local(): gate_up = lax.psum(dot(x_rows, w_cat).astype(bf16), 'gy')  38.9 us
    dot_general x9, matrix products, dot(): lax.dot_general(left, right, dims, preferred_element_type=jnp.float32)  38.9 us
    all_to_all x3, waiting for transfers between devices, to_expert(): return lax.all_to_all(rows, 'gx', split_axis=0, concat_axis=0, tiled=True)  24.3 us
    ppermute x11, starting transfers between devices, shift(): lax.ppermute(array, 'gz', [(i, (i + steps) % size) for i in range(size)])  18.2 us
    all_to_all x3, starting transfers between devices, to_expert(): return lax.all_to_all(rows, 'gx', split_axis=0, concat_axis=0, tiled=True)  15.2 us
    unnamed x38, local copies, waits for them, and re-layouts  11.1 us
  transfers between devices with their start and end apart: 17, of which 10 were waited for; matrix products, arithmetic and copies ran while one was open for 16% of the time, Pallas kernels for 0%

profile of v1, /device:TPU:1, one launch (start us, length us, event | category | flops | bytes accessed | tf_op | source)
XLA Modules:
  0.0 294.3 jit_solution(10393292483426969793)
XLA Ops:
  8.9 3.1 %convolution_convert_fusion.4 = bf16[256,1792]{1,0:T(8,128)(2,1)} fusion(bf16[512,1792]{1,0:T(8,128)(2,1)} %param.9, s32[256]{0:T(256)S(1)} %eq.46, pred[256]{0:T(512)(128)(4,1)S(1)} %lt.40), kind=kOutput, calls=%fused_computation.12 | convolution fusion | flops 470614016 | bytes 2753792 | tf_op jit(solution)/shard_map/dot_general | solution.py:11
  12.0 5.8 %all-to-all-start = ((bf16[8,32,1792]{2,1,0:T(8,128)(2,1)}), bf16[8,32,1792]{2,1,0:T(8,128)(2,1)S(1)}, u32[]{:S(2)}, u32[]{:S(2)}) async-start(bf16[8,32,1792]{2,1,0:T(8,128)(2,1)} %bitcast.49), calls=%async_computation | async-start | bytes 1835008 | tf_op jit(solution)/shard_map/all_to_all | solution.py:62
  17.9 3.1 %convolution_convert_fusion.3 = bf16[256,1792]{1,0:T(8,128)(2,1)} fusion(bf16[512,1792]{1,0:T(8,128)(2,1)} %param.10, s32[256]{0:T(256)S(1)} %eq.46, pred[256]{0:T(512)(128)(4,1)S(1)} %lt.40, bf16[256]{0:T(256)(128)(2,1)S(1)} %broadcast_in_dim.70), kind=kOutput, calls=%fused_computation.11 | convolution fusion | flops 470614016 | bytes 2754304 | tf_op jit(solution)/shard_map/dot_general | solution.py:11
  21.1 10.5 %all-to-all-done = bf16[8,32,1792]{2,1,0:T(8,128)(2,1)S(1)} async-done(((bf16[8,32,1792]{2,1,0:T(8,128)(2,1)}), bf16[8,32,1792]{2,1,0:T(8,128)(2,1)S(1)}, u32[]{:S(2)}, u32[]{:S(2)}) %all-to-all-start) | async-done | bytes 917536 | tf_op jit(solution)/shard_map/all_to_all | solution.py:62
  32.5 4.3 %all-to-all-start.1 = ((bf16[8,32,1792]{2,1,0:T(8,128)(2,1)}), bf16[8,32,1792]{2,1,0:T(8,128)(2,1)S(1)}, u32[]{:S(2)}, u32[]{:S(2)}) async-start(bf16[8,32,1792]{2,1,0:T(8,128)(2,1)} %bitcast.48), calls=%async_computation.1 | async-start | bytes 1835008 | tf_op jit(solution)/shard_map/all_to_all | solution.py:62
  36.8 3.8 %collective-permute-start.1 = (bf16[256,1792]{1,0:T(8,128)(2,1)}, bf16[256,1792]{1,0:T(8,128)(2,1)}, u32[]{:S(2)}, u32[]{:S(2)}) collective-permute-start(bf16[256,1792]{1,0:T(8,128)(2,1)} %bitcast.45), channel_id=1, source_target_pairs={{0,3},{1,0},{2,1},{3,2},{4,7},{5,4},{6,5},{7,6},{8,11},{9,8},{10,9... | collective-permute-start | bytes 2752520 | tf_op jit(solution)/shard_map/ppermute | solution.py:16
  40.5 9.9 %all-to-all-done.1 = bf16[8,32,1792]{2,1,0:T(8,128)(2,1)S(1)} async-done(((bf16[8,32,1792]{2,1,0:T(8,128)(2,1)}), bf16[8,32,1792]{2,1,0:T(8,128)(2,1)S(1)}, u32[]{:S(2)}, u32[]{:S(2)}) %all-to-all-start.1) | async-done | bytes 917536 | tf_op jit(solution)/shard_map/all_to_all | solution.py:62
  50.5 3.8 %collective-permute-start.5 = (bf16[256,1792]{1,0:T(8,128)(2,1)S(1)}, bf16[256,1792]{1,0:T(8,128)(2,1)}, u32[]{:S(2)}, u32[]{:S(2)}) collective-permute-start(bf16[256,1792]{1,0:T(8,128)(2,1)S(1)} %bitcast.42), channel_id=1, source_target_pairs={{0,3},{1,0},{2,1},{3,2},{4,7},{5,4},{6,5},{7,6},{8,11},{9,8},{10,9... | collective-permute-start | bytes 2752520 | tf_op jit(solution)/shard_map/ppermute | solution.py:16
  55.5 4.9 %collective-permute-done.1 = bf16[256,1792]{1,0:T(8,128)(2,1)} collective-permute-done((bf16[256,1792]{1,0:T(8,128)(2,1)}, bf16[256,1792]{1,0:T(8,128)(2,1)}, u32[]{:S(2)}, u32[]{:S(2)}) %collective-permute-start.1) | collective-permute-done | bytes 917536 | tf_op jit(solution)/shard_map/ppermute | solution.py:16
  61.4 3.5 %collective-permute-start.3 = (bf16[128,1792]{1,0:T(8,128)(2,1)S(1)}, bf16[128,1792]{1,0:T(8,128)(2,1)S(1)}, u32[]{:S(2)}, u32[]{:S(2)}) collective-permute-start(bf16[128,1792]{1,0:T(8,128)(2,1)S(1)} %slice.44), channel_id=1, source_target_pairs={{0,3},{1,0},{2,1},{3,2},{4,7},{5,4},{6,5},{7,6},{8,11},{9,8},{10,9... | collective-permute-start | bytes 1376264 | tf_op jit(solution)/shard_map/ppermute | solution.py:16
  68.6 24.3 %collective-permute-done.2 = bf16[128,1792]{1,0:T(8,128)(2,1)S(1)} collective-permute-done((bf16[128,1792]{1,0:T(8,128)(2,1)S(1)}, bf16[128,1792]{1,0:T(8,128)(2,1)S(1)}, u32[]{:S(2)}, u32[]{:S(2)}) %collective-permute-start.2) | collective-permute-done | bytes 458784 | tf_op jit(solution)/shard_map/ppermute | solution.py:16
  93.0 1.9 copy-done.4
  94.9 5.4 %fusion.14 = bf16[1024,1024]{1,0:T(8,128)(2,1)} fusion(bf16[1024,1792]{1,0:T(8,128)(2,1)S(1)} %constant_dynamic-update-slice_fusion, bf16[1792,512]{1,0:T(8,128)(2,1)S(1)} %bitcast.55, bf16[1792,512]{1,0:T(8,128)(2,1)S(1)} %bitcast.57), kind=kOutput, calls=%fused_computation.26 | convolution fusion | flops 3766484992 | bytes 9437184 | tf_op jit(solution)/shard_map/dot_general | solution.py:11
  106.6 8.3 %collective-permute-done.6 = bf16[128,1792]{1,0:T(8,128)(2,1)S(1)} collective-permute-done((bf16[128,1792]{1,0:T(8,128)(2,1)S(1)}, bf16[128,1792]{1,0:T(8,128)(2,1)S(1)}, u32[]{:S(2)}, u32[]{:S(2)}) %collective-permute-start.6) | collective-permute-done | bytes 458784 | tf_op jit(solution)/shard_map/ppermute | solution.py:16
  116.9 3.1 %fusion.20 = bf16[1024,512]{1,0:T(8,128)(2,1)} fusion(bf16[1024,1792]{1,0:T(8,128)(2,1)S(1)} %constant_dynamic-update-slice_fusion.5, bf16[1,512,1792]{2,1,0:T(8,128)(2,1)S(1)} %copy-done), kind=kOutput, calls=%fused_computation.33 | convolution fusion | flops 1879572480 | bytes 6553600 | tf_op jit(solution)/shard_map/dot_general | solution.py:11
  120.0 38.9 %all-reduce.3.cloned.1.call-done = bf16[1024,1024]{1,0:T(8,128)(2,1)} async-done(((bf16[1024,1024]{1,0:T(8,128)(2,1)}), bf16[1024,1024]{1,0:T(8,128)(2,1)}) %all-reduce.3.cloned.1.call-update) | async-done | bytes 2097168 | tf_op jit(solution)/shard_map/psum | solution.py:67
  158.9 4.0 %convert_element_type.66 = f32[1024,1024]{1,0:T(8,128)} convert(bf16[1024,1024]{1,0:T(8,128)(2,1)} %all-reduce.3.cloned.1.call-done) | non-fusion elementwise | flops 1048576 | bytes 6291456 | tf_op jit(solution)/shard_map/convert_element_type | solution.py:71
  162.9 43.2 %all-reduce.5.cloned.1.call-done = bf16[1024,512]{1,0:T(8,128)(2,1)} async-done(((bf16[1024,512]{1,0:T(8,128)(2,1)}), bf16[1024,512]{1,0:T(8,128)(2,1)}) %all-reduce.5.cloned.1.call-update) | async-done | bytes 1048592 | tf_op jit(solution)/shard_map/psum | solution.py:72
  206.1 4.0 %fusion.9 = (f32[1024]{0:T(1024)S(1)}, bf16[1024,512]{1,0:T(8,128)(2,1)S(1)}, bf16[1024,512]{1,0:T(8,128)(2,1)S(1)}, bf16[1024,512]{1,0:T(8,128)(2,1)S(1)}) fusion(bf16[1024,512]{1,0:T(8,128)(2,1)} %all-reduce.5.cloned.1.call-done, f32[1024,1024]{1,0:T(8,128)} %convert_element_type.66), kind=kLoop, calls=%fused_computation.19 | loop fusion | flops 9960448 | bytes 8392704 | tf_op jit(solution)/shard_map/reduce_sum | solution.py:32
  210.2 6.1 %fusion.53 = (bf16[1024,1792]{1,0:T(8,128)(2,1)S(1)}, f32[1024,1792]{1,0:T(8,128)}) fusion(bf16[1792,512]{1,0:T(8,128)(2,1)S(1)} %bitcast.56, bf16[1792,512]{1,0:T(8,128)(2,1)S(1)} %bitcast.58, bf16[1024,512]{1,0:T(8,128)(2,1)S(1)} %get-tuple-element.11, bf16[1024,512]{1,0:T(8,128)(2,1)S(1)} %get-tuple-element.12), kind=kOutput, calls=%fused_computation.80 | convolution fusion | flops 3771465728 | bytes 16777216 | tf_op jit(solution)/shard_map/dot_general | solution.py:11
  217.9 2.9 collective-permute-start.8
  221.1 2.3 collective-permute-start.9
  224.3 7.3 %all-to-all-start.3 = ((f32[32,1,32]{2,1,0:T(1,128)}), f32[32,1,32]{2,1,0:T(1,128)S(1)}, u32[]{:S(2)}, u32[]{:S(2)}) async-start(f32[32,1,32]{2,1,0:T(1,128)} %bitcast.13), calls=%async_computation.3 | async-start | bytes 32768 | tf_op jit(solution)/shard_map/all_to_all | solution.py:103
  231.6 5.7 %fusion.1 = bf16[1,1792,512]{2,1,0:T(8,128)(2,1)} fusion(bf16[1024,1792]{1,0:T(8,128)(2,1)} %copy-done.4, bf16[1024,512]{1,0:T(8,128)(2,1)} %copy-done.3), kind=kOutput, calls=%fused_computation.9 | convolution fusion | flops 1879965696 | bytes 6553600 | tf_op jit(solution)/shard_map/dot_general | solution.py:11
  237.3 2.3 collective-permute-done.8
  239.6 22.1 %collective-permute-done.10 = bf16[256,1792]{1,0:T(8,128)(2,1)} collective-permute-done((bf16[256,1792]{1,0:T(8,128)(2,1)}, bf16[256,1792]{1,0:T(8,128)(2,1)}, u32[]{:S(2)}, u32[]{:S(2)}) %collective-permute-start.10) | collective-permute-done | bytes 917536 | tf_op jit(solution)/shard_map/ppermute | solution.py:16
  261.8 3.6 %fusion.17 = bf16[256,1792]{1,0:T(8,128)(2,1)} fusion(f32[1024,1792]{1,0:T(8,128)} %get-tuple-element.17, bf16[256,1792]{1,0:T(8,128)(2,1)} %collective-permute-done.10, bf16[256,1792]{1,0:T(8,128)(2,1)} %collective-permute-done.9, bf16[256,1792]{1,0:T(8,128)(2,1)} %collective-permute-done.8), kind=kLoop, calls=%fused_computation.30 | loop fusion | flops 3211264 | bytes 5505024 | tf_op jit(solution)/shard_map/convert_element_type | solution.py:88
  265.4 5.1 %all-to-all-start.2 = ((bf16[8,32,1792]{2,1,0:T(8,128)(2,1)}), bf16[8,32,1792]{2,1,0:T(8,128)(2,1)}, u32[]{:S(2)}, u32[]{:S(2)}) async-start(bf16[8,32,1792]{2,1,0:T(8,128)(2,1)} %bitcast.9), calls=%async_computation.2 | async-start | bytes 1835008 | tf_op jit(solution)/shard_map/all_to_all | solution.py:62
  270.4 5.8 %fusion = bf16[1,1792,512]{2,1,0:T(8,128)(2,1)} fusion(bf16[1024,1792]{1,0:T(8,128)(2,1)} %copy-done.4, bf16[1024,512]{1,0:T(8,128)(2,1)} %copy-done.2), kind=kOutput, calls=%fused_computation.8 | convolution fusion | flops 1879965696 | bytes 6553600 | tf_op jit(solution)/shard_map/dot_general | solution.py:11
  276.3 3.4 %fusion.2 = bf16[1,512,1792]{2,1,0:T(8,128)(2,1)} fusion(bf16[1024,512]{1,0:T(8,128)(2,1)S(1)} %get-tuple-element.10, bf16[1024,1792]{1,0:T(8,128)(2,1)S(1)} %copy-done.6), kind=kOutput, calls=%fused_computation.10 | convolution fusion | flops 1879965696 | bytes 6553600 | tf_op jit(solution)/shard_map/dot_general | solution.py:11
  280.4 3.9 %all-to-all-done.2 = bf16[8,32,1792]{2,1,0:T(8,128)(2,1)} async-done(((bf16[8,32,1792]{2,1,0:T(8,128)(2,1)}), bf16[8,32,1792]{2,1,0:T(8,128)(2,1)}, u32[]{:S(2)}, u32[]{:S(2)}) %all-to-all-start.2) | async-done | bytes 917536 | tf_op jit(solution)/shard_map/all_to_all | solution.py:62
  284.2 3.2 %bitcast_convert_fusion = bf16[512,1792]{1,0:T(8,128)(2,1)} fusion(bf16[8,32,1792]{2,1,0:T(8,128)(2,1)} %all-to-all-done.2, s32[8,32]{1,0:T(8,128)S(1)} %bitcast.52, pred[8,32]{1,0:T(8,128)(4,1)S(1)} %iota_compare_fusion.3), kind=kOutput, calls=%fused_computation.1 | convolution fusion | flops 471072768 | bytes 2753792 | tf_op jit(solution)/shard_map/dot_general | solution.py:11
  (73 shorter events, 20.6 us)
Async XLA Ops:
  7.2 109.8 %copy-start = (bf16[1,512,1792]{2,1,0:T(8,128)(2,1)S(1)}, bf16[1,512,1792]{2,1,0:T(8,128)(2,1)}, u32[]{:S(2)}) copy-start(bf16[1,512,1792]{2,1,0:T(8,128)(2,1)} %param.16) | copy-start | bytes 5505028
  7.2 10.7 %copy-start.7 = (bf16[1,8,32]{2,1,0:T(8,128)(2,1)S(1)}, bf16[1,8,32]{2,1,0:T(8,128)(2,1)}, u32[]{:S(2)}) copy-start(bf16[1,8,32]{2,1,0:T(8,128)(2,1)} %param.13) | copy-start | bytes 1540
  12.0 19.5 %all-to-all-start = ((bf16[8,32,1792]{2,1,0:T(8,128)(2,1)}), bf16[8,32,1792]{2,1,0:T(8,128)(2,1)S(1)}, u32[]{:S(2)}, u32[]{:S(2)}) async-start(bf16[8,32,1792]{2,1,0:T(8,128)(2,1)} %bitcast.49), calls=%async_computation | async-start | bytes 1835008 | tf_op jit(solution)/shard_map/all_to_all | solution.py:62
  31.5 0.9 copy-start.1
  32.5 18.0 %all-to-all-start.1 = ((bf16[8,32,1792]{2,1,0:T(8,128)(2,1)}), bf16[8,32,1792]{2,1,0:T(8,128)(2,1)S(1)}, u32[]{:S(2)}, u32[]{:S(2)}) async-start(bf16[8,32,1792]{2,1,0:T(8,128)(2,1)} %bitcast.48), calls=%async_computation.1 | async-start | bytes 1835008 | tf_op jit(solution)/shard_map/all_to_all | solution.py:62
  36.8 122.1 %all-reduce.3.cloned.1.call-start = ((), (), s32[]{:S(2)}) async-start(), calls=%async_computation.4 | async-start | bytes 4194304 | tf_op jit(solution)/shard_map/psum | solution.py:67
  36.8 23.6 %collective-permute-start.1 = (bf16[256,1792]{1,0:T(8,128)(2,1)}, bf16[256,1792]{1,0:T(8,128)(2,1)}, u32[]{:S(2)}, u32[]{:S(2)}) collective-permute-start(bf16[256,1792]{1,0:T(8,128)(2,1)} %bitcast.45), channel_id=1, source_target_pairs={{0,3},{1,0},{2,1},{3,2},{4,7},{5,4},{6,5},{7,6},{8,11},{9,8},{10,9... | collective-permute-start | bytes 2752520 | tf_op jit(solution)/shard_map/ppermute | solution.py:16
  40.5 24.4 %collective-permute-start = (bf16[256,1792]{1,0:T(8,128)(2,1)}, bf16[256,1792]{1,0:T(8,128)(2,1)}, u32[]{:S(2)}, u32[]{:S(2)}) collective-permute-start(bf16[256,1792]{1,0:T(8,128)(2,1)} %bitcast.46), channel_id=1, source_target_pairs={{0,1},{1,2},{2,3},{3,0},{4,5},{5,6},{6,7},{7,4},{8,9},{9,10},{10,1... | collective-permute-start | bytes 2752520 | tf_op jit(solution)/shard_map/ppermute | solution.py:16
  50.5 49.9 %collective-permute-start.5 = (bf16[256,1792]{1,0:T(8,128)(2,1)S(1)}, bf16[256,1792]{1,0:T(8,128)(2,1)}, u32[]{:S(2)}, u32[]{:S(2)}) collective-permute-start(bf16[256,1792]{1,0:T(8,128)(2,1)S(1)} %bitcast.42), channel_id=1, source_target_pairs={{0,3},{1,0},{2,1},{3,2},{4,7},{5,4},{6,5},{7,6},{8,11},{9,8},{10,9... | collective-permute-start | bytes 2752520 | tf_op jit(solution)/shard_map/ppermute | solution.py:16
  54.3 47.6 %collective-permute-start.4 = (bf16[256,1792]{1,0:T(8,128)(2,1)S(1)}, bf16[256,1792]{1,0:T(8,128)(2,1)}, u32[]{:S(2)}, u32[]{:S(2)}) collective-permute-start(bf16[256,1792]{1,0:T(8,128)(2,1)S(1)} %bitcast.43), channel_id=1, source_target_pairs={{0,1},{1,2},{2,3},{3,0},{4,5},{5,6},{6,7},{7,4},{8,9},{9,10},{10,1... | collective-permute-start | bytes 2752520 | tf_op jit(solution)/shard_map/ppermute | solution.py:16
  55.5 39.4 %copy-start.10 = (bf16[1,1792,512]{2,1,0:T(8,128)(2,1)S(1)}, bf16[1,1792,512]{2,1,0:T(8,128)(2,1)}, u32[]{:S(2)}) copy-start(bf16[1,1792,512]{2,1,0:T(8,128)(2,1)} %param.15) | copy-start | bytes 5505028
  55.5 39.4 %copy-start.12 = (bf16[1,1792,512]{2,1,0:T(8,128)(2,1)S(1)}, bf16[1,1792,512]{2,1,0:T(8,128)(2,1)}, u32[]{:S(2)}) copy-start(bf16[1,1792,512]{2,1,0:T(8,128)(2,1)} %param.14) | copy-start | bytes 5505028
  61.4 31.5 %collective-permute-start.3 = (bf16[128,1792]{1,0:T(8,128)(2,1)S(1)}, bf16[128,1792]{1,0:T(8,128)(2,1)S(1)}, u32[]{:S(2)}, u32[]{:S(2)}) collective-permute-start(bf16[128,1792]{1,0:T(8,128)(2,1)S(1)} %slice.44), channel_id=1, source_target_pairs={{0,3},{1,0},{2,1},{3,2},{4,7},{5,4},{6,5},{7,6},{8,11},{9,8},{10,9... | collective-permute-start | bytes 1376264 | tf_op jit(solution)/shard_map/ppermute | solution.py:16
  66.0 26.9 %collective-permute-start.2 = (bf16[128,1792]{1,0:T(8,128)(2,1)S(1)}, bf16[128,1792]{1,0:T(8,128)(2,1)S(1)}, u32[]{:S(2)}, u32[]{:S(2)}) collective-permute-start(bf16[128,1792]{1,0:T(8,128)(2,1)S(1)} %slice.43), channel_id=1, source_target_pairs={{0,1},{1,2},{2,3},{3,0},{4,5},{5,6},{6,7},{7,4},{8,9},{9,10},{10,1... | collective-permute-start | bytes 1376264 | tf_op jit(solution)/shard_map/ppermute | solution.py:16
  93.0 1.9 copy-start.4
  100.3 105.8 %all-reduce.5.cloned.1.call-start = ((), (), s32[]{:S(2)}) async-start(), calls=%async_computation.5 | async-start | bytes 2097152 | tf_op jit(solution)/shard_map/psum | solution.py:72
  101.5 13.5 %collective-permute-start.7 = (bf16[128,1792]{1,0:T(8,128)(2,1)S(1)}, bf16[128,1792]{1,0:T(8,128)(2,1)S(1)}, u32[]{:S(2)}, u32[]{:S(2)}) collective-permute-start(bf16[128,1792]{1,0:T(8,128)(2,1)S(1)} %slice.46), channel_id=1, source_target_pairs={{0,3},{1,0},{2,1},{3,2},{4,7},{5,4},{6,5},{7,6},{8,11},{9,8},{10,9... | collective-permute-start | bytes 1376264 | tf_op jit(solution)/shard_map/ppermute | solution.py:16
  102.9 12.1 %collective-permute-start.6 = (bf16[128,1792]{1,0:T(8,128)(2,1)S(1)}, bf16[128,1792]{1,0:T(8,128)(2,1)S(1)}, u32[]{:S(2)}, u32[]{:S(2)}) collective-permute-start(bf16[128,1792]{1,0:T(8,128)(2,1)S(1)} %slice.45), channel_id=1, source_target_pairs={{0,1},{1,2},{2,3},{3,0},{4,5},{5,6},{6,7},{7,4},{8,9},{9,10},{10,1... | collective-permute-start | bytes 1376264 | tf_op jit(solution)/shard_map/ppermute | solution.py:16
  115.0 1.9 copy-start.5
  206.1 4.0 %copy-start.11 = (bf16[1,1792,512]{2,1,0:T(8,128)(2,1)S(1)}, bf16[1,1792,512]{2,1,0:T(8,128)(2,1)}, u32[]{:S(2)}) copy-start(bf16[1,1792,512]{2,1,0:T(8,128)(2,1)} %param.15) | copy-start | bytes 5505028
  206.1 4.0 %copy-start.13 = (bf16[1,1792,512]{2,1,0:T(8,128)(2,1)S(1)}, bf16[1,1792,512]{2,1,0:T(8,128)(2,1)}, u32[]{:S(2)}) copy-start(bf16[1,1792,512]{2,1,0:T(8,128)(2,1)} %param.14) | copy-start | bytes 5505028
  210.1 6.1 %copy-start.2 = (bf16[1024,512]{1,0:T(8,128)(2,1)}, bf16[1024,512]{1,0:T(8,128)(2,1)S(1)}, u32[]{:S(2)}) copy-start(bf16[1024,512]{1,0:T(8,128)(2,1)S(1)} %get-tuple-element.12) | copy-start | bytes 3145732
  210.2 6.1 %copy-start.3 = (bf16[1024,512]{1,0:T(8,128)(2,1)}, bf16[1024,512]{1,0:T(8,128)(2,1)S(1)}, u32[]{:S(2)}) copy-start(bf16[1024,512]{1,0:T(8,128)(2,1)S(1)} %get-tuple-element.11) | copy-start | bytes 3145732
  216.2 7.2 %copy-start.14 = (s32[4]{0:T(128)S(1)}, s32[4]{0:T(128)}, u32[]{:S(2)}) copy-start(s32[4]{0:T(128)} %constant.20.clone) | copy-start | bytes 52
  217.9 21.8 %collective-permute-start.8 = (bf16[256,1792]{1,0:T(8,128)(2,1)}, bf16[256,1792]{1,0:T(8,128)(2,1)}, u32[]{:S(2)}, u32[]{:S(2)}) collective-permute-start(bf16[256,1792]{1,0:T(8,128)(2,1)} %get-tuple-element.13), channel_id=1, source_target_pairs={{0,2},{1,3},{2,0},{3,1},{4,6},{5,7},{6,4},{7,5},{8,10},{9,11},{10,... | collective-permute-start | bytes 2752520 | tf_op jit(solution)/shard_map/ppermute | solution.py:16
  220.7 41.0 %collective-permute-start.10 = (bf16[256,1792]{1,0:T(8,128)(2,1)}, bf16[256,1792]{1,0:T(8,128)(2,1)}, u32[]{:S(2)}, u32[]{:S(2)}) collective-permute-start(bf16[256,1792]{1,0:T(8,128)(2,1)} %get-tuple-element.14), channel_id=1, source_target_pairs={{0,1},{1,2},{2,3},{3,0},{4,5},{5,6},{6,7},{7,4},{8,9},{9,10},{10,1... | collective-permute-start | bytes 2752520 | tf_op jit(solution)/shard_map/ppermute | solution.py:16
  221.1 40.7 %collective-permute-start.9 = (bf16[256,1792]{1,0:T(8,128)(2,1)}, bf16[256,1792]{1,0:T(8,128)(2,1)}, u32[]{:S(2)}, u32[]{:S(2)}) collective-permute-start(bf16[256,1792]{1,0:T(8,128)(2,1)} %get-tuple-element.15), channel_id=1, source_target_pairs={{0,3},{1,0},{2,1},{3,2},{4,7},{5,4},{6,5},{7,6},{8,11},{9,8},{10,9... | collective-permute-start | bytes 2752520 | tf_op jit(solution)/shard_map/ppermute | solution.py:16
  224.3 41.1 %all-to-all-start.3 = ((f32[32,1,32]{2,1,0:T(1,128)}), f32[32,1,32]{2,1,0:T(1,128)S(1)}, u32[]{:S(2)}, u32[]{:S(2)}) async-start(f32[32,1,32]{2,1,0:T(1,128)} %bitcast.13), calls=%async_computation.3 | async-start | bytes 32768 | tf_op jit(solution)/shard_map/all_to_all | solution.py:103
  265.4 18.9 %all-to-all-start.2 = ((bf16[8,32,1792]{2,1,0:T(8,128)(2,1)}), bf16[8,32,1792]{2,1,0:T(8,128)(2,1)}, u32[]{:S(2)}, u32[]{:S(2)}) async-start(bf16[8,32,1792]{2,1,0:T(8,128)(2,1)} %bitcast.9), calls=%async_computation.2 | async-start | bytes 1835008 | tf_op jit(solution)/shard_map/all_to_all | solution.py:62
  270.4 5.8 %copy-start.6 = (bf16[1024,1792]{1,0:T(8,128)(2,1)S(1)}, bf16[1024,1792]{1,0:T(8,128)(2,1)}, u32[]{:S(2)}) copy-start(bf16[1024,1792]{1,0:T(8,128)(2,1)} %copy-done.5) | copy-start | bytes 11010052
  276.3 3.4 %copy-start.9 = (s32[1,8]{1,0:T(1,128)S(1)}, s32[1,8]{1,0:T(1,128)}, u32[]{:S(2)}) copy-start(s32[1,8]{1,0:T(1,128)} %param.12) | copy-start | bytes 100
  276.3 8.0 %copy-start.8 = (s32[1,8,32]{2,1,0:T(8,128)S(1)}, s32[1,8,32]{2,1,0:T(8,128)}, u32[]{:S(2)}) copy-start(s32[1,8,32]{2,1,0:T(8,128)} %param.11) | copy-start | bytes 3076
Sparse Core Ops, SparseCore 0:
  100.4 58.4 all-reduce.2
  161.9 44.1 all-reduce.4

commit v2 on v1

v2 whole, which is shorter than its diff:
```python
import functools
import jax
import jax.numpy as jnp
from jax import lax
from jax.experimental import pallas as pl
from jax.experimental.pallas import tpu as pltpu
from jax.sharding import PartitionSpec as P

CONTRACT_LAST = (((1,), (1,)), ((), ()))
CONTRACT_FIRST = (((0,), (0,)), ((), ()))
CHUNKS = 2
LANES = 128
VMEM_LIMIT = 20 * 1024 * 1024
BF16 = jnp.bfloat16
F32 = jnp.float32


def dot(left, right, dims=(((1,), (0,)), ((), ()))):
    return lax.dot_general(left, right, dims, preferred_element_type=F32)


def shift(array, steps):
    size = lax.axis_size("gz")
    return lax.ppermute(array, "gz", [(i, (i + steps) % size) for i in range(size)])


def swap(array, bit):
    if bit:
        pairs = [(1, 2), (2, 1), (3, 0), (0, 3)]
    else:
        pairs = [(0, 1), (1, 0), (2, 3), (3, 2)]
    return lax.ppermute(array, "gy", pairs)


def add(left, right):
    return left.astype(F32) + right.astype(F32)


def fence(*arrays):
    return lax.optimization_barrier(arrays)


def to_experts(rows):
    return lax.all_to_all(rows, "gx", split_axis=0, concat_axis=0, tiled=True)


def call(kernel, outs, scratch, args, flops, aliases=None, free=(), in_hbm=(), out_hbm=()):
    vmem, hbm = pl.BlockSpec(memory_space=pltpu.VMEM), pl.BlockSpec(memory_space=pltpu.HBM)
    return pl.pallas_call(
        kernel,
        out_shape=[
            pltpu.HBM(*o) if i in out_hbm else jax.ShapeDtypeStruct(*o)
            for i, o in enumerate(outs)
        ],
        in_specs=[
            hbm if i in in_hbm else pl.BlockSpec(memory_space=pl.ANY) if i in free else vmem
            for i in range(len(args))
        ],
        out_specs=[hbm if i in out_hbm else vmem for i in range(len(outs))],
        scratch_shapes=scratch,
        input_output_aliases=aliases or {},
        cost_estimate=pl.CostEstimate(flops=1, bytes_accessed=1, transcendentals=0),
        compiler_params=pltpu.CompilerParams(vmem_limit_bytes=VMEM_LIMIT),
    )(*args)


def partial_kernel(pieces, base, aliased, *refs):
    inputs, refs = refs[:pieces], refs[pieces:]
    weights = refs[:3]
    refs = refs[4:] if aliased else refs[3:]
    *outs, all_rows, rows, w_gate, w_up, w_down, sems, w_sems = refs
    width, units = w_gate.shape
    at, copies = 0, []
    for i, piece in enumerate(inputs):
        place = pl.ds(at, piece.shape[0])
        copies.append(pltpu.make_async_copy(piece, rows.at[place], sems.at[i]))
        at += piece.shape[0]
    held = (w_gate, w_up, w_down)
    w_copies = [pltpu.make_async_copy(weights[i], held[i], w_sems.at[i]) for i in range(3)]
    for copy in copies + w_copies:
        copy.start()
    for copy in copies:
        copy.wait()
    keep = pltpu.make_async_copy(rows, all_rows.at[pl.ds(base, at)], sems.at[pieces])
    keep.start()
    size = at // len(outs)

    def store(k, part):
        for i, out in enumerate(outs):
            out[:, k * units : (k + 1) * units] = part[i * size : (i + 1) * size].astype(BF16)

    w_copies[0].wait()
    store(0, dot(rows[:, :width], w_gate[...]))
    w_copies[1].wait()
    store(1, dot(rows[:, :width], w_up[...]))
    w_copies[2].wait()
    store(2, dot(rows[:, width:], w_down[...], CONTRACT_LAST))
    keep.wait()


def partial(pieces, weights, all_rows, base, total_rows, parts):
    count = sum(p.shape[0] for p in pieces)
    width, units = weights[0].shape
    n = len(pieces)
    args = list(pieces) + list(weights)
    aliases, in_hbm = {}, (n, n + 1, n + 2)
    if all_rows is not None:
        aliases, in_hbm = {len(args): parts}, (n, n + 1, n + 2, n + 3)
        args.append(all_rows)
    return call(
        functools.partial(partial_kernel, n, base, all_rows is not None),
        [((count // parts, 3 * units), BF16)] * parts + [((total_rows, 2 * width), BF16)],
        [pltpu.VMEM((count, 2 * width), BF16)]
        + [pltpu.VMEM(w.shape, BF16) for w in weights]
        + [pltpu.SemaphoreType.DMA((n + 1,)), pltpu.SemaphoreType.DMA((3,))],
        args,
        6 * count * width * units,
        aliases,
        tuple(range(n)),
        in_hbm,
        (parts,),
    )


def add_kernel(top, top_in, bottom, bottom_in, top_out, bottom_out):
    top_out[...] = add(top[...], top_in[...]).astype(BF16)
    bottom_out[...] = add(bottom[...], bottom_in[...]).astype(BF16)


def add_halves(top, top_in, bottom, bottom_in):
    return call(
        add_kernel,
        [(top.shape, BF16), (bottom.shape, BF16)],
        [],
        [top, top_in, bottom, bottom_in],
        2 * top.size,
    )


def two_parts(score):
    high = score.astype(BF16).astype(F32)
    lane = lax.broadcasted_iota(jnp.int32, (score.shape[0], LANES), 1)
    return jnp.where(lane == 0, high, jnp.where(lane == 1, score - high, 0.0)).astype(BF16)


def act_kernel(base, near, aliased, *refs):
    top, top_in, bottom, bottom_in = refs[:4]
    weights = refs[4:6]
    refs = refs[8:] if aliased else refs[6:]
    *outs, all_hidden, all_both, hidden_rows, both_rows, w_gate, w_up, sems = refs
    width, units = w_gate.shape
    half = top.shape[0]
    w_copies = [
        pltpu.make_async_copy(weights[0], w_gate, sems.at[2]),
        pltpu.make_async_copy(weights[1], w_up, sems.at[3]),
    ]
    for copy in w_copies:
        copy.start()
    score_parts = []
    for start, own, arrived in ((0, top, top_in), (half, bottom, bottom_in)):
        gate_value = add(own[:, :units], arrived[:, :units])
        up_value = add(own[:, units : 2 * units], arrived[:, units : 2 * units])
        hidden_grad = add(own[:, 2 * units :], arrived[:, 2 * units :])
        sigmoid_gate = jax.nn.sigmoid(gate_value)
        activated = gate_value * sigmoid_gate
        hidden = (activated * up_value).astype(BF16)
        score_part = jnp.sum(hidden.astype(F32) * hidden_grad, axis=1, keepdims=True)
        score_parts.append(two_parts(score_part))
        hidden_rows[start : start + half] = hidden
        both_rows[start : start + half, :units] = (
            hidden_grad * up_value * sigmoid_gate * (1.0 + gate_value * (1.0 - sigmoid_gate))
        ).astype(BF16)
        both_rows[start : start + half, units:] = (hidden_grad * activated).astype(BF16)
    place = pl.ds(base, 2 * half)
    copies = [
        pltpu.make_async_copy(hidden_rows, all_hidden.at[place], sems.at[0]),
        pltpu.make_async_copy(both_rows, all_both.at[place], sems.at[1]),
    ]
    for copy in copies:
        copy.start()
    for copy in w_copies:
        copy.wait()
    part = dot(both_rows[:, :units], w_gate[...], CONTRACT_LAST)
    part = (part + dot(both_rows[:, units:], w_up[...], CONTRACT_LAST)).astype(BF16)
    outs[0][:, :width] = part[:near]
    outs[1][:, :width] = part[half : half + near]
    outs[0][:, width:] = score_parts[0][:near]
    outs[1][:, width:] = score_parts[1][:near]
    if near < half:
        far = half - near
        outs[2][:far, :width] = part[near:half]
        outs[2][far:, :width] = part[half + near :]
        outs[2][:far, width:] = score_parts[0][near:]
        outs[2][far:, width:] = score_parts[1][near:]
    for copy in copies:
        copy.wait()


def act(top, top_in, bottom, bottom_in, weights, gathered, base, near, total_rows):
    width, units = weights[0].shape
    half = top.shape[0]
    args = [top, top_in, bottom, bottom_in, weights[0], weights[1]]
    outs = [((near, width + LANES), BF16)] * 2
    if near < half:
        outs.append(((2 * (half - near), width + LANES), BF16))
    n = len(outs)
    outs += [((total_rows, units), BF16), ((total_rows, 2 * units), BF16)]
    aliases, in_hbm = {}, (4, 5)
    if gathered is not None:
        aliases, in_hbm = {6: n, 7: n + 1}, (4, 5, 6, 7)
        args += list(gathered)
    return call(
        functools.partial(act_kernel, base, near, gathered is not None),
        outs,
        [
            pltpu.VMEM((2 * half, units), BF16),
            pltpu.VMEM((2 * half, 2 * units), BF16),
            pltpu.VMEM((width, units), BF16),
            pltpu.VMEM((width, units), BF16),
            pltpu.SemaphoreType.DMA((4,)),
        ],
        args,
        8 * half * width * units,
        aliases,
        (),
        in_hbm,
        (n, n + 1),
    )


def total_kernel(width, own, first, second, third, out):
    total = add(own[...], first[...]) + add(second[...], third[...])
    out[:, :width] = total[:, :width].astype(BF16)
    out[:, width:] = two_parts(jnp.sum(total[:, width:], axis=1, keepdims=True))


def total_of(own, first, second, third):
    kernel = functools.partial(total_kernel, own.shape[1] - LANES)
    return call(kernel, [(own.shape, BF16)], [], [own, first, second, third], 4 * own.size)[0]


def local(
    tokens, grad_out, slot_token, slot_count, slot_score, gate_weight, up_weight, down_weight
):
    chosen = slot_token[0]
    counts = slot_count[0]
    experts, slots = chosen.shape
    group, width = tokens.shape
    usable = jnp.arange(slots, dtype=jnp.int32)[None, :] < counts[:, None]
    score = slot_score[0]
    picked = (
        chosen[:, :, None] == jnp.arange(group, dtype=jnp.int32)[None, None, :]
    ) & usable[:, :, None]
    zero = jnp.zeros((), BF16)
    pick = jnp.where(picked, jnp.ones((), BF16), zero)
    pick_scaled = jnp.where(picked, score[:, :, None], zero)

    weights = [
        pltpu.with_memory_space_constraint(w[0], pltpu.HBM)
        for w in (gate_weight, up_weight, down_weight)
    ]
    units = weights[2].shape[0]
    part_slots = slots // CHUNKS
    own_rows = experts * part_slots
    half = own_rows // 2
    total_rows = own_rows * CHUNKS * lax.axis_size("gz")

    def chunk_of(array, c):
        return array[:, c * part_slots : (c + 1) * part_slots].reshape(own_rows, -1)

    picks = [chunk_of(pick, c) for c in range(CHUNKS)]
    scaled_picks = [chunk_of(pick_scaled, c) for c in range(CHUNKS)]

    def dispatch(pick_x, pick_g):
        return jnp.concatenate(
            [dot(pick_x, tokens).astype(BF16), dot(pick_g, grad_out).astype(BF16)], axis=1
        )

    sent0 = dispatch(picks[0], scaled_picks[0])
    own0 = to_experts(sent0)
    sent0, pick1 = fence(sent0, picks[1])
    sent1 = dispatch(pick1, scaled_picks[1])
    own0, sent1 = fence(own0, sent1)
    before0, after0 = shift(own0, 1), shift(own0, -1)
    own1 = to_experts(sent1)
    own_top, all_rows = partial((own0,), weights, None, 0, total_rows, 1)
    own_top_in = swap(own_top, 0)
    before0, after0, own1, all_rows = fence(before0, after0, own1, all_rows)
    cut_top0, cut_bottom0 = before0[:half], after0[half:]
    far_top0, far_bottom0 = shift(cut_top0, 1), shift(cut_bottom0, -1)
    own1, all_rows, cut_top0, cut_bottom0 = fence(own1, all_rows, cut_top0, cut_bottom0)
    own_bottom, all_rows = partial((own1,), weights, all_rows, own_rows, total_rows, 1)
    own_bottom_in = swap(own_bottom, 1)
    far_top0, far_bottom0, all_rows, own1 = fence(far_top0, far_bottom0, all_rows, own1)
    before1, after1 = shift(own1, 1), shift(own1, -1)
    own_top_in, own_bottom_in, far_top0 = fence(own_top_in, own_bottom_in, far_top0)
    own_top, own_bottom = add_halves(own_top, own_top_in, own_bottom, own_bottom_in)
    own_top_in, own_bottom_in = swap(own_top, 1), swap(own_bottom, 0)
    own_top, all_rows = fence(own_top, all_rows)
    base0, base1 = CHUNKS * own_rows, (CHUNKS + 3) * own_rows
    top0, bottom0, all_rows = partial(
        (before0, far_top0, after0, far_bottom0), weights, all_rows, base0, total_rows, 2
    )
    own_top_in, own_bottom_in, top0, bottom0 = fence(own_top_in, own_bottom_in, top0, bottom0)
    top_in0, bottom_in0 = swap(top0, 0), swap(bottom0, 1)
    own_part0, own_part1, *gathered = act(
        own_top, own_top_in, own_bottom, own_bottom_in, weights, None, 0, own_rows, total_rows
    )
    before1, after1, own_part0 = fence(before1, after1, own_part0)
    cut_top1, cut_bottom1 = before1[:half], after1[half:]
    far_top1, far_bottom1 = shift(cut_top1, 1), shift(cut_bottom1, -1)
    top_in0, bottom_in0, cut_top1, cut_bottom1 = fence(
        top_in0, bottom_in0, cut_top1, cut_bottom1
    )
    top0, bottom0 = add_halves(top0, top_in0, bottom0, bottom_in0)
    top_in0, bottom_in0 = swap(top0, 1), swap(bottom0, 0)
    far_top1, far_bottom1, top0, bottom0 = fence(far_top1, far_bottom1, top0, bottom0)
    top1, bottom1, all_rows = partial(
        (before1, far_top1, after1, far_bottom1), weights, all_rows, base1, total_rows, 2
    )
    top_in1, bottom_in1 = swap(top1, 0), swap(bottom1, 1)
    top_in0, bottom_in0, all_rows = fence(top_in0, bottom_in0, all_rows)
    near_top0, near_bottom0, far0, *gathered = act(
        top0, top_in0, bottom0, bottom_in0, weights, gathered, base0, own_rows, total_rows
    )
    home0 = [shift(near_top0, -1), shift(near_bottom0, 1), shift(far0, 2)]
    top_in1, bottom_in1, far0 = fence(top_in1, bottom_in1, far0)
    top1, bottom1 = add_halves(top1, top_in1, bottom1, bottom_in1)
    top_in1, bottom_in1 = swap(top1, 1), swap(bottom1, 0)
    top_in1, bottom_in1, top1, bottom1, *home0 = fence(
        top_in1, bottom_in1, top1, bottom1, *home0
    )
    near_top1, near_bottom1, far1, *gathered = act(
        top1, top_in1, bottom1, bottom_in1, weights, gathered, base1, own_rows, total_rows
    )
    home1 = [shift(near_top1, -1), shift(near_bottom1, 1), shift(far1, 2)]
    *home0, far1 = fence(*home0, far1)
    total0 = total_of(own_part0, *home0)
    back0 = to_experts(total0)
    all_hidden, all_both = gathered
    total0, all_rows, all_hidden, all_both = fence(total0, all_rows, all_hidden, all_both)
    gate_grad = dot(all_rows[:, :width], all_both[:, :units], CONTRACT_FIRST).astype(BF16)
    up_grad = dot(all_rows[:, :width], all_both[:, units:], CONTRACT_FIRST).astype(BF16)
    *home1, gate_grad, up_grad, back0 = fence(*home1, gate_grad, up_grad, back0)
    total1 = total_of(own_part1, *home1)
    back1 = to_experts(total1)
    total1, all_hidden = fence(total1, all_hidden)
    down_grad = dot(all_hidden, all_rows[:, width:], CONTRACT_FIRST).astype(BF16)
    back1, down_grad = fence(back1, down_grad)
    back = jnp.concatenate([back0, back1])
    input_grad = dot(jnp.concatenate(picks), back[:, :width], CONTRACT_FIRST).astype(BF16)
    back_score = jnp.sum(back[:, width : width + 2].astype(F32), axis=1)
    back_score = back_score.reshape(CHUNKS, experts, part_slots).transpose(1, 0, 2)
    back_score = back_score.reshape(experts, slots)
    score_grad = jnp.where(usable, back_score / score.astype(F32), 0.0)[None]
    return input_grad, score_grad, gate_grad[None], up_grad[None], down_grad[None]


def solution(mesh):
    in_specs = (
        P(("gx", "gz"), "gy"),
        P(("gx", "gz"), "gy"),
        P(("gx", "gz"), None, None),
        P(("gx", "gz"), None),
        P(("gx", "gz"), None, None),
        P("gx", "gy", "gz"),
        P("gx", "gy", "gz"),
        P("gx", "gz", "gy"),
    )
    out_specs = (
        P(("gx", "gz"), "gy"),
        P(("gx", "gz"), None, None),
        P("gx", "gy", "gz"),
        P("gx", "gy", "gz"),
        P("gx", "gz", "gy"),
    )
    return jax.shard_map(local, mesh=mesh, in_specs=in_specs, out_specs=out_specs, check_vma=False)
```

time: 295 us -> 196 us (0.66)
  waiting for transfers between devices: 168 us -> 67.5 us
  Pallas kernels: 0 us -> 37.8 us
  matrix products: 38.9 us -> 21.5 us
  starting transfers between devices: 40.8 us -> 55.6 us
  between operations: 14.3 us -> 0.89 us
  local copies, waits for them, and re-layouts: 18.6 us -> 6.24 us
  other arithmetic: 13.3 us -> 5.33 us
    psum x2 -> x0, waiting for transfers between devices: 82.1 us -> none  [the longest x1 43.2 us: local(): pulled = lax.psum(pulled_part, 'gy').astype(jnp.float32)]
    pallas_call x0 -> x12, Pallas kernels: none -> 37.8 us  [call(): pl.pallas_call(kernel, out_shape=[pltpu.HBM(*o) if i in out_hbm else jax....]
    ppermute x11 -> x14, waiting for transfers between devices: 62 us -> 30 us  [shift(): lax.ppermute(array, 'gz', [(i, (i + steps) % size) for i in range(size)])]
    dot_general x9 -> x8, matrix products: 38.9 us -> 21.5 us  [dot(): return lax.dot_general(left, right, dims, preferred_element_type=F32)]
    ppermute x0 -> x12, waiting for transfers between devices: none -> 15 us  [swap(): return lax.ppermute(array, 'gy', pairs)]
    ppermute x0 -> x12, starting transfers between devices: none -> 13.4 us  [swap(): return lax.ppermute(array, 'gy', pairs)]
    unnamed x38 -> x23, local copies, waits for them, and re-layouts: 11.1 us -> 3 us
    convert_element_type x2 -> x0, other arithmetic: 7.6 us -> none  [the longest x1 4 us: local(): gate_up = gate_up.astype(jnp.float32)]
  transfers between devices with their start and end apart: 17 -> 30, of which waited for: 10 -> 20; matrix products, arithmetic and copies ran while one was open for 16% -> 10% of each run, Pallas kernels for 0% -> 15%
where the time goes in v2:
time: 196 us; the launch traced here: 195 us
  waiting for transfers between devices  67.5 us (34%)
  starting transfers between devices  55.6 us (28%)
  Pallas kernels  37.8 us (19%)
  matrix products  21.5 us (11%)
  local copies, waits for them, and re-layouts  6.24 us (3%)
  other arithmetic  5.33 us (3%)
    pallas_call x12, Pallas kernels, call(): pl.pallas_call(kernel, out_shape=[pltpu.HBM(*o) if i in out_hbm else jax....  37.8 us
    ppermute x14, waiting for transfers between devices, shift(): lax.ppermute(array, 'gz', [(i, (i + steps) % size) for i in range(size)])  30 us
    all_to_all x4, starting transfers between devices, to_experts(): return lax.all_to_all(rows, 'gx', split_axis=0, concat_axis=0, tiled=True)  29.9 us
    all_to_all x4, waiting for transfers between devices, to_experts(): return lax.all_to_all(rows, 'gx', split_axis=0, concat_axis=0, tiled=True)  22.6 us
    dot_general x8, matrix products, dot(): return lax.dot_general(left, right, dims, preferred_element_type=F32)  21.5 us
    ppermute x12, waiting for transfers between devices, swap(): return lax.ppermute(array, 'gy', pairs)  15 us
    ppermute x12, starting transfers between devices, swap(): return lax.ppermute(array, 'gy', pairs)  13.4 us
    ppermute x14, starting transfers between devices, shift(): lax.ppermute(array, 'gz', [(i, (i + steps) % size) for i in range(size)])  12.3 us
  transfers between devices with their start and end apart: 30, of which 20 were waited for; matrix products, arithmetic and copies ran while one was open for 10% of the time, Pallas kernels for 15%

profile of v2, /device:TPU:1, one launch (start us, length us, event | category | flops | bytes accessed | tf_op | source)
XLA Modules:
  0.0 194.8 jit_solution(10377657820067642401)
XLA Ops:
  2.5 2.0 %convolution_convert_fusion.4 = bf16[128,1792]{1,0:T(8,128)(2,1)S(1)} fusion(bf16[128,512]{1,0:T(8,128)(2,1)S(1)} %bitcast.59, bf16[512,1792]{1,0:T(8,128)(2,1)} %param.8), kind=kOutput, calls=%fused_computation.13 | convolution fusion | flops 235110400 | bytes 2424832 | tf_op jit(solution)/shard_map/dot_general | solution.py:19
  5.9 5.8 %all-to-all-start = ((bf16[8,16,3584]{2,1,0:T(8,128)(2,1)}), bf16[8,16,3584]{2,1,0:T(8,128)(2,1)S(1)}, u32[]{:S(2)}, u32[]{:S(2)}) async-start(bf16[8,16,3584]{2,1,0:T(8,128)(2,1)} %bitcast.55), calls=%async_computation | async-start | bytes 1835008 | tf_op jit(solution)/shard_map/all_to_all | solution.py:44
  14.6 10.8 %all-to-all-done = bf16[8,16,3584]{2,1,0:T(8,128)(2,1)S(1)} async-done(((bf16[8,16,3584]{2,1,0:T(8,128)(2,1)}), bf16[8,16,3584]{2,1,0:T(8,128)(2,1)S(1)}, u32[]{:S(2)}, u32[]{:S(2)}) %all-to-all-start) | async-done | bytes 917536 | tf_op jit(solution)/shard_map/all_to_all | solution.py:44
  25.4 3.8 %collective-permute-start.1 = (bf16[128,3584]{1,0:T(8,128)(2,1)S(1)}, bf16[128,3584]{1,0:T(8,128)(2,1)}, u32[]{:S(2)}, u32[]{:S(2)}) collective-permute-start(bf16[128,3584]{1,0:T(8,128)(2,1)S(1)} %bitcast.31), channel_id=1, source_target_pairs={{0,3},{1,0},{2,1},{3,2},{4,7},{5,4},{6,5},{7,6},{8,11},{9,8},{10,9... | collective-permute-start | bytes 2752520 | tf_op jit(solution)/shard_map/ppermute | solution.py:24
  29.1 5.3 %all-to-all-start.1 = ((bf16[8,16,3584]{2,1,0:T(8,128)(2,1)}), bf16[8,16,3584]{2,1,0:T(8,128)(2,1)}, u32[]{:S(2)}, u32[]{:S(2)}) async-start(bf16[8,16,3584]{2,1,0:T(8,128)(2,1)} %bitcast.54), calls=%async_computation.1 | async-start | bytes 1835008 | tf_op jit(solution)/shard_map/all_to_all | solution.py:44
  34.4 3.9 %shard_map.119 = (bf16[128,1536]{1,0:T(8,128)(2,1)S(1)}, bf16[1024,3584]{1,0:T(8,128)(2,1)}) custom-call(bf16[128,3584]{1,0:T(8,128)(2,1)S(1)} %bitcast.33, bf16[1792,512]{1,0:T(8,128)(2,1)} %bitcast.34, bf16[1792,512]{1,0:T(8,128)(2,1)} %bitcast.41, bf16[512,1792]{1,0:T(8,128)(2,1)} %bitcast.50), custom_call_target="tpu_custom_call" | custom-call | flops 1 | bytes 1 | tf_op jit(solution)/shard_map/pallas_call | solution.py:49
  38.3 9.9 %all-to-all-done.1 = bf16[8,16,3584]{2,1,0:T(8,128)(2,1)} async-done(((bf16[8,16,3584]{2,1,0:T(8,128)(2,1)}), bf16[8,16,3584]{2,1,0:T(8,128)(2,1)}, u32[]{:S(2)}, u32[]{:S(2)}) %all-to-all-start.1) | async-done | bytes 917536 | tf_op jit(solution)/shard_map/all_to_all | solution.py:44
  48.2 2.9 %collective-permute-done.refs_0_ = bf16[128,3584]{1,0:T(8,128)(2,1)} collective-permute-done((bf16[128,3584]{1,0:T(8,128)(2,1)S(1)}, bf16[128,3584]{1,0:T(8,128)(2,1)}, u32[]{:S(2)}, u32[]{:S(2)}) %collective-permute-start) | collective-permute-done | bytes 917536 | tf_op jit(solution)/shard_map/ppermute | solution.py:24
  56.1 3.9 %shard_map.120 = (bf16[128,1536]{1,0:T(8,128)(2,1)S(1)}, bf16[1024,3584]{1,0:T(8,128)(2,1)}) custom-call(bf16[128,3584]{1,0:T(8,128)(2,1)} %bitcast.10.refs_0_, bf16[1792,512]{1,0:T(8,128)(2,1)} %bitcast.35, bf16[1792,512]{1,0:T(8,128)(2,1)} %bitcast.42, bf16[512,1792]{1,0:T(8,128)(2,1)} %bitcast.51, ...), custom_call_target="tpu_custom_call", output_to_operand_aliasing={{1}: (4, {})} | custom-call | flops 1 | bytes 1 | tf_op jit(solution)/shard_map/pallas_call | solution.py:49
  60.0 2.0 %collective-permute-start.7 = (bf16[128,1536]{1,0:T(8,128)(2,1)S(1)}, bf16[128,1536]{1,0:T(8,128)(2,1)S(1)}, u32[]{:S(2)}, u32[]{:S(2)}) collective-permute-start(bf16[128,1536]{1,0:T(8,128)(2,1)S(1)} %get-tuple-element.106.bottom), channel_id=1, source_target_pairs={{4,8},{8,4},{12,0},{0,12},{5,9},{9,5},{13,1},{1,13},{6,10},{10,6},... | collective-permute-start | bytes 1179656 | tf_op jit(solution)/shard_map/ppermute | solution.py:32
  66.2 2.7 %collective-permute-done.7.bottom_in = bf16[128,1536]{1,0:T(8,128)(2,1)S(1)} collective-permute-done((bf16[128,1536]{1,0:T(8,128)(2,1)S(1)}, bf16[128,1536]{1,0:T(8,128)(2,1)S(1)}, u32[]{:S(2)}, u32[]{:S(2)}) %collective-permute-start.7) | collective-permute-done | bytes 393248 | tf_op jit(solution)/shard_map/ppermute | solution.py:32
  69.1 2.0 %collective-permute-start.8 = (bf16[128,1536]{1,0:T(8,128)(2,1)S(1)}, bf16[128,1536]{1,0:T(8,128)(2,1)S(1)}, u32[]{:S(2)}, u32[]{:S(2)}) collective-permute-start(bf16[128,1536]{1,0:T(8,128)(2,1)S(1)} %get-tuple-element.112.refs_0_), channel_id=1, source_target_pairs={{4,8},{8,4},{12,0},{0,12},{5,9},{9,5},{13,1},{1,13},{6,10},{10,6},... | collective-permute-start | bytes 1179656 | tf_op jit(solution)/shard_map/ppermute | solution.py:32
  71.1 5.3 %shard_map.122 = (bf16[192,1536]{1,0:T(8,128)(2,1)S(1)}, bf16[192,1536]{1,0:T(8,128)(2,1)S(1)}, bf16[1024,3584]{1,0:T(8,128)(2,1)}) custom-call(bf16[128,3584]{1,0:T(8,128)(2,1)} %collective-permute-done.refs_0_, bf16[64,3584]{1,0:T(8,128)(2,1)S(1)} %collective-permute-done.2.refs_1_, ...), custom_call_target="tpu_custom_call", output_to_operand_aliasing={{2}: (7, {})} | custom-call | flops 1 | bytes 1 | tf_op jit(solution)/shard_map/pallas_call | solution.py:49
  79.2 3.9 %shard_map.123 = (bf16[128,1920]{1,0:T(8,128)(2,1)S(1)}, bf16[128,1920]{1,0:T(8,128)(2,1)S(1)}, bf16[1024,512]{1,0:T(8,128)(2,1)}, bf16[1024,1024]{1,0:T(8,128)(2,1)}) custom-call(bf16[128,1536]{1,0:T(8,128)(2,1)S(1)} %get-tuple-element.112.refs_0_, bf16[128,1536]{1,0:T(8,128)(2,1)S(1)} %collective-permute-done.8.refs_1_, ...), custom_call_target="tpu_custom_call" | custom-call | flops 1 | bytes 1 | tf_op jit(solution)/shard_map/pallas_call | solution.py:49
  87.0 2.8 %collective-permute-done.12.top_in = bf16[192,1536]{1,0:T(8,128)(2,1)S(1)} collective-permute-done((bf16[192,1536]{1,0:T(8,128)(2,1)S(1)}, bf16[192,1536]{1,0:T(8,128)(2,1)S(1)}, u32[]{:S(2)}, u32[]{:S(2)}) %collective-permute-start.12) | collective-permute-done | bytes 589856 | tf_op jit(solution)/shard_map/ppermute | solution.py:32
  91.6 1.9 collective-permute-done.11.refs_3_
  94.6 6.2 %shard_map.125 = (bf16[192,1536]{1,0:T(8,128)(2,1)S(1)}, bf16[192,1536]{1,0:T(8,128)(2,1)S(1)}, bf16[1024,3584]{1,0:T(8,128)(2,1)}) custom-call(bf16[128,3584]{1,0:T(8,128)(2,1)S(1)} %collective-permute-done.4.refs_0_, bf16[64,3584]{1,0:T(8,128)(2,1)S(1)} %collective-permute-done.10.refs_1_, ...), custom_call_target="tpu_custom_call", output_to_operand_aliasing={{2}: (7, {})} | custom-call | flops 1 | bytes 1 | tf_op jit(solution)/shard_map/pallas_call | solution.py:49
  101.9 1.9 collective-permute-start.15
  103.8 4.8 %shard_map.126 = (bf16[128,1920]{1,0:T(8,128)(2,1)S(1)}, bf16[128,1920]{1,0:T(8,128)(2,1)S(1)}, bf16[128,1920]{1,0:T(8,128)(2,1)S(1)}, bf16[1024,512]{1,0:T(8,128)(2,1)}, bf16[1024,1024]{1,0:T(8,128)(2,1)}) custom-call(bf16[192,1536]{1,0:T(8,128)(2,1)S(1)} %get-tuple-element.135.refs_0_, ...), custom_call_target="tpu_custom_call", output_to_operand_aliasing={{3}: (6, {}), {4}: (7, {})} | custom-call | flops 1 | bytes 1 | tf_op jit(solution)/shard_map/pallas_call | solution.py:49
  108.6 7.7 %collective-permute-done.14.top_in = bf16[192,1536]{1,0:T(8,128)(2,1)S(1)} collective-permute-done((bf16[192,1536]{1,0:T(8,128)(2,1)S(1)}, bf16[192,1536]{1,0:T(8,128)(2,1)S(1)}, u32[]{:S(2)}, u32[]{:S(2)}) %collective-permute-start.14) | collective-permute-done | bytes 589856 | tf_op jit(solution)/shard_map/ppermute | solution.py:32
  116.6 2.5 %collective-permute-start.18 = (bf16[192,1536]{1,0:T(8,128)(2,1)S(1)}, bf16[192,1536]{1,0:T(8,128)(2,1)S(1)}, u32[]{:S(2)}, u32[]{:S(2)}) collective-permute-start(bf16[192,1536]{1,0:T(8,128)(2,1)S(1)} %get-tuple-element.149.refs_0_), channel_id=1, source_target_pairs={{4,8},{8,4},{12,0},{0,12},{5,9},{9,5},{13,1},{1,13},{6,10},{10,6},... | collective-permute-start | bytes 1769480 | tf_op jit(solution)/shard_map/ppermute | solution.py:32
  121.2 5.9 %collective-permute-done.20.first = bf16[128,1920]{1,0:T(8,128)(2,1)S(1)} collective-permute-done((bf16[128,1920]{1,0:T(8,128)(2,1)S(1)}, bf16[128,1920]{1,0:T(8,128)(2,1)S(1)}, u32[]{:S(2)}, u32[]{:S(2)}) %collective-permute-start.20) | collective-permute-done | bytes 491552 | tf_op jit(solution)/shard_map/ppermute | solution.py:24
  127.1 3.8 %collective-permute-done.21.second = bf16[128,1920]{1,0:T(8,128)(2,1)S(1)} collective-permute-done((bf16[128,1920]{1,0:T(8,128)(2,1)S(1)}, bf16[128,1920]{1,0:T(8,128)(2,1)S(1)}, u32[]{:S(2)}, u32[]{:S(2)}) %collective-permute-start.21) | collective-permute-done | bytes 491552 | tf_op jit(solution)/shard_map/ppermute | solution.py:24
  130.9 6.0 %collective-permute-done.22.third = bf16[128,1920]{1,0:T(8,128)(2,1)S(1)} collective-permute-done((bf16[128,1920]{1,0:T(8,128)(2,1)S(1)}, bf16[128,1920]{1,0:T(8,128)(2,1)S(1)}, u32[]{:S(2)}, u32[]{:S(2)}) %collective-permute-start.22) | collective-permute-done | bytes 491552 | tf_op jit(solution)/shard_map/ppermute | solution.py:24
  136.9 5.6 %shard_map.128 = (bf16[128,1920]{1,0:T(8,128)(2,1)S(1)}, bf16[128,1920]{1,0:T(8,128)(2,1)S(1)}, bf16[128,1920]{1,0:T(8,128)(2,1)}, bf16[1024,512]{1,0:T(8,128)(2,1)}, bf16[1024,1024]{1,0:T(8,128)(2,1)}) custom-call(bf16[192,1536]{1,0:T(8,128)(2,1)S(1)} %get-tuple-element.149.refs_0_, ...), custom_call_target="tpu_custom_call", output_to_operand_aliasing={{3}: (6, {}), {4}: (7, {})} | custom-call | flops 1 | bytes 1 | tf_op jit(solution)/shard_map/pallas_call | solution.py:49
  144.3 13.2 %all-to-all-start.2 = ((bf16[8,16,1920]{2,1,0:T(8,128)(2,1)}), bf16[8,16,1920]{2,1,0:T(8,128)(2,1)}, u32[]{:S(2)}, u32[]{:S(2)}) async-start(bf16[8,16,1920]{2,1,0:T(8,128)(2,1)} %bitcast.14), calls=%async_computation.2 | async-start | bytes 983040 | tf_op jit(solution)/shard_map/all_to_all | solution.py:44
  159.0 6.3 %fusion.9 = bf16[1792,512]{1,0:T(8,128)(2,1)} fusion(bf16[1024,3584]{1,0:T(8,128)(2,1)} %get-tuple-element.168, bf16[1024,1024]{1,0:T(8,128)(2,1)} %get-tuple-element.169), kind=kOutput, calls=%fused_computation.7 | convolution fusion | flops 1879965696 | bytes 6553600 | tf_op jit(solution)/shard_map/dot_general | solution.py:19
  165.3 3.4 %fusion.6 = bf16[1792,512]{1,0:T(8,128)(2,1)} fusion(bf16[1024,3584]{1,0:T(8,128)(2,1)S(1)} %bitcast.49, bf16[1024,1024]{1,0:T(8,128)(2,1)S(1)} %copy-done.3), kind=kOutput, calls=%fused_computation.6 | convolution fusion | flops 1879965696 | bytes 6553600 | tf_op jit(solution)/shard_map/dot_general | solution.py:19
  172.0 2.3 %shard_map.130 = bf16[128,1920]{1,0:T(8,128)(2,1)} custom-call(bf16[128,1920]{1,0:T(8,128)(2,1)S(1)} %get-tuple-element.171.own, bf16[128,1920]{1,0:T(8,128)(2,1)S(1)} %collective-permute-done.23.first, bf16[128,1920]{1,0:T(8,128)(2,1)} %collective-permute-done.24.second, bf16[128,1920]{1,0:T(8,128)(2,1)S(1)} %collective-permute-done.25.third), custom_call_target="tpu_custom_call" | custom-call | flops 1 | bytes 1 | tf_op jit(solution)/shard_map/pallas_call | solution.py:49
  174.2 5.6 %all-to-all-start.3 = ((bf16[8,16,1920]{2,1,0:T(8,128)(2,1)}), bf16[8,16,1920]{2,1,0:T(8,128)(2,1)S(1)}, u32[]{:S(2)}, u32[]{:S(2)}) async-start(bf16[8,16,1920]{2,1,0:T(8,128)(2,1)} %bitcast.16), calls=%async_computation.3 | async-start | bytes 983040 | tf_op jit(solution)/shard_map/all_to_all | solution.py:44
  181.7 5.4 %fusion.12 = bf16[512,1792]{1,0:T(8,128)(2,1)} fusion(bf16[1024,512]{1,0:T(8,128)(2,1)S(1)} %copy-done.5, bf16[1024,3584]{1,0:T(8,128)(2,1)} %get-tuple-element.168), kind=kOutput, calls=%fused_computation.8 | convolution fusion | flops 1879965696 | bytes 6553600 | tf_op jit(solution)/shard_map/dot_general | solution.py:19
  190.8 3.2 %convolution_convert_fusion = bf16[512,1792]{1,0:T(8,128)(2,1)} fusion(bf16[256,1920]{1,0:T(8,128)(2,1)} %constant_dynamic-update-slice_fusion, bf16[128,512]{1,0:T(8,128)(2,1)S(1)} %bitcast.58, bf16[128,512]{1,0:T(8,128)(2,1)} %bitcast.60), kind=kOutput, calls=%fused_computation.9 | convolution fusion | flops 471203840 | bytes 3014656 | tf_op jit(solution)/shard_map/dot_general | solution.py:19
  (87 shorter events, 41.4 us)
Async XLA Ops:
  5.9 19.5 %all-to-all-start = ((bf16[8,16,3584]{2,1,0:T(8,128)(2,1)}), bf16[8,16,3584]{2,1,0:T(8,128)(2,1)S(1)}, u32[]{:S(2)}, u32[]{:S(2)}) async-start(bf16[8,16,3584]{2,1,0:T(8,128)(2,1)} %bitcast.55), calls=%async_computation | async-start | bytes 1835008 | tf_op jit(solution)/shard_map/all_to_all | solution.py:44
  25.4 22.8 %collective-permute-start.1 = (bf16[128,3584]{1,0:T(8,128)(2,1)S(1)}, bf16[128,3584]{1,0:T(8,128)(2,1)}, u32[]{:S(2)}, u32[]{:S(2)}) collective-permute-start(bf16[128,3584]{1,0:T(8,128)(2,1)S(1)} %bitcast.31), channel_id=1, source_target_pairs={{0,3},{1,0},{2,1},{3,2},{4,7},{5,4},{6,5},{7,6},{8,11},{9,8},{10,9... | collective-permute-start | bytes 2752520 | tf_op jit(solution)/shard_map/ppermute | solution.py:24
  29.1 22.0 %collective-permute-start = (bf16[128,3584]{1,0:T(8,128)(2,1)S(1)}, bf16[128,3584]{1,0:T(8,128)(2,1)}, u32[]{:S(2)}, u32[]{:S(2)}) collective-permute-start(bf16[128,3584]{1,0:T(8,128)(2,1)S(1)} %bitcast.32), channel_id=1, source_target_pairs={{0,1},{1,2},{2,3},{3,0},{4,5},{5,6},{6,7},{7,4},{8,9},{9,10},{10,1... | collective-permute-start | bytes 2752520 | tf_op jit(solution)/shard_map/ppermute | solution.py:24
  29.1 19.1 %all-to-all-start.1 = ((bf16[8,16,3584]{2,1,0:T(8,128)(2,1)}), bf16[8,16,3584]{2,1,0:T(8,128)(2,1)}, u32[]{:S(2)}, u32[]{:S(2)}) async-start(bf16[8,16,3584]{2,1,0:T(8,128)(2,1)} %bitcast.54), calls=%async_computation.1 | async-start | bytes 1835008 | tf_op jit(solution)/shard_map/all_to_all | solution.py:44
  53.2 10.0 %collective-permute-start.3 = (bf16[64,3584]{1,0:T(8,128)(2,1)S(1)}, bf16[64,3584]{1,0:T(8,128)(2,1)S(1)}, u32[]{:S(2)}, u32[]{:S(2)}) collective-permute-start(bf16[64,3584]{1,0:T(8,128)(2,1)S(1)} %slice.48), channel_id=1, source_target_pairs={{0,3},{1,0},{2,1},{3,2},{4,7},{5,4},{6,5},{7,6},{8,11},{9,8},{10,9... | collective-permute-start | bytes 1376264 | tf_op jit(solution)/shard_map/ppermute | solution.py:24
  53.6 11.2 %collective-permute-start.2 = (bf16[64,3584]{1,0:T(8,128)(2,1)S(1)}, bf16[64,3584]{1,0:T(8,128)(2,1)S(1)}, u32[]{:S(2)}, u32[]{:S(2)}) collective-permute-start(bf16[64,3584]{1,0:T(8,128)(2,1)S(1)} %slice.47), channel_id=1, source_target_pairs={{0,1},{1,2},{2,3},{3,0},{4,5},{5,6},{6,7},{7,4},{8,9},{9,10},{10,1... | collective-permute-start | bytes 1376264 | tf_op jit(solution)/shard_map/ppermute | solution.py:24
  54.8 11.5 %collective-permute-start.6 = (bf16[128,1536]{1,0:T(8,128)(2,1)S(1)}, bf16[128,1536]{1,0:T(8,128)(2,1)S(1)}, u32[]{:S(2)}, u32[]{:S(2)}) collective-permute-start(bf16[128,1536]{1,0:T(8,128)(2,1)S(1)} %get-tuple-element.105.top), channel_id=1, source_target_pairs={{0,4},{4,0},{8,12},{12,8},{1,5},{5,1},{9,13},{13,9},{2,6},{6,2},{1... | collective-permute-start | bytes 1179656 | tf_op jit(solution)/shard_map/ppermute | solution.py:32
  60.0 9.0 %collective-permute-start.7 = (bf16[128,1536]{1,0:T(8,128)(2,1)S(1)}, bf16[128,1536]{1,0:T(8,128)(2,1)S(1)}, u32[]{:S(2)}, u32[]{:S(2)}) collective-permute-start(bf16[128,1536]{1,0:T(8,128)(2,1)S(1)} %get-tuple-element.106.bottom), channel_id=1, source_target_pairs={{4,8},{8,4},{12,0},{0,12},{5,9},{9,5},{13,1},{1,13},{6,10},{10,6},... | collective-permute-start | bytes 1179656 | tf_op jit(solution)/shard_map/ppermute | solution.py:32
  64.8 19.1 %collective-permute-start.5 = (bf16[128,3584]{1,0:T(8,128)(2,1)}, bf16[128,3584]{1,0:T(8,128)(2,1)S(1)}, u32[]{:S(2)}, u32[]{:S(2)}) collective-permute-start(bf16[128,3584]{1,0:T(8,128)(2,1)} %bitcast.10.refs_0_), channel_id=1, source_target_pairs={{0,3},{1,0},{2,1},{3,2},{4,7},{5,4},{6,5},{7,6},{8,11},{9,8},{10,9... | collective-permute-start | bytes 2752520 | tf_op jit(solution)/shard_map/ppermute | solution.py:24
  65.1 20.3 %collective-permute-start.4 = (bf16[128,3584]{1,0:T(8,128)(2,1)}, bf16[128,3584]{1,0:T(8,128)(2,1)S(1)}, u32[]{:S(2)}, u32[]{:S(2)}) collective-permute-start(bf16[128,3584]{1,0:T(8,128)(2,1)} %bitcast.10.refs_0_), channel_id=1, source_target_pairs={{0,1},{1,2},{2,3},{3,0},{4,5},{5,6},{6,7},{7,4},{8,9},{9,10},{10,1... | collective-permute-start | bytes 2752520 | tf_op jit(solution)/shard_map/ppermute | solution.py:24
  69.1 8.2 %collective-permute-start.8 = (bf16[128,1536]{1,0:T(8,128)(2,1)S(1)}, bf16[128,1536]{1,0:T(8,128)(2,1)S(1)}, u32[]{:S(2)}, u32[]{:S(2)}) collective-permute-start(bf16[128,1536]{1,0:T(8,128)(2,1)S(1)} %get-tuple-element.112.refs_0_), channel_id=1, source_target_pairs={{4,8},{8,4},{12,0},{0,12},{5,9},{9,5},{13,1},{1,13},{6,10},{10,6},... | collective-permute-start | bytes 1179656 | tf_op jit(solution)/shard_map/ppermute | solution.py:32
  71.1 6.9 %collective-permute-start.9 = (bf16[128,1536]{1,0:T(8,128)(2,1)S(1)}, bf16[128,1536]{1,0:T(8,128)(2,1)S(1)}, u32[]{:S(2)}, u32[]{:S(2)}) collective-permute-start(bf16[128,1536]{1,0:T(8,128)(2,1)S(1)} %get-tuple-element.113.refs_2_), channel_id=1, source_target_pairs={{0,4},{4,0},{8,12},{12,8},{1,5},{5,1},{9,13},{13,9},{2,6},{6,2},{1... | collective-permute-start | bytes 1179656 | tf_op jit(solution)/shard_map/ppermute | solution.py:32
  78.0 11.8 %collective-permute-start.12 = (bf16[192,1536]{1,0:T(8,128)(2,1)S(1)}, bf16[192,1536]{1,0:T(8,128)(2,1)S(1)}, u32[]{:S(2)}, u32[]{:S(2)}) collective-permute-start(bf16[192,1536]{1,0:T(8,128)(2,1)S(1)} %get-tuple-element.124.top), channel_id=1, source_target_pairs={{0,4},{4,0},{8,12},{12,8},{1,5},{5,1},{9,13},{13,9},{2,6},{6,2},{1... | collective-permute-start | bytes 1769480 | tf_op jit(solution)/shard_map/ppermute | solution.py:32
  78.0 11.8 %collective-permute-start.13 = (bf16[192,1536]{1,0:T(8,128)(2,1)S(1)}, bf16[192,1536]{1,0:T(8,128)(2,1)S(1)}, u32[]{:S(2)}, u32[]{:S(2)}) collective-permute-start(bf16[192,1536]{1,0:T(8,128)(2,1)S(1)} %get-tuple-element.125.bottom), channel_id=1, source_target_pairs={{4,8},{8,4},{12,0},{0,12},{5,9},{9,5},{13,1},{1,13},{6,10},{10,6},... | collective-permute-start | bytes 1769480 | tf_op jit(solution)/shard_map/ppermute | solution.py:32
  85.4 8.0 %collective-permute-start.11 = (bf16[64,3584]{1,0:T(8,128)(2,1)S(1)}, bf16[64,3584]{1,0:T(8,128)(2,1)S(1)}, u32[]{:S(2)}, u32[]{:S(2)}) collective-permute-start(bf16[64,3584]{1,0:T(8,128)(2,1)S(1)} %slice.50), channel_id=1, source_target_pairs={{0,3},{1,0},{2,1},{3,2},{4,7},{5,4},{6,5},{7,6},{8,11},{9,8},{10,9... | collective-permute-start | bytes 1376264 | tf_op jit(solution)/shard_map/ppermute | solution.py:24
  85.8 8.8 %collective-permute-start.10 = (bf16[64,3584]{1,0:T(8,128)(2,1)S(1)}, bf16[64,3584]{1,0:T(8,128)(2,1)S(1)}, u32[]{:S(2)}, u32[]{:S(2)}) collective-permute-start(bf16[64,3584]{1,0:T(8,128)(2,1)S(1)} %slice.49), channel_id=1, source_target_pairs={{0,1},{1,2},{2,3},{3,0},{4,5},{5,6},{6,7},{7,4},{8,9},{9,10},{10,1... | collective-permute-start | bytes 1376264 | tf_op jit(solution)/shard_map/ppermute | solution.py:24
  90.1 13.7 %collective-permute-start.16 = (bf16[192,1536]{1,0:T(8,128)(2,1)S(1)}, bf16[192,1536]{1,0:T(8,128)(2,1)S(1)}, u32[]{:S(2)}, u32[]{:S(2)}) collective-permute-start(bf16[192,1536]{1,0:T(8,128)(2,1)S(1)} %get-tuple-element.135.refs_0_), channel_id=1, source_target_pairs={{4,8},{8,4},{12,0},{0,12},{5,9},{9,5},{13,1},{1,13},{6,10},{10,6},... | collective-permute-start | bytes 1769480 | tf_op jit(solution)/shard_map/ppermute | solution.py:32
  91.6 12.3 %collective-permute-start.17 = (bf16[192,1536]{1,0:T(8,128)(2,1)S(1)}, bf16[192,1536]{1,0:T(8,128)(2,1)S(1)}, u32[]{:S(2)}, u32[]{:S(2)}) collective-permute-start(bf16[192,1536]{1,0:T(8,128)(2,1)S(1)} %get-tuple-element.138.refs_2_), channel_id=1, source_target_pairs={{0,4},{4,0},{8,12},{12,8},{1,5},{5,1},{9,13},{13,9},{2,6},{6,2},{1... | collective-permute-start | bytes 1769480 | tf_op jit(solution)/shard_map/ppermute | solution.py:32
  100.8 15.5 %collective-permute-start.14 = (bf16[192,1536]{1,0:T(8,128)(2,1)S(1)}, bf16[192,1536]{1,0:T(8,128)(2,1)S(1)}, u32[]{:S(2)}, u32[]{:S(2)}) collective-permute-start(bf16[192,1536]{1,0:T(8,128)(2,1)S(1)} %get-tuple-element.133.top), channel_id=1, source_target_pairs={{0,4},{4,0},{8,12},{12,8},{1,5},{5,1},{9,13},{13,9},{2,6},{6,2},{1... | collective-permute-start | bytes 1769480 | tf_op jit(solution)/shard_map/ppermute | solution.py:32
  101.9 14.4 %collective-permute-start.15 = (bf16[192,1536]{1,0:T(8,128)(2,1)S(1)}, bf16[192,1536]{1,0:T(8,128)(2,1)S(1)}, u32[]{:S(2)}, u32[]{:S(2)}) collective-permute-start(bf16[192,1536]{1,0:T(8,128)(2,1)S(1)} %get-tuple-element.134.bottom), channel_id=1, source_target_pairs={{4,8},{8,4},{12,0},{0,12},{5,9},{9,5},{13,1},{1,13},{6,10},{10,6},... | collective-permute-start | bytes 1769480 | tf_op jit(solution)/shard_map/ppermute | solution.py:32
  116.6 20.3 %collective-permute-start.18 = (bf16[192,1536]{1,0:T(8,128)(2,1)S(1)}, bf16[192,1536]{1,0:T(8,128)(2,1)S(1)}, u32[]{:S(2)}, u32[]{:S(2)}) collective-permute-start(bf16[192,1536]{1,0:T(8,128)(2,1)S(1)} %get-tuple-element.149.refs_0_), channel_id=1, source_target_pairs={{4,8},{8,4},{12,0},{0,12},{5,9},{9,5},{13,1},{1,13},{6,10},{10,6},... | collective-permute-start | bytes 1769480 | tf_op jit(solution)/shard_map/ppermute | solution.py:32
  119.1 17.8 %collective-permute-start.19 = (bf16[192,1536]{1,0:T(8,128)(2,1)S(1)}, bf16[192,1536]{1,0:T(8,128)(2,1)S(1)}, u32[]{:S(2)}, u32[]{:S(2)}) collective-permute-start(bf16[192,1536]{1,0:T(8,128)(2,1)S(1)} %get-tuple-element.151.refs_2_), channel_id=1, source_target_pairs={{0,4},{4,0},{8,12},{12,8},{1,5},{5,1},{9,13},{13,9},{2,6},{6,2},{1... | collective-permute-start | bytes 1769480 | tf_op jit(solution)/shard_map/ppermute | solution.py:32
  119.1 8.0 %collective-permute-start.20 = (bf16[128,1920]{1,0:T(8,128)(2,1)S(1)}, bf16[128,1920]{1,0:T(8,128)(2,1)S(1)}, u32[]{:S(2)}, u32[]{:S(2)}) collective-permute-start(bf16[128,1920]{1,0:T(8,128)(2,1)S(1)} %get-tuple-element.147), channel_id=1, source_target_pairs={{0,3},{1,0},{2,1},{3,2},{4,7},{5,4},{6,5},{7,6},{8,11},{9,8},{10,9... | collective-permute-start | bytes 1474568 | tf_op jit(solution)/shard_map/ppermute | solution.py:24
  119.6 11.3 %collective-permute-start.21 = (bf16[128,1920]{1,0:T(8,128)(2,1)S(1)}, bf16[128,1920]{1,0:T(8,128)(2,1)S(1)}, u32[]{:S(2)}, u32[]{:S(2)}) collective-permute-start(bf16[128,1920]{1,0:T(8,128)(2,1)S(1)} %get-tuple-element.148), channel_id=1, source_target_pairs={{0,1},{1,2},{2,3},{3,0},{4,5},{5,6},{6,7},{7,4},{8,9},{9,10},{10,1... | collective-permute-start | bytes 1474568 | tf_op jit(solution)/shard_map/ppermute | solution.py:24
  120.6 16.3 %collective-permute-start.22 = (bf16[128,1920]{1,0:T(8,128)(2,1)S(1)}, bf16[128,1920]{1,0:T(8,128)(2,1)S(1)}, u32[]{:S(2)}, u32[]{:S(2)}) collective-permute-start(bf16[128,1920]{1,0:T(8,128)(2,1)S(1)} %get-tuple-element.142), channel_id=1, source_target_pairs={{0,2},{1,3},{2,0},{3,1},{4,6},{5,7},{6,4},{7,5},{8,10},{9,11},{10,... | collective-permute-start | bytes 1474568 | tf_op jit(solution)/shard_map/ppermute | solution.py:24
  142.5 29.4 %collective-permute-start.25 = (bf16[128,1920]{1,0:T(8,128)(2,1)}, bf16[128,1920]{1,0:T(8,128)(2,1)S(1)}, u32[]{:S(2)}, u32[]{:S(2)}) collective-permute-start(bf16[128,1920]{1,0:T(8,128)(2,1)} %get-tuple-element.157), channel_id=1, source_target_pairs={{0,2},{1,3},{2,0},{3,1},{4,6},{5,7},{6,4},{7,5},{8,10},{9,11},{10,... | collective-permute-start | bytes 1474568 | tf_op jit(solution)/shard_map/ppermute | solution.py:24
  144.3 24.4 %all-to-all-start.2 = ((bf16[8,16,1920]{2,1,0:T(8,128)(2,1)}), bf16[8,16,1920]{2,1,0:T(8,128)(2,1)}, u32[]{:S(2)}, u32[]{:S(2)}) async-start(bf16[8,16,1920]{2,1,0:T(8,128)(2,1)} %bitcast.14), calls=%async_computation.2 | async-start | bytes 983040 | tf_op jit(solution)/shard_map/all_to_all | solution.py:44
  157.5 12.9 %collective-permute-start.23 = (bf16[128,1920]{1,0:T(8,128)(2,1)}, bf16[128,1920]{1,0:T(8,128)(2,1)S(1)}, u32[]{:S(2)}, u32[]{:S(2)}) collective-permute-start(bf16[128,1920]{1,0:T(8,128)(2,1)} %copy-done.2), channel_id=1, source_target_pairs={{0,3},{1,0},{2,1},{3,2},{4,7},{5,4},{6,5},{7,6},{8,11},{9,8},{10,9... | collective-permute-start | bytes 1474568 | tf_op jit(solution)/shard_map/ppermute | solution.py:24
  157.5 7.8 %slice-start = ((s8[7340032]{0:T(1024)(128)(4,1)}), s8[4194304]{0:T(1024)(128)(4,1)S(1)}, s32[]{:S(2)}) async-start(s8[7340032]{0:T(1024)(128)(4,1)} %bitcast.48), calls=%async_computation.4 | async-start | bytes 8388608
  157.5 7.8 %slice-start.1 = ((s8[7340032]{0:T(1024)(128)(4,1)}), s8[3145728]{0:T(1024)(128)(4,1)S(1)}, s32[]{:S(2)}) async-start(s8[7340032]{0:T(1024)(128)(4,1)} %bitcast.48), calls=%async_computation.5 | async-start | bytes 6291456
  157.5 14.4 %collective-permute-start.24 = (bf16[128,1920]{1,0:T(8,128)(2,1)}, bf16[128,1920]{1,0:T(8,128)(2,1)}, u32[]{:S(2)}, u32[]{:S(2)}) collective-permute-start(bf16[128,1920]{1,0:T(8,128)(2,1)} %copy-done.1), channel_id=1, source_target_pairs={{0,1},{1,2},{2,3},{3,0},{4,5},{5,6},{6,7},{7,4},{8,9},{9,10},{10,1... | collective-permute-start | bytes 1474568 | tf_op jit(solution)/shard_map/ppermute | solution.py:24
  174.2 14.7 %all-to-all-start.3 = ((bf16[8,16,1920]{2,1,0:T(8,128)(2,1)}), bf16[8,16,1920]{2,1,0:T(8,128)(2,1)S(1)}, u32[]{:S(2)}, u32[]{:S(2)}) async-start(bf16[8,16,1920]{2,1,0:T(8,128)(2,1)} %bitcast.16), calls=%async_computation.3 | async-start | bytes 983040 | tf_op jit(solution)/shard_map/all_to_all | solution.py:44
  (9 other events, 36.4 us)

commit v3 on v2

v3 whole, which is shorter than its diff:
```python
import functools
import jax
import jax.numpy as jnp
from jax import lax
from jax.experimental import pallas as pl
from jax.experimental.pallas import tpu as pltpu
from jax.sharding import PartitionSpec as P

CONTRACT_MIDDLE = (((1,), (0,)), ((), ()))
CONTRACT_LAST = (((1,), (1,)), ((), ()))
CONTRACT_FIRST = (((0,), (0,)), ((), ()))
CHUNKS = 2
LANES = 128
TOTAL_FLOPS = 20_000_000_000
VMEM_LIMIT = 20 * 1024 * 1024
BF16 = jnp.bfloat16
F32 = jnp.float32


def dot(left, right, dims=CONTRACT_MIDDLE):
    return lax.dot_general(left, right, dims, preferred_element_type=F32)


def shift(array, steps):
    size = lax.axis_size("gz")
    return lax.ppermute(array, "gz", [(i, (i + steps) % size) for i in range(size)])


def swap(array, bit):
    if bit:
        pairs = [(1, 2), (2, 1), (3, 0), (0, 3)]
    else:
        pairs = [(0, 1), (1, 0), (2, 3), (3, 2)]
    return lax.ppermute(array, "gy", pairs)


def add(left, right):
    return left.astype(F32) + right.astype(F32)


def fence(*arrays):
    return lax.optimization_barrier(arrays)


def to_experts(rows):
    return lax.all_to_all(rows, "gx", split_axis=0, concat_axis=0, tiled=True)


def call(kernel, outs, scratch, args, aliases=None, free=(), in_hbm=(), out_hbm=(), flops=1):
    vmem, hbm = pl.BlockSpec(memory_space=pltpu.VMEM), pl.BlockSpec(memory_space=pltpu.HBM)
    return pl.pallas_call(
        kernel,
        out_shape=[
            pltpu.HBM(*o) if i in out_hbm else jax.ShapeDtypeStruct(*o)
            for i, o in enumerate(outs)
        ],
        in_specs=[
            hbm if i in in_hbm else pl.BlockSpec(memory_space=pl.ANY) if i in free else vmem
            for i in range(len(args))
        ],
        out_specs=[hbm if i in out_hbm else vmem for i in range(len(outs))],
        scratch_shapes=scratch,
        input_output_aliases=aliases or {},
        cost_estimate=pl.CostEstimate(flops=flops, bytes_accessed=1, transcendentals=0),
        compiler_params=pltpu.CompilerParams(vmem_limit_bytes=VMEM_LIMIT),
    )(*args)


def hold_kernel(*refs):
    count = len(refs) // 2
    copies = [
        pltpu.make_async_copy(refs[i], refs[count + i], refs[-1].at[i]) for i in range(count)
    ]
    for copy in copies:
        copy.start()
    for copy in copies:
        copy.wait()


def hold(arrays):
    copies = pl.pallas_call(
        hold_kernel,
        out_shape=[pltpu.VMEM(a.shape, a.dtype) for a in arrays],
        in_specs=[pl.BlockSpec(memory_space=pltpu.HBM)] * len(arrays),
        out_specs=[pl.BlockSpec(memory_space=pltpu.VMEM)] * len(arrays),
        scratch_shapes=[pltpu.SemaphoreType.DMA((len(arrays),))],
        compiler_params=pltpu.CompilerParams(vmem_limit_bytes=VMEM_LIMIT),
    )(*arrays)
    return [pltpu.with_memory_space_constraint(a, pltpu.VMEM) for a in copies]


def partial_kernel(pieces, base, aliased, held, *refs):
    inputs, refs = refs[:pieces], refs[pieces:]
    weights = refs[:3]
    refs = refs[4:] if aliased else refs[3:]
    if held:
        *outs, all_rows, rows, sems = refs
    else:
        *outs, all_rows, rows, sems, w_gate, w_up, w_down, w_sems = refs
        copies = [
            pltpu.make_async_copy(w, v, w_sems.at[i])
            for i, (w, v) in enumerate(zip(weights, (w_gate, w_up, w_down)))
        ]
        weights = (w_gate, w_up, w_down)
    w_copies = [] if held else copies
    width, units = weights[0].shape
    at, copies = 0, []
    for i, piece in enumerate(inputs):
        place = pl.ds(at, piece.shape[0])
        copies.append(pltpu.make_async_copy(piece, rows.at[place], sems.at[i]))
        at += piece.shape[0]
    for copy in copies + w_copies:
        copy.start()
    for copy in copies:
        copy.wait()
    keep = pltpu.make_async_copy(rows, all_rows.at[pl.ds(base, at)], sems.at[pieces])
    keep.start()
    size = at // len(outs)

    def store(k, left, dims):
        if not held:
            w_copies[k].wait()
        part = dot(left, weights[k][...], dims)
        for i, out in enumerate(outs):
            out[:, k * units : (k + 1) * units] = part[i * size : (i + 1) * size].astype(BF16)

    store(0, rows[:, :width], CONTRACT_MIDDLE)
    store(1, rows[:, :width], CONTRACT_MIDDLE)
    store(2, rows[:, width:], CONTRACT_LAST)
    keep.wait()


def partial(pieces, weights, all_rows, base, total_rows, held):
    count = sum(p.shape[0] for p in pieces)
    width, units = weights[0].shape
    n = len(pieces)
    args = list(pieces) + list(weights)
    aliases, in_hbm = {}, () if held else (n, n + 1, n + 2)
    if all_rows is not None:
        aliases, in_hbm = {len(args): 2}, in_hbm + (n + 3,)
        args.append(all_rows)
    scratch = [pltpu.VMEM((count, 2 * width), BF16), pltpu.SemaphoreType.DMA((n + 1,))]
    if not held:
        scratch += [pltpu.VMEM(w.shape, BF16) for w in weights]
        scratch.append(pltpu.SemaphoreType.DMA((3,)))
    return call(
        functools.partial(partial_kernel, n, base, all_rows is not None, held),
        [((count // 2, 3 * units), BF16)] * 2 + [((total_rows, 2 * width), BF16)],
        scratch,
        args,
        aliases,
        tuple(range(n)),
        in_hbm,
        (2,),
    )


def add_kernel(top, top_in, bottom, bottom_in, top_out, bottom_out):
    top_out[...] = add(top[...], top_in[...]).astype(BF16)
    bottom_out[...] = add(bottom[...], bottom_in[...]).astype(BF16)


def add_halves(top, top_in, bottom, bottom_in):
    return call(
        add_kernel,
        [(top.shape, BF16), (bottom.shape, BF16)],
        [],
        [top, top_in, bottom, bottom_in],
    )


def two_parts(score):
    high = score.astype(BF16).astype(F32)
    lane = lax.broadcasted_iota(jnp.int32, (score.shape[0], LANES), 1)
    return jnp.where(lane == 0, high, jnp.where(lane == 1, score - high, 0.0)).astype(BF16)


def act_kernel(pairs, base, layout, aliased, *refs):
    values, refs = refs[: 2 * pairs], refs[2 * pairs :]
    w_gate, w_up = refs[:2]
    refs = refs[4:] if aliased else refs[2:]
    *outs, all_hidden, all_both, hidden_rows, both_rows, sems = refs
    width, units = w_gate.shape
    size = values[0].shape[0]
    scores = []
    for i in range(pairs):
        own, arrived = values[2 * i], values[2 * i + 1]
        place = slice(i * size, (i + 1) * size)
        gate_value = add(own[:, :units], arrived[:, :units])
        up_value = add(own[:, units : 2 * units], arrived[:, units : 2 * units])
        hidden_grad = add(own[:, 2 * units :], arrived[:, 2 * units :])
        sigmoid_gate = jax.nn.sigmoid(gate_value)
        activated = gate_value * sigmoid_gate
        hidden = (activated * up_value).astype(BF16)
        score_part = jnp.sum(hidden.astype(F32) * hidden_grad, axis=1, keepdims=True)
        scores.append(two_parts(score_part))
        hidden_rows[place] = hidden
        both_rows[place, :units] = (
            hidden_grad * up_value * sigmoid_gate * (1.0 + gate_value * (1.0 - sigmoid_gate))
        ).astype(BF16)
        both_rows[place, units:] = (hidden_grad * activated).astype(BF16)
    place = pl.ds(base, pairs * size)
    copies = [
        pltpu.make_async_copy(hidden_rows, all_hidden.at[place], sems.at[0]),
        pltpu.make_async_copy(both_rows, all_both.at[place], sems.at[1]),
    ]
    for copy in copies:
        copy.start()
    part = dot(both_rows[:, :units], w_gate[...], CONTRACT_LAST)
    part = (part + dot(both_rows[:, units:], w_up[...], CONTRACT_LAST)).astype(BF16)
    for out, blocks in zip(outs, layout):
        at = 0
        for i, first, last in blocks:
            end = at + last - first
            out[at:end, :width] = part[i * size + first : i * size + last]
            out[at:end, width:] = scores[i][first:last]
            at = end
    for copy in copies:
        copy.wait()


def act(pairs, weights, gathered, base, layout, total_rows):
    width, units = weights[0].shape
    rows = sum(own.shape[0] for own, _ in pairs)
    args = [a for pair in pairs for a in pair] + [weights[0], weights[1]]
    outs = [
        ((sum(last - first for _, first, last in blocks), width + LANES), BF16)
        for blocks in layout
    ]
    n = len(outs)
    outs += [((total_rows, units), BF16), ((total_rows, 2 * units), BF16)]
    aliases, in_hbm = {}, ()
    if gathered is not None:
        in_hbm = (len(args), len(args) + 1)
        aliases = {in_hbm[0]: n, in_hbm[1]: n + 1}
        args += list(gathered)
    return call(
        functools.partial(act_kernel, len(pairs), base, layout, gathered is not None),
        outs,
        [
            pltpu.VMEM((rows, units), BF16),
            pltpu.VMEM((rows, 2 * units), BF16),
            pltpu.SemaphoreType.DMA((2,)),
        ],
        args,
        aliases,
        (),
        in_hbm,
        (n, n + 1),
    )


def total_kernel(width, own, first, second, third, out):
    total = add(own[...], first[...]) + add(second[...], third[...])
    out[:, :width] = total[:, :width].astype(BF16)
    out[:, width:] = two_parts(jnp.sum(total[:, width:], axis=1, keepdims=True))


def total_of(own, first, second, third, flops=1):
    kernel = functools.partial(total_kernel, own.shape[1] - LANES)
    args = [own, first, second, third]
    return call(kernel, [(own.shape, BF16)], [], args, flops=flops)[0]


def final_kernel(chunks, usable, score, *refs):
    picks, backs = refs[:chunks], refs[chunks : 2 * chunks]
    input_grad, score_grad = refs[2 * chunks :]
    width = input_grad.shape[1]
    experts, slots = score.shape
    rows = backs[0].shape[0]
    part_slots = rows // experts
    total = sum(dot(p[...], b[:, :width], CONTRACT_FIRST) for p, b in zip(picks, backs))
    input_grad[...] = total.astype(BF16)
    row = lax.broadcasted_iota(jnp.int32, (rows, slots), 0)
    column = lax.broadcasted_iota(jnp.int32, (rows, slots), 1)
    expert = (
        lax.broadcasted_iota(jnp.int32, (experts, rows), 1) // part_slots
        == lax.broadcasted_iota(jnp.int32, (experts, rows), 0)
    ).astype(F32).astype(BF16)
    table = jnp.zeros((experts, slots), F32)
    for c, back in enumerate(backs):
        for k in range(2):
            value = back[:, width + k : width + k + 1].astype(F32)
            spread = jnp.where(column == c * part_slots + row % part_slots, value, 0.0)
            table += dot(expert, spread.astype(BF16))
    score_grad[...] = jnp.where(usable[...] > 0, table / score[...], 0.0)


def final(usable, score, picks, backs):
    group, width = picks[0].shape[1], backs[0].shape[1] - LANES
    return call(
        functools.partial(final_kernel, len(picks)),
        [((group, width), BF16), (score.shape, F32)],
        [],
        [usable.astype(jnp.int32), score.astype(F32), *picks, *backs],
    )


def local(
    tokens, grad_out, slot_token, slot_count, slot_score, gate_weight, up_weight, down_weight
):
    chosen = slot_token[0]
    counts = slot_count[0]
    experts, slots = chosen.shape
    group, width = tokens.shape
    usable = jnp.arange(slots, dtype=jnp.int32)[None, :] < counts[:, None]
    score = slot_score[0]
    picked = (
        chosen[:, :, None] == jnp.arange(group, dtype=jnp.int32)[None, None, :]
    ) & usable[:, :, None]
    zero = jnp.zeros((), BF16)
    pick = jnp.where(picked, jnp.ones((), BF16), zero)
    pick_scaled = jnp.where(picked, score[:, :, None], zero)

    weights = [
        pltpu.with_memory_space_constraint(w[0], pltpu.HBM)
        for w in (gate_weight, up_weight, down_weight)
    ]
    units = weights[2].shape[0]
    part_slots = slots // CHUNKS
    own_rows = experts * part_slots
    half = own_rows // 2
    total_rows = own_rows * CHUNKS * lax.axis_size("gz")

    def chunk_of(array, c):
        return array[:, c * part_slots : (c + 1) * part_slots].reshape(own_rows, -1)

    picks = [chunk_of(pick, c) for c in range(CHUNKS)]
    scaled_picks = [chunk_of(pick_scaled, c) for c in range(CHUNKS)]

    def dispatch(pick_x, pick_g):
        return jnp.concatenate(
            [dot(pick_x, tokens).astype(BF16), dot(pick_g, grad_out).astype(BF16)], axis=1
        )

    sent0 = dispatch(picks[0], scaled_picks[0])
    own0 = to_experts(sent0)
    sent0, pick1 = fence(sent0, picks[1])
    sent1 = dispatch(pick1, scaled_picks[1])
    own0, sent1 = fence(own0, sent1)
    before0, after0 = shift(own0, 1), shift(own0, -1)
    own1 = to_experts(sent1)
    a_top, a_bottom, all_rows = partial((own0,), weights, None, 0, total_rows, False)
    a_top_in, a_bottom_in = swap(a_top, 0), swap(a_bottom, 1)
    a_top, a_bottom = add_halves(a_top, a_top_in, a_bottom, a_bottom_in)
    a_top_in, a_bottom_in = swap(a_top, 1), swap(a_bottom, 0)
    own1, all_rows, a_top = fence(own1, all_rows, a_top)
    b_top, b_bottom, all_rows = partial((own1,), weights, all_rows, own_rows, total_rows, False)
    a_top_in, a_bottom_in, b_top, b_bottom = fence(a_top_in, a_bottom_in, b_top, b_bottom)
    b_top_in, b_bottom_in = swap(b_top, 0), swap(b_bottom, 1)
    before0, after0, b_top = fence(before0, after0, b_top)
    cut_top0, cut_bottom0 = before0[:half], after0[half:]
    far_top0, far_bottom0 = shift(cut_top0, 1), shift(cut_bottom0, -1)
    cut_top0, cut_bottom0, *weights = fence(cut_top0, cut_bottom0, *weights)
    held = hold(weights)
    b_top_in, b_bottom_in, cut_top0, cut_bottom0, *held = fence(
        b_top_in, b_bottom_in, cut_top0, cut_bottom0, *held
    )
    b_top, b_bottom = add_halves(b_top, b_top_in, b_bottom, b_bottom_in)
    b_top_in, b_bottom_in = swap(b_top, 1), swap(b_bottom, 0)
    far_top0, far_bottom0, b_top, b_bottom, own1 = fence(
        far_top0, far_bottom0, b_top, b_bottom, own1
    )
    before1, after1 = shift(own1, 1), shift(own1, -1)
    base0, base1 = CHUNKS * own_rows, (CHUNKS + 3) * own_rows
    top0, bottom0, all_rows = partial(
        (before0, far_top0, after0, far_bottom0), held, all_rows, base0, total_rows, True
    )
    b_top_in, b_bottom_in, top0, bottom0 = fence(b_top_in, b_bottom_in, top0, bottom0)
    top_in0, bottom_in0 = swap(top0, 0), swap(bottom0, 1)
    own_pairs = [
        (a_top, a_top_in),
        (a_bottom, a_bottom_in),
        (b_top, b_top_in),
        (b_bottom, b_bottom_in),
    ]
    own_layout = (((0, 0, half), (1, 0, half)), ((2, 0, half), (3, 0, half)))
    own_part0, own_part1, *gathered = act(own_pairs, held, None, 0, own_layout, total_rows)
    before1, after1, own_part0 = fence(before1, after1, own_part0)
    cut_top1, cut_bottom1 = before1[:half], after1[half:]
    far_top1, far_bottom1 = shift(cut_top1, 1), shift(cut_bottom1, -1)
    top_in0, bottom_in0, cut_top1, cut_bottom1 = fence(
        top_in0, bottom_in0, cut_top1, cut_bottom1
    )
    top0, bottom0 = add_halves(top0, top_in0, bottom0, bottom_in0)
    top_in0, bottom_in0 = swap(top0, 1), swap(bottom0, 0)
    far_top1, far_bottom1, top0, bottom0 = fence(far_top1, far_bottom1, top0, bottom0)
    top1, bottom1, all_rows = partial(
        (before1, far_top1, after1, far_bottom1), held, all_rows, base1, total_rows, True
    )
    top_in1, bottom_in1 = swap(top1, 0), swap(bottom1, 1)
    top_in0, bottom_in0, all_rows = fence(top_in0, bottom_in0, all_rows)
    layout = (
        ((0, 0, own_rows),),
        ((1, 0, own_rows),),
        ((0, own_rows, own_rows + half), (1, own_rows, own_rows + half)),
    )
    near_top0, near_bottom0, far0, *gathered = act(
        [(top0, top_in0), (bottom0, bottom_in0)], held, gathered, base0, layout, total_rows
    )
    home0 = [shift(near_top0, -1), shift(near_bottom0, 1), shift(far0, 2)]
    top_in1, bottom_in1, far0 = fence(top_in1, bottom_in1, far0)
    top1, bottom1 = add_halves(top1, top_in1, bottom1, bottom_in1)
    top_in1, bottom_in1 = swap(top1, 1), swap(bottom1, 0)
    *home0, top1, bottom1 = fence(*home0, top1, bottom1)
    total0 = total_of(own_part0, *home0, flops=TOTAL_FLOPS)
    top_in1, bottom_in1, top1, total0 = fence(top_in1, bottom_in1, top1, total0)
    near_top1, near_bottom1, far1, *gathered = act(
        [(top1, top_in1), (bottom1, bottom_in1)], held, gathered, base1, layout, total_rows
    )
    total0, far1 = fence(total0, far1)
    home1 = [shift(near_top1, -1), shift(near_bottom1, 1), shift(far1, 2)]
    back0 = to_experts(total0)
    all_hidden, all_both = gathered
    total0, all_rows, all_hidden, all_both = fence(total0, all_rows, all_hidden, all_both)
    gate_grad = dot(all_rows[:, :width], all_both[:, :units], CONTRACT_FIRST).astype(BF16)
    up_grad = dot(all_rows[:, :width], all_both[:, units:], CONTRACT_FIRST).astype(BF16)
    *home1, gate_grad, up_grad = fence(*home1, gate_grad, up_grad)
    total1 = total_of(own_part1, *home1)
    total1, back0 = fence(total1, back0)
    back1 = to_experts(total1)
    total1, all_hidden = fence(total1, all_hidden)
    down_grad = dot(all_hidden, all_rows[:, width:], CONTRACT_FIRST).astype(BF16)
    back1, down_grad = fence(back1, down_grad)
    input_grad, score_grad = final(usable, score, picks, [back0, back1])
    return input_grad, score_grad[None], gate_grad[None], up_grad[None], down_grad[None]


def solution(mesh):
    in_specs = (
        P(("gx", "gz"), "gy"),
        P(("gx", "gz"), "gy"),
        P(("gx", "gz"), None, None),
        P(("gx", "gz"), None),
        P(("gx", "gz"), None, None),
        P("gx", "gy", "gz"),
        P("gx", "gy", "gz"),
        P("gx", "gz", "gy"),
    )
    out_specs = (
        P(("gx", "gz"), "gy"),
        P(("gx", "gz"), None, None),
        P("gx", "gy", "gz"),
        P("gx", "gy", "gz"),
        P("gx", "gz", "gy"),
    )
    return jax.shard_map(local, mesh=mesh, in_specs=in_specs, out_specs=out_specs, check_vma=False)
```

time: 196 us -> 181 us (0.923)
  waiting for transfers between devices: 67.5 us -> 53.1 us
  starting transfers between devices: 55.6 us -> 68.2 us
  Pallas kernels: 37.8 us -> 32.3 us
  local copies, waits for them, and re-layouts: 6.24 us -> 3.3 us
  matrix products: 21.5 us -> 18.7 us
    all_to_all x4, waiting for transfers between devices: 22.6 us -> 14.1 us  [to_experts(): return lax.all_to_all(rows, 'gx', split_axis=0, concat_axis=0, tiled=True)]
    pallas_call x12 -> x14, Pallas kernels: 37.8 us -> 29.7 us  [call(): pl.pallas_call(kernel, out_shape=[pltpu.HBM(*o) if i in out_hbm else jax....]
    ppermute x14, waiting for transfers between devices: 30 us -> 22.5 us  [shift(): lax.ppermute(array, 'gz', [(i, (i + steps) % size) for i in range(size)])]
    ppermute x14, starting transfers between devices: 12.3 us -> 19.5 us  [shift(): lax.ppermute(array, 'gz', [(i, (i + steps) % size) for i in range(size)])]
    ppermute x12 -> x16, starting transfers between devices: 13.4 us -> 16.5 us  [swap(): return lax.ppermute(array, 'gy', pairs)]
    dot_general x8 -> x7, matrix products: 21.5 us -> 18.7 us  [dot(): return lax.dot_general(left, right, dims, preferred_element_type=F32)]
    pallas_call x0 -> x1, Pallas kernels: none -> 2.63 us  [hold(): pl.pallas_call(hold_kernel, out_shape=[pltpu.VMEM(a.shape, a.dtype) for a...]
    all_to_all x4, starting transfers between devices: 29.9 us -> 32.2 us  [to_experts(): return lax.all_to_all(rows, 'gx', split_axis=0, concat_axis=0, tiled=True)]
  transfers between devices with their start and end apart: 30 -> 34, of which waited for: 20 -> 19; matrix products, arithmetic and copies ran while one was open for 10% -> 10% of each run, Pallas kernels for 15% -> 14%
where the time goes in v3:
time: 181 us; the launch traced here: 180 us
  starting transfers between devices  68.2 us (38%)
  waiting for transfers between devices  53.1 us (29%)
  Pallas kernels  32.3 us (18%)
  matrix products  18.7 us (10%)
  other arithmetic  3.72 us (2%)
  local copies, waits for them, and re-layouts  3.3 us (2%)
    all_to_all x4, starting transfers between devices, to_experts(): return lax.all_to_all(rows, 'gx', split_axis=0, concat_axis=0, tiled=True)  32.2 us
    pallas_call x14, Pallas kernels, call(): pl.pallas_call(kernel, out_shape=[pltpu.HBM(*o) if i in out_hbm else jax....  29.7 us
    ppermute x14, waiting for transfers between devices, shift(): lax.ppermute(array, 'gz', [(i, (i + steps) % size) for i in range(size)])  22.5 us
    ppermute x14, starting transfers between devices, shift(): lax.ppermute(array, 'gz', [(i, (i + steps) % size) for i in range(size)])  19.5 us
    dot_general x7, matrix products, dot(): return lax.dot_general(left, right, dims, preferred_element_type=F32)  18.7 us
    ppermute x16, starting transfers between devices, swap(): return lax.ppermute(array, 'gy', pairs)  16.5 us
    ppermute x16, waiting for transfers between devices, swap(): return lax.ppermute(array, 'gy', pairs)  16.5 us
    all_to_all x4, waiting for transfers between devices, to_experts(): return lax.all_to_all(rows, 'gx', split_axis=0, concat_axis=0, tiled=True)  14.1 us
  transfers between devices with their start and end apart: 34, of which 19 were waited for; matrix products, arithmetic and copies ran while one was open for 10% of the time, Pallas kernels for 14%

profile of v3, /device:TPU:1, one launch (start us, length us, event | category | flops | bytes accessed | tf_op | source)
XLA Modules:
  0.0 180.2 jit_solution(7058725296033773602)
XLA Ops:
  5.3 5.8 %all-to-all-start = ((bf16[8,16,3584]{2,1,0:T(8,128)(2,1)}), bf16[8,16,3584]{2,1,0:T(8,128)(2,1)S(1)}, u32[]{:S(2)}, u32[]{:S(2)}) async-start(bf16[8,16,3584]{2,1,0:T(8,128)(2,1)} %bitcast.55), calls=%async_computation | async-start | bytes 1835008 | tf_op jit(solution)/shard_map/all_to_all | solution.py:46
  14.0 10.8 %all-to-all-done = bf16[8,16,3584]{2,1,0:T(8,128)(2,1)S(1)} async-done(((bf16[8,16,3584]{2,1,0:T(8,128)(2,1)}), bf16[8,16,3584]{2,1,0:T(8,128)(2,1)S(1)}, u32[]{:S(2)}, u32[]{:S(2)}) %all-to-all-start) | async-done | bytes 917536 | tf_op jit(solution)/shard_map/all_to_all | solution.py:46
  26.5 2.1 %collective-permute-start.5 = (bf16[128,3584]{1,0:T(8,128)(2,1)S(1)}, bf16[128,3584]{1,0:T(8,128)(2,1)}, u32[]{:S(2)}, u32[]{:S(2)}) collective-permute-start(bf16[128,3584]{1,0:T(8,128)(2,1)S(1)} %bitcast.33), channel_id=1, source_target_pairs={{0,3},{1,0},{2,1},{3,2},{4,7},{5,4},{6,5},{7,6},{8,11},{9,8},{10,9... | collective-permute-start | bytes 2752520 | tf_op jit(solution)/shard_map/ppermute | solution.py:26
  28.6 4.6 %all-to-all-start.1 = ((bf16[8,16,3584]{2,1,0:T(8,128)(2,1)}), bf16[8,16,3584]{2,1,0:T(8,128)(2,1)S(1)}, u32[]{:S(2)}, u32[]{:S(2)}) async-start(bf16[8,16,3584]{2,1,0:T(8,128)(2,1)} %bitcast.54), calls=%async_computation.1 | async-start | bytes 1835008 | tf_op jit(solution)/shard_map/all_to_all | solution.py:46
  33.2 3.9 %shard_map.119 = (bf16[64,1536]{1,0:T(8,128)(2,1)S(1)}, bf16[64,1536]{1,0:T(8,128)(2,1)S(1)}, bf16[1024,3584]{1,0:T(8,128)(2,1)}) custom-call(bf16[128,3584]{1,0:T(8,128)(2,1)S(1)} %bitcast.34, bf16[1792,512]{1,0:T(8,128)(2,1)} %bitcast.45, bf16[1792,512]{1,0:T(8,128)(2,1)} %bitcast.48, bf16[512,1792]{1,0:T(8,128)(2,1)} %bitcast.51), custom_call_target="tpu_custom_call" | custom-call | flops 1 | bytes 1 | tf_op jit(solution)/shard_map/pallas_call | solution.py:51
  38.5 1.9 %collective-permute-start.1 = (bf16[64,1536]{1,0:T(8,128)(2,1)S(1)}, bf16[64,1536]{1,0:T(8,128)(2,1)S(1)}, u32[]{:S(2)}, u32[]{:S(2)}) collective-permute-start(bf16[64,1536]{1,0:T(8,128)(2,1)S(1)} %get-tuple-element.117.bottom), channel_id=1, source_target_pairs={{4,8},{8,4},{12,0},{0,12},{5,9},{9,5},{13,1},{1,13},{6,10},{10,6},... | collective-permute-start | bytes 589832 | tf_op jit(solution)/shard_map/ppermute | solution.py:34
  40.4 3.2 %collective-permute-done.top_in = bf16[64,1536]{1,0:T(8,128)(2,1)S(1)} collective-permute-done((bf16[64,1536]{1,0:T(8,128)(2,1)S(1)}, bf16[64,1536]{1,0:T(8,128)(2,1)S(1)}, u32[]{:S(2)}, u32[]{:S(2)}) %collective-permute-start) | collective-permute-done | bytes 196640 | tf_op jit(solution)/shard_map/ppermute | solution.py:34
  43.7 2.2 %collective-permute-done.1.bottom_in = bf16[64,1536]{1,0:T(8,128)(2,1)S(1)} collective-permute-done((bf16[64,1536]{1,0:T(8,128)(2,1)S(1)}, bf16[64,1536]{1,0:T(8,128)(2,1)S(1)}, u32[]{:S(2)}, u32[]{:S(2)}) %collective-permute-start.1) | collective-permute-done | bytes 196640 | tf_op jit(solution)/shard_map/ppermute | solution.py:34
  46.0 2.0 %collective-permute-start.2 = (bf16[64,1536]{1,0:T(8,128)(2,1)S(1)}, bf16[64,1536]{1,0:T(8,128)(2,1)}, u32[]{:S(2)}, u32[]{:S(2)}) collective-permute-start(bf16[64,1536]{1,0:T(8,128)(2,1)S(1)} %get-tuple-element.119.refs_0_), channel_id=1, source_target_pairs={{4,8},{8,4},{12,0},{0,12},{5,9},{9,5},{13,1},{1,13},{6,10},{10,6},... | collective-permute-start | bytes 589832 | tf_op jit(solution)/shard_map/ppermute | solution.py:34
  47.9 3.9 %shard_map.121 = (bf16[64,1536]{1,0:T(8,128)(2,1)S(1)}, bf16[64,1536]{1,0:T(8,128)(2,1)S(1)}, bf16[1024,3584]{1,0:T(8,128)(2,1)}) custom-call(bf16[128,3584]{1,0:T(8,128)(2,1)S(1)} %bitcast.35, bf16[1792,512]{1,0:T(8,128)(2,1)} %bitcast.46, bf16[1792,512]{1,0:T(8,128)(2,1)} %bitcast.49, bf16[512,1792]{1,0:T(8,128)(2,1)} %bitcast.52, ...), custom_call_target="tpu_custom_call", output_to_operand_aliasing={{2}: (4, {})} | custom-call | flops 1 | bytes 1 | tf_op jit(solution)/shard_map/pallas_call | solution.py:51
  54.1 2.7 %collective-permute-start.7 = (bf16[64,3584]{1,0:T(8,128)(2,1)S(1)}, bf16[64,3584]{1,0:T(8,128)(2,1)S(1)}, u32[]{:S(2)}, u32[]{:S(2)}) collective-permute-start(bf16[64,3584]{1,0:T(8,128)(2,1)S(1)} %slice.42), channel_id=1, source_target_pairs={{0,3},{1,0},{2,1},{3,2},{4,7},{5,4},{6,5},{7,6},{8,11},{9,8},{10,9... | collective-permute-start | bytes 1376264 | tf_op jit(solution)/shard_map/ppermute | solution.py:26
  58.3 2.6 %shard_map.122 = (bf16[1792,512]{1,0:T(8,128)(2,1)S(1)}, bf16[1792,512]{1,0:T(8,128)(2,1)S(1)}, bf16[512,1792]{1,0:T(8,128)(2,1)S(1)}) custom-call(bf16[1792,512]{1,0:T(8,128)(2,1)} %bitcast.47, bf16[1792,512]{1,0:T(8,128)(2,1)} %bitcast.50, bf16[512,1792]{1,0:T(8,128)(2,1)} %bitcast.53), custom_call_target="tpu_custom_call" | custom-call | tf_op jit(solution)/shard_map/pallas_call | solution.py:81
  65.0 2.7 %collective-permute-start.13 = (bf16[128,3584]{1,0:T(8,128)(2,1)S(1)}, bf16[128,3584]{1,0:T(8,128)(2,1)S(1)}, u32[]{:S(2)}, u32[]{:S(2)}) collective-permute-start(bf16[128,3584]{1,0:T(8,128)(2,1)S(1)} %bitcast.37), channel_id=1, source_target_pairs={{0,3},{1,0},{2,1},{3,2},{4,7},{5,4},{6,5},{7,6},{8,11},{9,8},{10,9... | collective-permute-start | bytes 2752520 | tf_op jit(solution)/shard_map/ppermute | solution.py:26
  69.4 4.0 %shard_map.124 = (bf16[192,1536]{1,0:T(8,128)(2,1)S(1)}, bf16[192,1536]{1,0:T(8,128)(2,1)S(1)}, bf16[1024,3584]{1,0:T(8,128)(2,1)}) custom-call(bf16[128,3584]{1,0:T(8,128)(2,1)S(1)} %collective-permute-done.4.refs_0_, bf16[64,3584]{1,0:T(8,128)(2,1)S(1)} %collective-permute-done.6.refs_1_, ...), custom_call_target="tpu_custom_call", output_to_operand_aliasing={{2}: (7, {})} | custom-call | flops 1 | bytes 1 | tf_op jit(solution)/shard_map/pallas_call | solution.py:51
  75.9 3.1 %shard_map.125 = (bf16[128,1920]{1,0:T(8,128)(2,1)S(1)}, bf16[128,1920]{1,0:T(8,128)(2,1)S(1)}, bf16[1024,512]{1,0:T(8,128)(2,1)}, bf16[1024,1024]{1,0:T(8,128)(2,1)}) custom-call(bf16[64,1536]{1,0:T(8,128)(2,1)S(1)} %get-tuple-element.119.refs_0_, bf16[64,1536]{1,0:T(8,128)(2,1)} %collective-permute-done.2.refs_1_, ...), custom_call_target="tpu_custom_call" | custom-call | flops 1 | bytes 1 | tf_op jit(solution)/shard_map/pallas_call | solution.py:51
  79.0 5.7 %collective-permute-done.12.refs_0_ = bf16[128,3584]{1,0:T(8,128)(2,1)S(1)} collective-permute-done((bf16[128,3584]{1,0:T(8,128)(2,1)S(1)}, bf16[128,3584]{1,0:T(8,128)(2,1)S(1)}, u32[]{:S(2)}, u32[]{:S(2)}) %collective-permute-start.12) | collective-permute-done | bytes 917536 | tf_op jit(solution)/shard_map/ppermute | solution.py:26
  87.5 2.6 %collective-permute-start.15 = (bf16[64,3584]{1,0:T(8,128)(2,1)S(1)}, bf16[64,3584]{1,0:T(8,128)(2,1)S(1)}, u32[]{:S(2)}, u32[]{:S(2)}) collective-permute-start(bf16[64,3584]{1,0:T(8,128)(2,1)S(1)} %slice.44), channel_id=1, source_target_pairs={{0,3},{1,0},{2,1},{3,2},{4,7},{5,4},{6,5},{7,6},{8,11},{9,8},{10,9... | collective-permute-start | bytes 1376264 | tf_op jit(solution)/shard_map/ppermute | solution.py:26
  90.1 5.9 %collective-permute-done.14.refs_1_ = bf16[64,3584]{1,0:T(8,128)(2,1)S(1)} collective-permute-done((bf16[64,3584]{1,0:T(8,128)(2,1)S(1)}, bf16[64,3584]{1,0:T(8,128)(2,1)S(1)}, u32[]{:S(2)}, u32[]{:S(2)}) %collective-permute-start.14) | collective-permute-done | bytes 458784 | tf_op jit(solution)/shard_map/ppermute | solution.py:26
  96.0 3.3 %shard_map.127 = (bf16[192,1536]{1,0:T(8,128)(2,1)S(1)}, bf16[192,1536]{1,0:T(8,128)(2,1)S(1)}, bf16[1024,3584]{1,0:T(8,128)(2,1)}) custom-call(bf16[128,3584]{1,0:T(8,128)(2,1)S(1)} %collective-permute-done.12.refs_0_, bf16[64,3584]{1,0:T(8,128)(2,1)S(1)} %collective-permute-done.14.refs_1_, ...), custom_call_target="tpu_custom_call", output_to_operand_aliasing={{2}: (7, {})} | custom-call | flops 1 | bytes 1 | tf_op jit(solution)/shard_map/pallas_call | solution.py:51
  102.3 2.8 %shard_map.128 = (bf16[128,1920]{1,0:T(8,128)(2,1)S(1)}, bf16[128,1920]{1,0:T(8,128)(2,1)S(1)}, bf16[128,1920]{1,0:T(8,128)(2,1)S(1)}, bf16[1024,512]{1,0:T(8,128)(2,1)}, bf16[1024,1024]{1,0:T(8,128)(2,1)}) custom-call(bf16[192,1536]{1,0:T(8,128)(2,1)S(1)} %get-tuple-element.170.refs_0_, ...), custom_call_target="tpu_custom_call", output_to_operand_aliasing={{3}: (6, {}), {4}: (7, {})} | custom-call | flops 1 | bytes 1 | tf_op jit(solution)/shard_map/pallas_call | solution.py:51
  105.1 2.7 %collective-permute-start.24 = (bf16[128,1920]{1,0:T(8,128)(2,1)S(1)}, bf16[128,1920]{1,0:T(8,128)(2,1)S(1)}, u32[]{:S(2)}, u32[]{:S(2)}) collective-permute-start(bf16[128,1920]{1,0:T(8,128)(2,1)S(1)} %get-tuple-element.182), channel_id=1, source_target_pairs={{0,3},{1,0},{2,1},{3,2},{4,7},{5,4},{6,5},{7,6},{8,11},{9,8},{10,9... | collective-permute-start | bytes 1474568 | tf_op jit(solution)/shard_map/ppermute | solution.py:26
  113.0 5.9 %collective-permute-done.24.first = bf16[128,1920]{1,0:T(8,128)(2,1)S(1)} collective-permute-done((bf16[128,1920]{1,0:T(8,128)(2,1)S(1)}, bf16[128,1920]{1,0:T(8,128)(2,1)S(1)}, u32[]{:S(2)}, u32[]{:S(2)}) %collective-permute-start.24) | collective-permute-done | bytes 491552 | tf_op jit(solution)/shard_map/ppermute | solution.py:26
  118.9 3.4 %collective-permute-done.25.second = bf16[128,1920]{1,0:T(8,128)(2,1)S(1)} collective-permute-done((bf16[128,1920]{1,0:T(8,128)(2,1)S(1)}, bf16[128,1920]{1,0:T(8,128)(2,1)S(1)}, u32[]{:S(2)}, u32[]{:S(2)}) %collective-permute-start.25) | collective-permute-done | bytes 491552 | tf_op jit(solution)/shard_map/ppermute | solution.py:26
  122.8 4.1 %collective-permute-done.22.refs_1_ = bf16[192,1536]{1,0:T(8,128)(2,1)S(1)} collective-permute-done((bf16[192,1536]{1,0:T(8,128)(2,1)S(1)}, bf16[192,1536]{1,0:T(8,128)(2,1)S(1)}, u32[]{:S(2)}, u32[]{:S(2)}) %collective-permute-start.22) | collective-permute-done | bytes 589856 | tf_op jit(solution)/shard_map/ppermute | solution.py:34
  126.9 3.8 %shard_map.131 = (bf16[128,1920]{1,0:T(8,128)(2,1)}, bf16[128,1920]{1,0:T(8,128)(2,1)}, bf16[128,1920]{1,0:T(8,128)(2,1)}, bf16[1024,512]{1,0:T(8,128)(2,1)}, bf16[1024,1024]{1,0:T(8,128)(2,1)}) custom-call(bf16[192,1536]{1,0:T(8,128)(2,1)S(1)} %get-tuple-element.189.refs_0_, ...), custom_call_target="tpu_custom_call", output_to_operand_aliasing={{3}: (6, {}), {4}: (7, {})} | custom-call | flops 1 | bytes 1 | tf_op jit(solution)/shard_map/pallas_call | solution.py:51
  134.3 17.0 %all-to-all-start.2 = ((bf16[8,16,1920]{2,1,0:T(8,128)(2,1)}), bf16[8,16,1920]{2,1,0:T(8,128)(2,1)S(1)}, u32[]{:S(2)}, u32[]{:S(2)}) async-start(bf16[8,16,1920]{2,1,0:T(8,128)(2,1)} %bitcast.44), calls=%async_computation.2 | async-start | bytes 983040 | tf_op jit(solution)/shard_map/all_to_all | solution.py:46
  151.3 5.8 %fusion.9 = bf16[1792,512]{1,0:T(8,128)(2,1)} fusion(bf16[1024,3584]{1,0:T(8,128)(2,1)} %get-tuple-element.204, bf16[1024,1024]{1,0:T(8,128)(2,1)} %get-tuple-element.205), kind=kOutput, calls=%fused_computation.7 | convolution fusion | flops 1879965696 | bytes 6553600 | tf_op jit(solution)/shard_map/dot_general | solution.py:21
  157.1 5.4 %fusion.6 = bf16[1792,512]{1,0:T(8,128)(2,1)} fusion(bf16[1024,3584]{1,0:T(8,128)(2,1)} %get-tuple-element.204, bf16[1024,1024]{1,0:T(8,128)(2,1)S(1)} %copy-done.3), kind=kOutput, calls=%fused_computation.6 | convolution fusion | flops 1879965696 | bytes 6553600 | tf_op jit(solution)/shard_map/dot_general | solution.py:21
  163.8 4.8 %all-to-all-start.3 = ((bf16[8,16,1920]{2,1,0:T(8,128)(2,1)}), bf16[8,16,1920]{2,1,0:T(8,128)(2,1)S(1)}, u32[]{:S(2)}, u32[]{:S(2)}) async-start(bf16[8,16,1920]{2,1,0:T(8,128)(2,1)} %bitcast.16), calls=%async_computation.3 | async-start | bytes 983040 | tf_op jit(solution)/shard_map/all_to_all | solution.py:46
  168.6 5.8 %fusion.12 = bf16[512,1792]{1,0:T(8,128)(2,1)} fusion(bf16[1024,512]{1,0:T(8,128)(2,1)} %get-tuple-element.212, bf16[1024,3584]{1,0:T(8,128)(2,1)} %get-tuple-element.204), kind=kOutput, calls=%fused_computation.8 | convolution fusion | flops 1879965696 | bytes 6553600 | tf_op jit(solution)/shard_map/dot_general | solution.py:21
  174.4 3.3 %all-to-all-done.3 = bf16[8,16,1920]{2,1,0:T(8,128)(2,1)S(1)} async-done(((bf16[8,16,1920]{2,1,0:T(8,128)(2,1)}), bf16[8,16,1920]{2,1,0:T(8,128)(2,1)S(1)}, u32[]{:S(2)}, u32[]{:S(2)}) %all-to-all-start.3) | async-done | bytes 491552 | tf_op jit(solution)/shard_map/all_to_all | solution.py:46
  177.8 2.4 %shard_map.133 = (bf16[512,1792]{1,0:T(8,128)(2,1)}, f32[8,32]{1,0:T(8,128)}) custom-call(s32[8,32]{1,0:T(8,128)S(1)} %get-tuple-element.226.usable, f32[8,32]{1,0:T(8,128)S(1)} %bitcast_convert_fusion.score, bf16[128,512]{1,0:T(8,128)(2,1)S(1)} %bitcast.41, bf16[128,512]{1,0:T(8,128)(2,1)S(1)} %bitcast.43, bf16[128,1920]{1,0:T(8,128)(2,1)S(1)} %bitcast.38, ...), custom_call_target="tpu_custom_call" | custom-call | flops 1 | bytes 1 | tf_op jit(solution)/shard_map/pallas_call | solution.py:51
  (82 shorter events, 39.0 us)
Async XLA Ops:
  5.3 19.5 %all-to-all-start = ((bf16[8,16,3584]{2,1,0:T(8,128)(2,1)}), bf16[8,16,3584]{2,1,0:T(8,128)(2,1)S(1)}, u32[]{:S(2)}, u32[]{:S(2)}) async-start(bf16[8,16,3584]{2,1,0:T(8,128)(2,1)} %bitcast.55), calls=%async_computation | async-start | bytes 1835008 | tf_op jit(solution)/shard_map/all_to_all | solution.py:46
  24.8 28.2 %collective-permute-start.4 = (bf16[128,3584]{1,0:T(8,128)(2,1)S(1)}, bf16[128,3584]{1,0:T(8,128)(2,1)S(1)}, u32[]{:S(2)}, u32[]{:S(2)}) collective-permute-start(bf16[128,3584]{1,0:T(8,128)(2,1)S(1)} %bitcast.32), channel_id=1, source_target_pairs={{0,1},{1,2},{2,3},{3,0},{4,5},{5,6},{6,7},{7,4},{8,9},{9,10},{10,1... | collective-permute-start | bytes 2752520 | tf_op jit(solution)/shard_map/ppermute | solution.py:26
  26.5 26.5 %collective-permute-start.5 = (bf16[128,3584]{1,0:T(8,128)(2,1)S(1)}, bf16[128,3584]{1,0:T(8,128)(2,1)}, u32[]{:S(2)}, u32[]{:S(2)}) collective-permute-start(bf16[128,3584]{1,0:T(8,128)(2,1)S(1)} %bitcast.33), channel_id=1, source_target_pairs={{0,3},{1,0},{2,1},{3,2},{4,7},{5,4},{6,5},{7,6},{8,11},{9,8},{10,9... | collective-permute-start | bytes 2752520 | tf_op jit(solution)/shard_map/ppermute | solution.py:26
  28.6 19.4 %all-to-all-start.1 = ((bf16[8,16,3584]{2,1,0:T(8,128)(2,1)}), bf16[8,16,3584]{2,1,0:T(8,128)(2,1)S(1)}, u32[]{:S(2)}, u32[]{:S(2)}) async-start(bf16[8,16,3584]{2,1,0:T(8,128)(2,1)} %bitcast.54), calls=%async_computation.1 | async-start | bytes 1835008 | tf_op jit(solution)/shard_map/all_to_all | solution.py:46
  37.1 6.6 %collective-permute-start = (bf16[64,1536]{1,0:T(8,128)(2,1)S(1)}, bf16[64,1536]{1,0:T(8,128)(2,1)S(1)}, u32[]{:S(2)}, u32[]{:S(2)}) collective-permute-start(bf16[64,1536]{1,0:T(8,128)(2,1)S(1)} %get-tuple-element.116.top), channel_id=1, source_target_pairs={{0,4},{4,0},{8,12},{12,8},{1,5},{5,1},{9,13},{13,9},{2,6},{6,2},{1... | collective-permute-start | bytes 589832 | tf_op jit(solution)/shard_map/ppermute | solution.py:34
  38.5 7.3 %collective-permute-start.1 = (bf16[64,1536]{1,0:T(8,128)(2,1)S(1)}, bf16[64,1536]{1,0:T(8,128)(2,1)S(1)}, u32[]{:S(2)}, u32[]{:S(2)}) collective-permute-start(bf16[64,1536]{1,0:T(8,128)(2,1)S(1)} %get-tuple-element.117.bottom), channel_id=1, source_target_pairs={{4,8},{8,4},{12,0},{0,12},{5,9},{9,5},{13,1},{1,13},{6,10},{10,6},... | collective-permute-start | bytes 589832 | tf_op jit(solution)/shard_map/ppermute | solution.py:34
  46.0 6.6 %collective-permute-start.2 = (bf16[64,1536]{1,0:T(8,128)(2,1)S(1)}, bf16[64,1536]{1,0:T(8,128)(2,1)}, u32[]{:S(2)}, u32[]{:S(2)}) collective-permute-start(bf16[64,1536]{1,0:T(8,128)(2,1)S(1)} %get-tuple-element.119.refs_0_), channel_id=1, source_target_pairs={{4,8},{8,4},{12,0},{0,12},{5,9},{9,5},{13,1},{1,13},{6,10},{10,6},... | collective-permute-start | bytes 589832 | tf_op jit(solution)/shard_map/ppermute | solution.py:34
  47.9 5.0 %collective-permute-start.3 = (bf16[64,1536]{1,0:T(8,128)(2,1)S(1)}, bf16[64,1536]{1,0:T(8,128)(2,1)}, u32[]{:S(2)}, u32[]{:S(2)}) collective-permute-start(bf16[64,1536]{1,0:T(8,128)(2,1)S(1)} %get-tuple-element.120.refs_2_), channel_id=1, source_target_pairs={{0,4},{4,0},{8,12},{12,8},{1,5},{5,1},{9,13},{13,9},{2,6},{6,2},{1... | collective-permute-start | bytes 589832 | tf_op jit(solution)/shard_map/ppermute | solution.py:34
  54.1 10.9 %collective-permute-start.6 = (bf16[64,3584]{1,0:T(8,128)(2,1)S(1)}, bf16[64,3584]{1,0:T(8,128)(2,1)S(1)}, u32[]{:S(2)}, u32[]{:S(2)}) collective-permute-start(bf16[64,3584]{1,0:T(8,128)(2,1)S(1)} %slice.41), channel_id=1, source_target_pairs={{0,1},{1,2},{2,3},{3,0},{4,5},{5,6},{6,7},{7,4},{8,9},{9,10},{10,1... | collective-permute-start | bytes 1376264 | tf_op jit(solution)/shard_map/ppermute | solution.py:26
  54.1 10.8 %collective-permute-start.7 = (bf16[64,3584]{1,0:T(8,128)(2,1)S(1)}, bf16[64,3584]{1,0:T(8,128)(2,1)S(1)}, u32[]{:S(2)}, u32[]{:S(2)}) collective-permute-start(bf16[64,3584]{1,0:T(8,128)(2,1)S(1)} %slice.42), channel_id=1, source_target_pairs={{0,3},{1,0},{2,1},{3,2},{4,7},{5,4},{6,5},{7,6},{8,11},{9,8},{10,9... | collective-permute-start | bytes 1376264 | tf_op jit(solution)/shard_map/ppermute | solution.py:26
  57.2 6.0 %collective-permute-start.9 = (bf16[64,1536]{1,0:T(8,128)(2,1)S(1)}, bf16[64,1536]{1,0:T(8,128)(2,1)S(1)}, u32[]{:S(2)}, u32[]{:S(2)}) collective-permute-start(bf16[64,1536]{1,0:T(8,128)(2,1)S(1)} %get-tuple-element.131.bottom), channel_id=1, source_target_pairs={{4,8},{8,4},{12,0},{0,12},{5,9},{9,5},{13,1},{1,13},{6,10},{10,6},... | collective-permute-start | bytes 589832 | tf_op jit(solution)/shard_map/ppermute | solution.py:34
  65.0 19.7 %collective-permute-start.12 = (bf16[128,3584]{1,0:T(8,128)(2,1)S(1)}, bf16[128,3584]{1,0:T(8,128)(2,1)S(1)}, u32[]{:S(2)}, u32[]{:S(2)}) collective-permute-start(bf16[128,3584]{1,0:T(8,128)(2,1)S(1)} %bitcast.36), channel_id=1, source_target_pairs={{0,1},{1,2},{2,3},{3,0},{4,5},{5,6},{6,7},{7,4},{8,9},{9,10},{10,1... | collective-permute-start | bytes 2752520 | tf_op jit(solution)/shard_map/ppermute | solution.py:26
  65.0 19.7 %collective-permute-start.13 = (bf16[128,3584]{1,0:T(8,128)(2,1)S(1)}, bf16[128,3584]{1,0:T(8,128)(2,1)S(1)}, u32[]{:S(2)}, u32[]{:S(2)}) collective-permute-start(bf16[128,3584]{1,0:T(8,128)(2,1)S(1)} %bitcast.37), channel_id=1, source_target_pairs={{0,3},{1,0},{2,1},{3,2},{4,7},{5,4},{6,5},{7,6},{8,11},{9,8},{10,9... | collective-permute-start | bytes 2752520 | tf_op jit(solution)/shard_map/ppermute | solution.py:26
  67.6 6.0 %collective-permute-start.10 = (bf16[64,1536]{1,0:T(8,128)(2,1)S(1)}, bf16[64,1536]{1,0:T(8,128)(2,1)S(1)}, u32[]{:S(2)}, u32[]{:S(2)}) collective-permute-start(bf16[64,1536]{1,0:T(8,128)(2,1)S(1)} %get-tuple-element.142.refs_4_), channel_id=1, source_target_pairs={{4,8},{8,4},{12,0},{0,12},{5,9},{9,5},{13,1},{1,13},{6,10},{10,6},... | collective-permute-start | bytes 589832 | tf_op jit(solution)/shard_map/ppermute | solution.py:34
  74.2 11.6 %collective-permute-start.16 = (bf16[192,1536]{1,0:T(8,128)(2,1)S(1)}, bf16[192,1536]{1,0:T(8,128)(2,1)S(1)}, u32[]{:S(2)}, u32[]{:S(2)}) collective-permute-start(bf16[192,1536]{1,0:T(8,128)(2,1)S(1)} %get-tuple-element.159.top), channel_id=1, source_target_pairs={{0,4},{4,0},{8,12},{12,8},{1,5},{5,1},{9,13},{13,9},{2,6},{6,2},{1... | collective-permute-start | bytes 1769480 | tf_op jit(solution)/shard_map/ppermute | solution.py:34
  75.0 10.9 %collective-permute-start.17 = (bf16[192,1536]{1,0:T(8,128)(2,1)S(1)}, bf16[192,1536]{1,0:T(8,128)(2,1)S(1)}, u32[]{:S(2)}, u32[]{:S(2)}) collective-permute-start(bf16[192,1536]{1,0:T(8,128)(2,1)S(1)} %get-tuple-element.160.bottom), channel_id=1, source_target_pairs={{4,8},{8,4},{12,0},{0,12},{5,9},{9,5},{13,1},{1,13},{6,10},{10,6},... | collective-permute-start | bytes 1769480 | tf_op jit(solution)/shard_map/ppermute | solution.py:34
  86.2 16.2 %collective-permute-start.20 = (bf16[192,1536]{1,0:T(8,128)(2,1)S(1)}, bf16[192,1536]{1,0:T(8,128)(2,1)S(1)}, u32[]{:S(2)}, u32[]{:S(2)}) collective-permute-start(bf16[192,1536]{1,0:T(8,128)(2,1)S(1)} %get-tuple-element.170.refs_0_), channel_id=1, source_target_pairs={{4,8},{8,4},{12,0},{0,12},{5,9},{9,5},{13,1},{1,13},{6,10},{10,6},... | collective-permute-start | bytes 1769480 | tf_op jit(solution)/shard_map/ppermute | solution.py:34
  87.5 14.9 %collective-permute-start.21 = (bf16[192,1536]{1,0:T(8,128)(2,1)S(1)}, bf16[192,1536]{1,0:T(8,128)(2,1)S(1)}, u32[]{:S(2)}, u32[]{:S(2)}) collective-permute-start(bf16[192,1536]{1,0:T(8,128)(2,1)S(1)} %get-tuple-element.173.refs_2_), channel_id=1, source_target_pairs={{0,4},{4,0},{8,12},{12,8},{1,5},{5,1},{9,13},{13,9},{2,6},{6,2},{1... | collective-permute-start | bytes 1769480 | tf_op jit(solution)/shard_map/ppermute | solution.py:34
  87.5 8.5 %collective-permute-start.14 = (bf16[64,3584]{1,0:T(8,128)(2,1)S(1)}, bf16[64,3584]{1,0:T(8,128)(2,1)S(1)}, u32[]{:S(2)}, u32[]{:S(2)}) collective-permute-start(bf16[64,3584]{1,0:T(8,128)(2,1)S(1)} %slice.43), channel_id=1, source_target_pairs={{0,1},{1,2},{2,3},{3,0},{4,5},{5,6},{6,7},{7,4},{8,9},{9,10},{10,1... | collective-permute-start | bytes 1376264 | tf_op jit(solution)/shard_map/ppermute | solution.py:26
  87.5 8.5 %collective-permute-start.15 = (bf16[64,3584]{1,0:T(8,128)(2,1)S(1)}, bf16[64,3584]{1,0:T(8,128)(2,1)S(1)}, u32[]{:S(2)}, u32[]{:S(2)}) collective-permute-start(bf16[64,3584]{1,0:T(8,128)(2,1)S(1)} %slice.44), channel_id=1, source_target_pairs={{0,3},{1,0},{2,1},{3,2},{4,7},{5,4},{6,5},{7,6},{8,11},{9,8},{10,9... | collective-permute-start | bytes 1376264 | tf_op jit(solution)/shard_map/ppermute | solution.py:26
  99.3 10.8 %collective-permute-start.18 = (bf16[192,1536]{1,0:T(8,128)(2,1)S(1)}, bf16[192,1536]{1,0:T(8,128)(2,1)S(1)}, u32[]{:S(2)}, u32[]{:S(2)}) collective-permute-start(bf16[192,1536]{1,0:T(8,128)(2,1)S(1)} %get-tuple-element.168.top), channel_id=1, source_target_pairs={{0,4},{4,0},{8,12},{12,8},{1,5},{5,1},{9,13},{13,9},{2,6},{6,2},{1... | collective-permute-start | bytes 1769480 | tf_op jit(solution)/shard_map/ppermute | solution.py:34
  100.9 9.9 %collective-permute-start.19 = (bf16[192,1536]{1,0:T(8,128)(2,1)S(1)}, bf16[192,1536]{1,0:T(8,128)(2,1)S(1)}, u32[]{:S(2)}, u32[]{:S(2)}) collective-permute-start(bf16[192,1536]{1,0:T(8,128)(2,1)S(1)} %get-tuple-element.169.bottom), channel_id=1, source_target_pairs={{4,8},{8,4},{12,0},{0,12},{5,9},{9,5},{13,1},{1,13},{6,10},{10,6},... | collective-permute-start | bytes 1769480 | tf_op jit(solution)/shard_map/ppermute | solution.py:34
  105.1 13.8 %collective-permute-start.24 = (bf16[128,1920]{1,0:T(8,128)(2,1)S(1)}, bf16[128,1920]{1,0:T(8,128)(2,1)S(1)}, u32[]{:S(2)}, u32[]{:S(2)}) collective-permute-start(bf16[128,1920]{1,0:T(8,128)(2,1)S(1)} %get-tuple-element.182), channel_id=1, source_target_pairs={{0,3},{1,0},{2,1},{3,2},{4,7},{5,4},{6,5},{7,6},{8,11},{9,8},{10,9... | collective-permute-start | bytes 1474568 | tf_op jit(solution)/shard_map/ppermute | solution.py:26
  107.9 14.5 %collective-permute-start.25 = (bf16[128,1920]{1,0:T(8,128)(2,1)S(1)}, bf16[128,1920]{1,0:T(8,128)(2,1)S(1)}, u32[]{:S(2)}, u32[]{:S(2)}) collective-permute-start(bf16[128,1920]{1,0:T(8,128)(2,1)S(1)} %get-tuple-element.183), channel_id=1, source_target_pairs={{0,1},{1,2},{2,3},{3,0},{4,5},{5,6},{6,7},{7,4},{8,9},{9,10},{10,1... | collective-permute-start | bytes 1474568 | tf_op jit(solution)/shard_map/ppermute | solution.py:26
  107.9 14.5 %collective-permute-start.26 = (bf16[128,1920]{1,0:T(8,128)(2,1)S(1)}, bf16[128,1920]{1,0:T(8,128)(2,1)S(1)}, u32[]{:S(2)}, u32[]{:S(2)}) collective-permute-start(bf16[128,1920]{1,0:T(8,128)(2,1)S(1)} %get-tuple-element.177), channel_id=1, source_target_pairs={{0,2},{1,3},{2,0},{3,1},{4,6},{5,7},{6,4},{7,5},{8,10},{9,11},{10,... | collective-permute-start | bytes 1474568 | tf_op jit(solution)/shard_map/ppermute | solution.py:26
  111.1 15.8 %collective-permute-start.22 = (bf16[192,1536]{1,0:T(8,128)(2,1)S(1)}, bf16[192,1536]{1,0:T(8,128)(2,1)S(1)}, u32[]{:S(2)}, u32[]{:S(2)}) collective-permute-start(bf16[192,1536]{1,0:T(8,128)(2,1)S(1)} %get-tuple-element.189.refs_0_), channel_id=1, source_target_pairs={{4,8},{8,4},{12,0},{0,12},{5,9},{9,5},{13,1},{1,13},{6,10},{10,6},... | collective-permute-start | bytes 1769480 | tf_op jit(solution)/shard_map/ppermute | solution.py:34
  112.6 14.3 %collective-permute-start.23 = (bf16[192,1536]{1,0:T(8,128)(2,1)S(1)}, bf16[192,1536]{1,0:T(8,128)(2,1)S(1)}, u32[]{:S(2)}, u32[]{:S(2)}) collective-permute-start(bf16[192,1536]{1,0:T(8,128)(2,1)S(1)} %get-tuple-element.191.refs_2_), channel_id=1, source_target_pairs={{0,4},{4,0},{8,12},{12,8},{1,5},{5,1},{9,13},{13,9},{2,6},{6,2},{1... | collective-permute-start | bytes 1769480 | tf_op jit(solution)/shard_map/ppermute | solution.py:34
  130.7 31.8 %collective-permute-start.29 = (bf16[128,1920]{1,0:T(8,128)(2,1)}, bf16[128,1920]{1,0:T(8,128)(2,1)S(1)}, u32[]{:S(2)}, u32[]{:S(2)}) collective-permute-start(bf16[128,1920]{1,0:T(8,128)(2,1)} %get-tuple-element.199), channel_id=1, source_target_pairs={{0,2},{1,3},{2,0},{3,1},{4,6},{5,7},{6,4},{7,5},{8,10},{9,11},{10,... | collective-permute-start | bytes 1474568 | tf_op jit(solution)/shard_map/ppermute | solution.py:26
  132.5 30.0 %collective-permute-start.27 = (bf16[128,1920]{1,0:T(8,128)(2,1)}, bf16[128,1920]{1,0:T(8,128)(2,1)S(1)}, u32[]{:S(2)}, u32[]{:S(2)}) collective-permute-start(bf16[128,1920]{1,0:T(8,128)(2,1)} %get-tuple-element.195), channel_id=1, source_target_pairs={{0,3},{1,0},{2,1},{3,2},{4,7},{5,4},{6,5},{7,6},{8,11},{9,8},{10,9... | collective-permute-start | bytes 1474568 | tf_op jit(solution)/shard_map/ppermute | solution.py:26
  133.8 28.7 %collective-permute-start.28 = (bf16[128,1920]{1,0:T(8,128)(2,1)}, bf16[128,1920]{1,0:T(8,128)(2,1)S(1)}, u32[]{:S(2)}, u32[]{:S(2)}) collective-permute-start(bf16[128,1920]{1,0:T(8,128)(2,1)} %get-tuple-element.196), channel_id=1, source_target_pairs={{0,1},{1,2},{2,3},{3,0},{4,5},{5,6},{6,7},{7,4},{8,9},{9,10},{10,1... | collective-permute-start | bytes 1474568 | tf_op jit(solution)/shard_map/ppermute | solution.py:26
  134.3 29.5 %all-to-all-start.2 = ((bf16[8,16,1920]{2,1,0:T(8,128)(2,1)}), bf16[8,16,1920]{2,1,0:T(8,128)(2,1)S(1)}, u32[]{:S(2)}, u32[]{:S(2)}) async-start(bf16[8,16,1920]{2,1,0:T(8,128)(2,1)} %bitcast.44), calls=%async_computation.2 | async-start | bytes 983040 | tf_op jit(solution)/shard_map/all_to_all | solution.py:46
  163.8 13.9 %all-to-all-start.3 = ((bf16[8,16,1920]{2,1,0:T(8,128)(2,1)}), bf16[8,16,1920]{2,1,0:T(8,128)(2,1)S(1)}, u32[]{:S(2)}, u32[]{:S(2)}) async-start(bf16[8,16,1920]{2,1,0:T(8,128)(2,1)} %bitcast.16), calls=%async_computation.3 | async-start | bytes 983040 | tf_op jit(solution)/shard_map/all_to_all | solution.py:46
  (9 other events, 50.1 us)

commit v4 on v3

--- a/solution.py
+++ b/solution.py
@@ -11,6 +11,7 @@
 CONTRACT_FIRST = (((0,), (0,)), ((), ()))
 CHUNKS = 2
 LANES = 128
+PARTIAL_FLOPS = 20000000000
 TOTAL_FLOPS = 20_000_000_000
 VMEM_LIMIT = 20 * 1024 * 1024
 BF16 = jnp.bfloat16
@@ -130,7 +131,7 @@
     keep.wait()
 
 
-def partial(pieces, weights, all_rows, base, total_rows, held):
+def partial(pieces, weights, all_rows, base, total_rows, held, flops=1):
     count = sum(p.shape[0] for p in pieces)
     width, units = weights[0].shape
     n = len(pieces)
@@ -152,6 +153,7 @@
         tuple(range(n)),
         in_hbm,
         (2,),
+        flops,
     )
 
 
@@ -386,7 +388,13 @@
     top_in0, bottom_in0 = swap(top0, 1), swap(bottom0, 0)
     far_top1, far_bottom1, top0, bottom0 = fence(far_top1, far_bottom1, top0, bottom0)
     top1, bottom1, all_rows = partial(
-        (before1, far_top1, after1, far_bottom1), held, all_rows, base1, total_rows, True
+        (before1, far_top1, after1, far_bottom1),
+        held,
+        all_rows,
+        base1,
+        total_rows,
+        True,
+        PARTIAL_FLOPS,
     )
     top_in1, bottom_in1 = swap(top1, 0), swap(bottom1, 1)
     top_in0, bottom_in0, all_rows = fence(top_in0, bottom_in0, all_rows)

time: 181 us -> 175 us (0.967)
  starting transfers between devices: 68.2 us -> 58.2 us
  waiting for transfers between devices: 53.1 us -> 57.1 us
    all_to_all x4, starting transfers between devices: 32.2 us -> 22.9 us  [to_experts(): return lax.all_to_all(rows, 'gx', split_axis=0, concat_axis=0, tiled=True)]
    ppermute x16, waiting for transfers between devices: 16.5 us -> 24.3 us  [swap(): return lax.ppermute(array, 'gy', pairs)]
    ppermute x14, waiting for transfers between devices: 22.5 us -> 18.6 us  [shift(): lax.ppermute(array, 'gz', [(i, (i + steps) % size) for i in range(size)])]
    ppermute x14, starting transfers between devices: 19.5 us -> 17.2 us  [shift(): lax.ppermute(array, 'gz', [(i, (i + steps) % size) for i in range(size)])]
  transfers between devices with their start and end apart: 34 -> 34, of which waited for: 19 -> 21; matrix products, arithmetic and copies ran while one was open for 10% -> 11% of each run, Pallas kernels for 14% -> 15%
where the time goes in v4:
time: 175 us; the launch traced here: 174 us
  starting transfers between devices  58.2 us (33%)
  waiting for transfers between devices  57.1 us (33%)
  Pallas kernels  32.3 us (18%)
  matrix products  18.7 us (11%)
  other arithmetic  3.72 us (2%)
  local copies, waits for them, and re-layouts  3.3 us (2%)
    pallas_call x14, Pallas kernels, call(): pl.pallas_call(kernel, out_shape=[pltpu.HBM(*o) if i in out_hbm else jax....  29.7 us
    ppermute x16, waiting for transfers between devices, swap(): return lax.ppermute(array, 'gy', pairs)  24.3 us
    all_to_all x4, starting transfers between devices, to_experts(): return lax.all_to_all(rows, 'gx', split_axis=0, concat_axis=0, tiled=True)  22.9 us
    dot_general x7, matrix products, dot(): return lax.dot_general(left, right, dims, preferred_element_type=F32)  18.7 us
    ppermute x14, waiting for transfers between devices, shift(): lax.ppermute(array, 'gz', [(i, (i + steps) % size) for i in range(size)])  18.6 us
    ppermute x16, starting transfers between devices, swap(): return lax.ppermute(array, 'gy', pairs)  18.1 us
    ppermute x14, starting transfers between devices, shift(): lax.ppermute(array, 'gz', [(i, (i + steps) % size) for i in range(size)])  17.2 us
    all_to_all x4, waiting for transfers between devices, to_experts(): return lax.all_to_all(rows, 'gx', split_axis=0, concat_axis=0, tiled=True)  14.1 us
  transfers between devices with their start and end apart: 34, of which 21 were waited for; matrix products, arithmetic and copies ran while one was open for 11% of the time, Pallas kernels for 15%

profile of v4, /device:TPU:1, one launch (start us, length us, event | category | flops | bytes accessed | tf_op | source)
XLA Modules:
  0.0 174.2 jit_solution(6722539581331852903)
XLA Ops:
  5.3 5.8 %all-to-all-start = ((bf16[8,16,3584]{2,1,0:T(8,128)(2,1)}), bf16[8,16,3584]{2,1,0:T(8,128)(2,1)S(1)}, u32[]{:S(2)}, u32[]{:S(2)}) async-start(bf16[8,16,3584]{2,1,0:T(8,128)(2,1)} %bitcast.55), calls=%async_computation | async-start | bytes 1835008 | tf_op jit(solution)/shard_map/all_to_all | solution.py:47
  14.0 10.8 %all-to-all-done = bf16[8,16,3584]{2,1,0:T(8,128)(2,1)S(1)} async-done(((bf16[8,16,3584]{2,1,0:T(8,128)(2,1)}), bf16[8,16,3584]{2,1,0:T(8,128)(2,1)S(1)}, u32[]{:S(2)}, u32[]{:S(2)}) %all-to-all-start) | async-done | bytes 917536 | tf_op jit(solution)/shard_map/all_to_all | solution.py:47
  28.6 4.6 %all-to-all-start.1 = ((bf16[8,16,3584]{2,1,0:T(8,128)(2,1)}), bf16[8,16,3584]{2,1,0:T(8,128)(2,1)S(1)}, u32[]{:S(2)}, u32[]{:S(2)}) async-start(bf16[8,16,3584]{2,1,0:T(8,128)(2,1)} %bitcast.54), calls=%async_computation.1 | async-start | bytes 1835008 | tf_op jit(solution)/shard_map/all_to_all | solution.py:47
  33.2 3.9 %shard_map.119 = (bf16[64,1536]{1,0:T(8,128)(2,1)S(1)}, bf16[64,1536]{1,0:T(8,128)(2,1)S(1)}, bf16[1024,3584]{1,0:T(8,128)(2,1)}) custom-call(bf16[128,3584]{1,0:T(8,128)(2,1)S(1)} %bitcast.34, bf16[1792,512]{1,0:T(8,128)(2,1)} %bitcast.45, bf16[1792,512]{1,0:T(8,128)(2,1)} %bitcast.48, bf16[512,1792]{1,0:T(8,128)(2,1)} %bitcast.51), custom_call_target="tpu_custom_call" | custom-call | flops 1 | bytes 1 | tf_op jit(solution)/shard_map/pallas_call | solution.py:52
  40.4 3.2 %collective-permute-done.top_in = bf16[64,1536]{1,0:T(8,128)(2,1)S(1)} collective-permute-done((bf16[64,1536]{1,0:T(8,128)(2,1)S(1)}, bf16[64,1536]{1,0:T(8,128)(2,1)S(1)}, u32[]{:S(2)}, u32[]{:S(2)}) %collective-permute-start) | collective-permute-done | bytes 196640 | tf_op jit(solution)/shard_map/ppermute | solution.py:35
  43.7 2.2 %collective-permute-done.1.bottom_in = bf16[64,1536]{1,0:T(8,128)(2,1)S(1)} collective-permute-done((bf16[64,1536]{1,0:T(8,128)(2,1)S(1)}, bf16[64,1536]{1,0:T(8,128)(2,1)S(1)}, u32[]{:S(2)}, u32[]{:S(2)}) %collective-permute-start.1) | collective-permute-done | bytes 196640 | tf_op jit(solution)/shard_map/ppermute | solution.py:35
  47.9 3.9 %shard_map.121 = (bf16[64,1536]{1,0:T(8,128)(2,1)S(1)}, bf16[64,1536]{1,0:T(8,128)(2,1)S(1)}, bf16[1024,3584]{1,0:T(8,128)(2,1)}) custom-call(bf16[128,3584]{1,0:T(8,128)(2,1)S(1)} %bitcast.35, bf16[1792,512]{1,0:T(8,128)(2,1)} %bitcast.46, bf16[1792,512]{1,0:T(8,128)(2,1)} %bitcast.49, bf16[512,1792]{1,0:T(8,128)(2,1)} %bitcast.52, ...), custom_call_target="tpu_custom_call", output_to_operand_aliasing={{2}: (4, {})} | custom-call | flops 1 | bytes 1 | tf_op jit(solution)/shard_map/pallas_call | solution.py:52
  54.1 2.7 %collective-permute-start.7 = (bf16[64,3584]{1,0:T(8,128)(2,1)S(1)}, bf16[64,3584]{1,0:T(8,128)(2,1)S(1)}, u32[]{:S(2)}, u32[]{:S(2)}) collective-permute-start(bf16[64,3584]{1,0:T(8,128)(2,1)S(1)} %slice.42), channel_id=1, source_target_pairs={{0,3},{1,0},{2,1},{3,2},{4,7},{5,4},{6,5},{7,6},{8,11},{9,8},{10,9... | collective-permute-start | bytes 1376264 | tf_op jit(solution)/shard_map/ppermute | solution.py:27
  58.3 2.6 %shard_map.122 = (bf16[1792,512]{1,0:T(8,128)(2,1)S(1)}, bf16[1792,512]{1,0:T(8,128)(2,1)S(1)}, bf16[512,1792]{1,0:T(8,128)(2,1)S(1)}) custom-call(bf16[1792,512]{1,0:T(8,128)(2,1)} %bitcast.47, bf16[1792,512]{1,0:T(8,128)(2,1)} %bitcast.50, bf16[512,1792]{1,0:T(8,128)(2,1)} %bitcast.53), custom_call_target="tpu_custom_call" | custom-call | tf_op jit(solution)/shard_map/pallas_call | solution.py:82
  65.0 2.7 %collective-permute-start.13 = (bf16[128,3584]{1,0:T(8,128)(2,1)S(1)}, bf16[128,3584]{1,0:T(8,128)(2,1)S(1)}, u32[]{:S(2)}, u32[]{:S(2)}) collective-permute-start(bf16[128,3584]{1,0:T(8,128)(2,1)S(1)} %bitcast.37), channel_id=1, source_target_pairs={{0,3},{1,0},{2,1},{3,2},{4,7},{5,4},{6,5},{7,6},{8,11},{9,8},{10,9... | collective-permute-start | bytes 2752520 | tf_op jit(solution)/shard_map/ppermute | solution.py:27
  69.4 4.0 %shard_map.124 = (bf16[192,1536]{1,0:T(8,128)(2,1)S(1)}, bf16[192,1536]{1,0:T(8,128)(2,1)S(1)}, bf16[1024,3584]{1,0:T(8,128)(2,1)}) custom-call(bf16[128,3584]{1,0:T(8,128)(2,1)S(1)} %collective-permute-done.4.refs_0_, bf16[64,3584]{1,0:T(8,128)(2,1)S(1)} %collective-permute-done.6.refs_1_, ...), custom_call_target="tpu_custom_call", output_to_operand_aliasing={{2}: (7, {})} | custom-call | flops 1 | bytes 1 | tf_op jit(solution)/shard_map/pallas_call | solution.py:52
  75.9 3.1 %shard_map.125 = (bf16[128,1920]{1,0:T(8,128)(2,1)S(1)}, bf16[128,1920]{1,0:T(8,128)(2,1)S(1)}, bf16[1024,512]{1,0:T(8,128)(2,1)}, bf16[1024,1024]{1,0:T(8,128)(2,1)}) custom-call(bf16[64,1536]{1,0:T(8,128)(2,1)S(1)} %get-tuple-element.119.refs_0_, bf16[64,1536]{1,0:T(8,128)(2,1)} %collective-permute-done.2.refs_1_, ...), custom_call_target="tpu_custom_call" | custom-call | flops 1 | bytes 1 | tf_op jit(solution)/shard_map/pallas_call | solution.py:52
  79.0 5.7 %collective-permute-done.12.refs_0_ = bf16[128,3584]{1,0:T(8,128)(2,1)S(1)} collective-permute-done((bf16[128,3584]{1,0:T(8,128)(2,1)S(1)}, bf16[128,3584]{1,0:T(8,128)(2,1)S(1)}, u32[]{:S(2)}, u32[]{:S(2)}) %collective-permute-start.12) | collective-permute-done | bytes 917536 | tf_op jit(solution)/shard_map/ppermute | solution.py:27
  85.3 2.4 %collective-permute-start.15 = (bf16[64,3584]{1,0:T(8,128)(2,1)S(1)}, bf16[64,3584]{1,0:T(8,128)(2,1)S(1)}, u32[]{:S(2)}, u32[]{:S(2)}) collective-permute-start(bf16[64,3584]{1,0:T(8,128)(2,1)S(1)} %slice.44), channel_id=1, source_target_pairs={{0,3},{1,0},{2,1},{3,2},{4,7},{5,4},{6,5},{7,6},{8,11},{9,8},{10,9... | collective-permute-start | bytes 1376264 | tf_op jit(solution)/shard_map/ppermute | solution.py:27
  88.0 2.1 %collective-permute-start.20 = (bf16[192,1536]{1,0:T(8,128)(2,1)S(1)}, bf16[192,1536]{1,0:T(8,128)(2,1)S(1)}, u32[]{:S(2)}, u32[]{:S(2)}) collective-permute-start(bf16[192,1536]{1,0:T(8,128)(2,1)S(1)} %get-tuple-element.170.refs_0_), channel_id=1, source_target_pairs={{4,8},{8,4},{12,0},{0,12},{5,9},{9,5},{13,1},{1,13},{6,10},{10,6},... | collective-permute-start | bytes 1769480 | tf_op jit(solution)/shard_map/ppermute | solution.py:35
  90.1 3.9 %collective-permute-done.14.refs_1_ = bf16[64,3584]{1,0:T(8,128)(2,1)S(1)} collective-permute-done((bf16[64,3584]{1,0:T(8,128)(2,1)S(1)}, bf16[64,3584]{1,0:T(8,128)(2,1)S(1)}, u32[]{:S(2)}, u32[]{:S(2)}) %collective-permute-start.14) | collective-permute-done | bytes 458784 | tf_op jit(solution)/shard_map/ppermute | solution.py:27
  94.0 3.3 %shard_map.127 = (bf16[192,1536]{1,0:T(8,128)(2,1)S(1)}, bf16[192,1536]{1,0:T(8,128)(2,1)S(1)}, bf16[1024,3584]{1,0:T(8,128)(2,1)}) custom-call(bf16[128,3584]{1,0:T(8,128)(2,1)S(1)} %collective-permute-done.12.refs_0_, bf16[64,3584]{1,0:T(8,128)(2,1)S(1)} %collective-permute-done.14.refs_1_, ...), custom_call_target="tpu_custom_call", output_to_operand_aliasing={{2}: (7, {})} | custom-call | flops 20000000000 | bytes 1 | tf_op jit(solution)/shard_map/pallas_call | solution.py:52
  100.2 2.8 %shard_map.128 = (bf16[128,1920]{1,0:T(8,128)(2,1)S(1)}, bf16[128,1920]{1,0:T(8,128)(2,1)S(1)}, bf16[128,1920]{1,0:T(8,128)(2,1)S(1)}, bf16[1024,512]{1,0:T(8,128)(2,1)}, bf16[1024,1024]{1,0:T(8,128)(2,1)}) custom-call(bf16[192,1536]{1,0:T(8,128)(2,1)S(1)} %get-tuple-element.170.refs_0_, ...), custom_call_target="tpu_custom_call", output_to_operand_aliasing={{3}: (6, {}), {4}: (7, {})} | custom-call | flops 1 | bytes 1 | tf_op jit(solution)/shard_map/pallas_call | solution.py:52
  103.0 2.2 %collective-permute-start.24 = (bf16[128,1920]{1,0:T(8,128)(2,1)S(1)}, bf16[128,1920]{1,0:T(8,128)(2,1)S(1)}, u32[]{:S(2)}, u32[]{:S(2)}) collective-permute-start(bf16[128,1920]{1,0:T(8,128)(2,1)S(1)} %get-tuple-element.182), channel_id=1, source_target_pairs={{0,3},{1,0},{2,1},{3,2},{4,7},{5,4},{6,5},{7,6},{8,11},{9,8},{10,9... | collective-permute-start | bytes 1474568 | tf_op jit(solution)/shard_map/ppermute | solution.py:27
  106.4 6.6 %collective-permute-done.18.top_in = bf16[192,1536]{1,0:T(8,128)(2,1)S(1)} collective-permute-done((bf16[192,1536]{1,0:T(8,128)(2,1)S(1)}, bf16[192,1536]{1,0:T(8,128)(2,1)S(1)}, u32[]{:S(2)}, u32[]{:S(2)}) %collective-permute-start.18) | collective-permute-done | bytes 589856 | tf_op jit(solution)/shard_map/ppermute | solution.py:35
  113.6 3.2 %collective-permute-start.22 = (bf16[192,1536]{1,0:T(8,128)(2,1)S(1)}, bf16[192,1536]{1,0:T(8,128)(2,1)S(1)}, u32[]{:S(2)}, u32[]{:S(2)}) collective-permute-start(bf16[192,1536]{1,0:T(8,128)(2,1)S(1)} %get-tuple-element.189.refs_0_), channel_id=1, source_target_pairs={{4,8},{8,4},{12,0},{0,12},{5,9},{9,5},{13,1},{1,13},{6,10},{10,6},... | collective-permute-start | bytes 1769480 | tf_op jit(solution)/shard_map/ppermute | solution.py:35
  117.0 3.3 %collective-permute-done.25.second = bf16[128,1920]{1,0:T(8,128)(2,1)S(1)} collective-permute-done((bf16[128,1920]{1,0:T(8,128)(2,1)S(1)}, bf16[128,1920]{1,0:T(8,128)(2,1)S(1)}, u32[]{:S(2)}, u32[]{:S(2)}) %collective-permute-start.25) | collective-permute-done | bytes 491552 | tf_op jit(solution)/shard_map/ppermute | solution.py:27
  120.7 5.5 %collective-permute-done.22.refs_1_ = bf16[192,1536]{1,0:T(8,128)(2,1)S(1)} collective-permute-done((bf16[192,1536]{1,0:T(8,128)(2,1)S(1)}, bf16[192,1536]{1,0:T(8,128)(2,1)S(1)}, u32[]{:S(2)}, u32[]{:S(2)}) %collective-permute-start.22) | collective-permute-done | bytes 589856 | tf_op jit(solution)/shard_map/ppermute | solution.py:35
  128.2 3.8 %shard_map.131 = (bf16[128,1920]{1,0:T(8,128)(2,1)}, bf16[128,1920]{1,0:T(8,128)(2,1)}, bf16[128,1920]{1,0:T(8,128)(2,1)}, bf16[1024,512]{1,0:T(8,128)(2,1)}, bf16[1024,1024]{1,0:T(8,128)(2,1)}) custom-call(bf16[192,1536]{1,0:T(8,128)(2,1)S(1)} %get-tuple-element.189.refs_0_, ...), custom_call_target="tpu_custom_call", output_to_operand_aliasing={{3}: (6, {}), {4}: (7, {})} | custom-call | flops 1 | bytes 1 | tf_op jit(solution)/shard_map/pallas_call | solution.py:52
  133.6 8.6 %all-to-all-start.2 = ((bf16[8,16,1920]{2,1,0:T(8,128)(2,1)}), bf16[8,16,1920]{2,1,0:T(8,128)(2,1)S(1)}, u32[]{:S(2)}, u32[]{:S(2)}) async-start(bf16[8,16,1920]{2,1,0:T(8,128)(2,1)} %bitcast.44), calls=%async_computation.2 | async-start | bytes 983040 | tf_op jit(solution)/shard_map/all_to_all | solution.py:47
  142.2 5.8 %fusion.9 = bf16[1792,512]{1,0:T(8,128)(2,1)} fusion(bf16[1024,3584]{1,0:T(8,128)(2,1)} %get-tuple-element.204, bf16[1024,1024]{1,0:T(8,128)(2,1)} %get-tuple-element.205), kind=kOutput, calls=%fused_computation.7 | convolution fusion | flops 1879965696 | bytes 6553600 | tf_op jit(solution)/shard_map/dot_general | solution.py:22
  148.0 5.4 %fusion.6 = bf16[1792,512]{1,0:T(8,128)(2,1)} fusion(bf16[1024,3584]{1,0:T(8,128)(2,1)} %get-tuple-element.204, bf16[1024,1024]{1,0:T(8,128)(2,1)S(1)} %copy-done.3), kind=kOutput, calls=%fused_computation.6 | convolution fusion | flops 1879965696 | bytes 6553600 | tf_op jit(solution)/shard_map/dot_general | solution.py:22
  153.4 4.0 %collective-permute-done.28.second = bf16[128,1920]{1,0:T(8,128)(2,1)S(1)} collective-permute-done((bf16[128,1920]{1,0:T(8,128)(2,1)}, bf16[128,1920]{1,0:T(8,128)(2,1)S(1)}, u32[]{:S(2)}, u32[]{:S(2)}) %collective-permute-start.28) | collective-permute-done | bytes 491552 | tf_op jit(solution)/shard_map/ppermute | solution.py:27
  158.7 3.9 %all-to-all-start.3 = ((bf16[8,16,1920]{2,1,0:T(8,128)(2,1)}), bf16[8,16,1920]{2,1,0:T(8,128)(2,1)S(1)}, u32[]{:S(2)}, u32[]{:S(2)}) async-start(bf16[8,16,1920]{2,1,0:T(8,128)(2,1)} %bitcast.16), calls=%async_computation.3 | async-start | bytes 983040 | tf_op jit(solution)/shard_map/all_to_all | solution.py:47
  162.6 5.8 %fusion.12 = bf16[512,1792]{1,0:T(8,128)(2,1)} fusion(bf16[1024,512]{1,0:T(8,128)(2,1)} %get-tuple-element.212, bf16[1024,3584]{1,0:T(8,128)(2,1)} %get-tuple-element.204), kind=kOutput, calls=%fused_computation.8 | convolution fusion | flops 1879965696 | bytes 6553600 | tf_op jit(solution)/shard_map/dot_general | solution.py:22
  168.4 3.3 %all-to-all-done.3 = bf16[8,16,1920]{2,1,0:T(8,128)(2,1)S(1)} async-done(((bf16[8,16,1920]{2,1,0:T(8,128)(2,1)}), bf16[8,16,1920]{2,1,0:T(8,128)(2,1)S(1)}, u32[]{:S(2)}, u32[]{:S(2)}) %all-to-all-start.3) | async-done | bytes 491552 | tf_op jit(solution)/shard_map/all_to_all | solution.py:47
  171.8 2.4 %shard_map.133 = (bf16[512,1792]{1,0:T(8,128)(2,1)}, f32[8,32]{1,0:T(8,128)}) custom-call(s32[8,32]{1,0:T(8,128)S(1)} %get-tuple-element.226.usable, f32[8,32]{1,0:T(8,128)S(1)} %bitcast_convert_fusion.score, bf16[128,512]{1,0:T(8,128)(2,1)S(1)} %bitcast.41, bf16[128,512]{1,0:T(8,128)(2,1)S(1)} %bitcast.43, bf16[128,1920]{1,0:T(8,128)(2,1)S(1)} %bitcast.38, ...), custom_call_target="tpu_custom_call" | custom-call | flops 1 | bytes 1 | tf_op jit(solution)/shard_map/pallas_call | solution.py:52
  (82 shorter events, 39.7 us)
Async XLA Ops:
  5.3 19.5 %all-to-all-start = ((bf16[8,16,3584]{2,1,0:T(8,128)(2,1)}), bf16[8,16,3584]{2,1,0:T(8,128)(2,1)S(1)}, u32[]{:S(2)}, u32[]{:S(2)}) async-start(bf16[8,16,3584]{2,1,0:T(8,128)(2,1)} %bitcast.55), calls=%async_computation | async-start | bytes 1835008 | tf_op jit(solution)/shard_map/all_to_all | solution.py:47
  24.8 28.2 %collective-permute-start.4 = (bf16[128,3584]{1,0:T(8,128)(2,1)S(1)}, bf16[128,3584]{1,0:T(8,128)(2,1)S(1)}, u32[]{:S(2)}, u32[]{:S(2)}) collective-permute-start(bf16[128,3584]{1,0:T(8,128)(2,1)S(1)} %bitcast.32), channel_id=1, source_target_pairs={{0,1},{1,2},{2,3},{3,0},{4,5},{5,6},{6,7},{7,4},{8,9},{9,10},{10,1... | collective-permute-start | bytes 2752520 | tf_op jit(solution)/shard_map/ppermute | solution.py:27
  26.5 26.5 %collective-permute-start.5 = (bf16[128,3584]{1,0:T(8,128)(2,1)S(1)}, bf16[128,3584]{1,0:T(8,128)(2,1)}, u32[]{:S(2)}, u32[]{:S(2)}) collective-permute-start(bf16[128,3584]{1,0:T(8,128)(2,1)S(1)} %bitcast.33), channel_id=1, source_target_pairs={{0,3},{1,0},{2,1},{3,2},{4,7},{5,4},{6,5},{7,6},{8,11},{9,8},{10,9... | collective-permute-start | bytes 2752520 | tf_op jit(solution)/shard_map/ppermute | solution.py:27
  28.6 19.4 %all-to-all-start.1 = ((bf16[8,16,3584]{2,1,0:T(8,128)(2,1)}), bf16[8,16,3584]{2,1,0:T(8,128)(2,1)S(1)}, u32[]{:S(2)}, u32[]{:S(2)}) async-start(bf16[8,16,3584]{2,1,0:T(8,128)(2,1)} %bitcast.54), calls=%async_computation.1 | async-start | bytes 1835008 | tf_op jit(solution)/shard_map/all_to_all | solution.py:47
  37.1 6.6 %collective-permute-start = (bf16[64,1536]{1,0:T(8,128)(2,1)S(1)}, bf16[64,1536]{1,0:T(8,128)(2,1)S(1)}, u32[]{:S(2)}, u32[]{:S(2)}) collective-permute-start(bf16[64,1536]{1,0:T(8,128)(2,1)S(1)} %get-tuple-element.116.top), channel_id=1, source_target_pairs={{0,4},{4,0},{8,12},{12,8},{1,5},{5,1},{9,13},{13,9},{2,6},{6,2},{1... | collective-permute-start | bytes 589832 | tf_op jit(solution)/shard_map/ppermute | solution.py:35
  38.5 7.3 %collective-permute-start.1 = (bf16[64,1536]{1,0:T(8,128)(2,1)S(1)}, bf16[64,1536]{1,0:T(8,128)(2,1)S(1)}, u32[]{:S(2)}, u32[]{:S(2)}) collective-permute-start(bf16[64,1536]{1,0:T(8,128)(2,1)S(1)} %get-tuple-element.117.bottom), channel_id=1, source_target_pairs={{4,8},{8,4},{12,0},{0,12},{5,9},{9,5},{13,1},{1,13},{6,10},{10,6},... | collective-permute-start | bytes 589832 | tf_op jit(solution)/shard_map/ppermute | solution.py:35
  46.0 6.6 %collective-permute-start.2 = (bf16[64,1536]{1,0:T(8,128)(2,1)S(1)}, bf16[64,1536]{1,0:T(8,128)(2,1)}, u32[]{:S(2)}, u32[]{:S(2)}) collective-permute-start(bf16[64,1536]{1,0:T(8,128)(2,1)S(1)} %get-tuple-element.119.refs_0_), channel_id=1, source_target_pairs={{4,8},{8,4},{12,0},{0,12},{5,9},{9,5},{13,1},{1,13},{6,10},{10,6},... | collective-permute-start | bytes 589832 | tf_op jit(solution)/shard_map/ppermute | solution.py:35
  47.9 5.0 %collective-permute-start.3 = (bf16[64,1536]{1,0:T(8,128)(2,1)S(1)}, bf16[64,1536]{1,0:T(8,128)(2,1)}, u32[]{:S(2)}, u32[]{:S(2)}) collective-permute-start(bf16[64,1536]{1,0:T(8,128)(2,1)S(1)} %get-tuple-element.120.refs_2_), channel_id=1, source_target_pairs={{0,4},{4,0},{8,12},{12,8},{1,5},{5,1},{9,13},{13,9},{2,6},{6,2},{1... | collective-permute-start | bytes 589832 | tf_op jit(solution)/shard_map/ppermute | solution.py:35
  54.1 10.9 %collective-permute-start.6 = (bf16[64,3584]{1,0:T(8,128)(2,1)S(1)}, bf16[64,3584]{1,0:T(8,128)(2,1)S(1)}, u32[]{:S(2)}, u32[]{:S(2)}) collective-permute-start(bf16[64,3584]{1,0:T(8,128)(2,1)S(1)} %slice.41), channel_id=1, source_target_pairs={{0,1},{1,2},{2,3},{3,0},{4,5},{5,6},{6,7},{7,4},{8,9},{9,10},{10,1... | collective-permute-start | bytes 1376264 | tf_op jit(solution)/shard_map/ppermute | solution.py:27
  54.1 10.8 %collective-permute-start.7 = (bf16[64,3584]{1,0:T(8,128)(2,1)S(1)}, bf16[64,3584]{1,0:T(8,128)(2,1)S(1)}, u32[]{:S(2)}, u32[]{:S(2)}) collective-permute-start(bf16[64,3584]{1,0:T(8,128)(2,1)S(1)} %slice.42), channel_id=1, source_target_pairs={{0,3},{1,0},{2,1},{3,2},{4,7},{5,4},{6,5},{7,6},{8,11},{9,8},{10,9... | collective-permute-start | bytes 1376264 | tf_op jit(solution)/shard_map/ppermute | solution.py:27
  57.2 6.0 %collective-permute-start.9 = (bf16[64,1536]{1,0:T(8,128)(2,1)S(1)}, bf16[64,1536]{1,0:T(8,128)(2,1)S(1)}, u32[]{:S(2)}, u32[]{:S(2)}) collective-permute-start(bf16[64,1536]{1,0:T(8,128)(2,1)S(1)} %get-tuple-element.131.bottom), channel_id=1, source_target_pairs={{4,8},{8,4},{12,0},{0,12},{5,9},{9,5},{13,1},{1,13},{6,10},{10,6},... | collective-permute-start | bytes 589832 | tf_op jit(solution)/shard_map/ppermute | solution.py:35
  65.0 19.7 %collective-permute-start.12 = (bf16[128,3584]{1,0:T(8,128)(2,1)S(1)}, bf16[128,3584]{1,0:T(8,128)(2,1)S(1)}, u32[]{:S(2)}, u32[]{:S(2)}) collective-permute-start(bf16[128,3584]{1,0:T(8,128)(2,1)S(1)} %bitcast.36), channel_id=1, source_target_pairs={{0,1},{1,2},{2,3},{3,0},{4,5},{5,6},{6,7},{7,4},{8,9},{9,10},{10,1... | collective-permute-start | bytes 2752520 | tf_op jit(solution)/shard_map/ppermute | solution.py:27
  65.0 19.7 %collective-permute-start.13 = (bf16[128,3584]{1,0:T(8,128)(2,1)S(1)}, bf16[128,3584]{1,0:T(8,128)(2,1)S(1)}, u32[]{:S(2)}, u32[]{:S(2)}) collective-permute-start(bf16[128,3584]{1,0:T(8,128)(2,1)S(1)} %bitcast.37), channel_id=1, source_target_pairs={{0,3},{1,0},{2,1},{3,2},{4,7},{5,4},{6,5},{7,6},{8,11},{9,8},{10,9... | collective-permute-start | bytes 2752520 | tf_op jit(solution)/shard_map/ppermute | solution.py:27
  67.6 6.0 %collective-permute-start.10 = (bf16[64,1536]{1,0:T(8,128)(2,1)S(1)}, bf16[64,1536]{1,0:T(8,128)(2,1)S(1)}, u32[]{:S(2)}, u32[]{:S(2)}) collective-permute-start(bf16[64,1536]{1,0:T(8,128)(2,1)S(1)} %get-tuple-element.142.refs_4_), channel_id=1, source_target_pairs={{4,8},{8,4},{12,0},{0,12},{5,9},{9,5},{13,1},{1,13},{6,10},{10,6},... | collective-permute-start | bytes 589832 | tf_op jit(solution)/shard_map/ppermute | solution.py:35
  74.2 13.5 %collective-permute-start.16 = (bf16[192,1536]{1,0:T(8,128)(2,1)S(1)}, bf16[192,1536]{1,0:T(8,128)(2,1)S(1)}, u32[]{:S(2)}, u32[]{:S(2)}) collective-permute-start(bf16[192,1536]{1,0:T(8,128)(2,1)S(1)} %get-tuple-element.159.top), channel_id=1, source_target_pairs={{0,4},{4,0},{8,12},{12,8},{1,5},{5,1},{9,13},{13,9},{2,6},{6,2},{1... | collective-permute-start | bytes 1769480 | tf_op jit(solution)/shard_map/ppermute | solution.py:35
  75.0 12.7 %collective-permute-start.17 = (bf16[192,1536]{1,0:T(8,128)(2,1)S(1)}, bf16[192,1536]{1,0:T(8,128)(2,1)S(1)}, u32[]{:S(2)}, u32[]{:S(2)}) collective-permute-start(bf16[192,1536]{1,0:T(8,128)(2,1)S(1)} %get-tuple-element.160.bottom), channel_id=1, source_target_pairs={{4,8},{8,4},{12,0},{0,12},{5,9},{9,5},{13,1},{1,13},{6,10},{10,6},... | collective-permute-start | bytes 1769480 | tf_op jit(solution)/shard_map/ppermute | solution.py:35
  84.8 9.2 %collective-permute-start.14 = (bf16[64,3584]{1,0:T(8,128)(2,1)S(1)}, bf16[64,3584]{1,0:T(8,128)(2,1)S(1)}, u32[]{:S(2)}, u32[]{:S(2)}) collective-permute-start(bf16[64,3584]{1,0:T(8,128)(2,1)S(1)} %slice.43), channel_id=1, source_target_pairs={{0,1},{1,2},{2,3},{3,0},{4,5},{5,6},{6,7},{7,4},{8,9},{9,10},{10,1... | collective-permute-start | bytes 1376264 | tf_op jit(solution)/shard_map/ppermute | solution.py:27
  85.3 8.7 %collective-permute-start.15 = (bf16[64,3584]{1,0:T(8,128)(2,1)S(1)}, bf16[64,3584]{1,0:T(8,128)(2,1)S(1)}, u32[]{:S(2)}, u32[]{:S(2)}) collective-permute-start(bf16[64,3584]{1,0:T(8,128)(2,1)S(1)} %slice.44), channel_id=1, source_target_pairs={{0,3},{1,0},{2,1},{3,2},{4,7},{5,4},{6,5},{7,6},{8,11},{9,8},{10,9... | collective-permute-start | bytes 1376264 | tf_op jit(solution)/shard_map/ppermute | solution.py:27
  88.0 11.9 %collective-permute-start.20 = (bf16[192,1536]{1,0:T(8,128)(2,1)S(1)}, bf16[192,1536]{1,0:T(8,128)(2,1)S(1)}, u32[]{:S(2)}, u32[]{:S(2)}) collective-permute-start(bf16[192,1536]{1,0:T(8,128)(2,1)S(1)} %get-tuple-element.170.refs_0_), channel_id=1, source_target_pairs={{4,8},{8,4},{12,0},{0,12},{5,9},{9,5},{13,1},{1,13},{6,10},{10,6},... | collective-permute-start | bytes 1769480 | tf_op jit(solution)/shard_map/ppermute | solution.py:35
  90.1 10.0 %collective-permute-start.21 = (bf16[192,1536]{1,0:T(8,128)(2,1)S(1)}, bf16[192,1536]{1,0:T(8,128)(2,1)S(1)}, u32[]{:S(2)}, u32[]{:S(2)}) collective-permute-start(bf16[192,1536]{1,0:T(8,128)(2,1)S(1)} %get-tuple-element.173.refs_2_), channel_id=1, source_target_pairs={{0,4},{4,0},{8,12},{12,8},{1,5},{5,1},{9,13},{13,9},{2,6},{6,2},{1... | collective-permute-start | bytes 1769480 | tf_op jit(solution)/shard_map/ppermute | solution.py:35
  97.4 15.6 %collective-permute-start.18 = (bf16[192,1536]{1,0:T(8,128)(2,1)S(1)}, bf16[192,1536]{1,0:T(8,128)(2,1)S(1)}, u32[]{:S(2)}, u32[]{:S(2)}) collective-permute-start(bf16[192,1536]{1,0:T(8,128)(2,1)S(1)} %get-tuple-element.168.top), channel_id=1, source_target_pairs={{0,4},{4,0},{8,12},{12,8},{1,5},{5,1},{9,13},{13,9},{2,6},{6,2},{1... | collective-permute-start | bytes 1769480 | tf_op jit(solution)/shard_map/ppermute | solution.py:35
  99.1 14.3 %collective-permute-start.19 = (bf16[192,1536]{1,0:T(8,128)(2,1)S(1)}, bf16[192,1536]{1,0:T(8,128)(2,1)S(1)}, u32[]{:S(2)}, u32[]{:S(2)}) collective-permute-start(bf16[192,1536]{1,0:T(8,128)(2,1)S(1)} %get-tuple-element.169.bottom), channel_id=1, source_target_pairs={{4,8},{8,4},{12,0},{0,12},{5,9},{9,5},{13,1},{1,13},{6,10},{10,6},... | collective-permute-start | bytes 1769480 | tf_op jit(solution)/shard_map/ppermute | solution.py:35
  103.0 14.0 %collective-permute-start.24 = (bf16[128,1920]{1,0:T(8,128)(2,1)S(1)}, bf16[128,1920]{1,0:T(8,128)(2,1)S(1)}, u32[]{:S(2)}, u32[]{:S(2)}) collective-permute-start(bf16[128,1920]{1,0:T(8,128)(2,1)S(1)} %get-tuple-element.182), channel_id=1, source_target_pairs={{0,3},{1,0},{2,1},{3,2},{4,7},{5,4},{6,5},{7,6},{8,11},{9,8},{10,9... | collective-permute-start | bytes 1474568 | tf_op jit(solution)/shard_map/ppermute | solution.py:27
  105.1 15.1 %collective-permute-start.25 = (bf16[128,1920]{1,0:T(8,128)(2,1)S(1)}, bf16[128,1920]{1,0:T(8,128)(2,1)S(1)}, u32[]{:S(2)}, u32[]{:S(2)}) collective-permute-start(bf16[128,1920]{1,0:T(8,128)(2,1)S(1)} %get-tuple-element.183), channel_id=1, source_target_pairs={{0,1},{1,2},{2,3},{3,0},{4,5},{5,6},{6,7},{7,4},{8,9},{9,10},{10,1... | collective-permute-start | bytes 1474568 | tf_op jit(solution)/shard_map/ppermute | solution.py:27
  105.1 15.1 %collective-permute-start.26 = (bf16[128,1920]{1,0:T(8,128)(2,1)S(1)}, bf16[128,1920]{1,0:T(8,128)(2,1)S(1)}, u32[]{:S(2)}, u32[]{:S(2)}) collective-permute-start(bf16[128,1920]{1,0:T(8,128)(2,1)S(1)} %get-tuple-element.177), channel_id=1, source_target_pairs={{0,2},{1,3},{2,0},{3,1},{4,6},{5,7},{6,4},{7,5},{8,10},{9,11},{10,... | collective-permute-start | bytes 1474568 | tf_op jit(solution)/shard_map/ppermute | solution.py:27
  113.6 12.6 %collective-permute-start.22 = (bf16[192,1536]{1,0:T(8,128)(2,1)S(1)}, bf16[192,1536]{1,0:T(8,128)(2,1)S(1)}, u32[]{:S(2)}, u32[]{:S(2)}) collective-permute-start(bf16[192,1536]{1,0:T(8,128)(2,1)S(1)} %get-tuple-element.189.refs_0_), channel_id=1, source_target_pairs={{4,8},{8,4},{12,0},{0,12},{5,9},{9,5},{13,1},{1,13},{6,10},{10,6},... | collective-permute-start | bytes 1769480 | tf_op jit(solution)/shard_map/ppermute | solution.py:35
  116.8 11.3 %collective-permute-start.23 = (bf16[192,1536]{1,0:T(8,128)(2,1)S(1)}, bf16[192,1536]{1,0:T(8,128)(2,1)S(1)}, u32[]{:S(2)}, u32[]{:S(2)}) collective-permute-start(bf16[192,1536]{1,0:T(8,128)(2,1)S(1)} %get-tuple-element.191.refs_2_), channel_id=1, source_target_pairs={{0,4},{4,0},{8,12},{12,8},{1,5},{5,1},{9,13},{13,9},{2,6},{6,2},{1... | collective-permute-start | bytes 1769480 | tf_op jit(solution)/shard_map/ppermute | solution.py:35
  132.0 21.5 %collective-permute-start.29 = (bf16[128,1920]{1,0:T(8,128)(2,1)}, bf16[128,1920]{1,0:T(8,128)(2,1)S(1)}, u32[]{:S(2)}, u32[]{:S(2)}) collective-permute-start(bf16[128,1920]{1,0:T(8,128)(2,1)} %get-tuple-element.199), channel_id=1, source_target_pairs={{0,2},{1,3},{2,0},{3,1},{4,6},{5,7},{6,4},{7,5},{8,10},{9,11},{10,... | collective-permute-start | bytes 1474568 | tf_op jit(solution)/shard_map/ppermute | solution.py:27
  132.1 21.4 %collective-permute-start.27 = (bf16[128,1920]{1,0:T(8,128)(2,1)}, bf16[128,1920]{1,0:T(8,128)(2,1)S(1)}, u32[]{:S(2)}, u32[]{:S(2)}) collective-permute-start(bf16[128,1920]{1,0:T(8,128)(2,1)} %get-tuple-element.195), channel_id=1, source_target_pairs={{0,3},{1,0},{2,1},{3,2},{4,7},{5,4},{6,5},{7,6},{8,11},{9,8},{10,9... | collective-permute-start | bytes 1474568 | tf_op jit(solution)/shard_map/ppermute | solution.py:27
  132.1 25.3 %collective-permute-start.28 = (bf16[128,1920]{1,0:T(8,128)(2,1)}, bf16[128,1920]{1,0:T(8,128)(2,1)S(1)}, u32[]{:S(2)}, u32[]{:S(2)}) collective-permute-start(bf16[128,1920]{1,0:T(8,128)(2,1)} %get-tuple-element.196), channel_id=1, source_target_pairs={{0,1},{1,2},{2,3},{3,0},{4,5},{5,6},{6,7},{7,4},{8,9},{9,10},{10,1... | collective-permute-start | bytes 1474568 | tf_op jit(solution)/shard_map/ppermute | solution.py:27
  133.6 25.1 %all-to-all-start.2 = ((bf16[8,16,1920]{2,1,0:T(8,128)(2,1)}), bf16[8,16,1920]{2,1,0:T(8,128)(2,1)S(1)}, u32[]{:S(2)}, u32[]{:S(2)}) async-start(bf16[8,16,1920]{2,1,0:T(8,128)(2,1)} %bitcast.44), calls=%async_computation.2 | async-start | bytes 983040 | tf_op jit(solution)/shard_map/all_to_all | solution.py:47
  158.7 13.0 %all-to-all-start.3 = ((bf16[8,16,1920]{2,1,0:T(8,128)(2,1)}), bf16[8,16,1920]{2,1,0:T(8,128)(2,1)S(1)}, u32[]{:S(2)}, u32[]{:S(2)}) async-start(bf16[8,16,1920]{2,1,0:T(8,128)(2,1)} %bitcast.16), calls=%async_computation.3 | async-start | bytes 983040 | tf_op jit(solution)/shard_map/all_to_all | solution.py:47
  (9 other events, 51.0 us)

commit v5 on v4

--- a/solution.py
+++ b/solution.py
@@ -11,6 +11,7 @@
 CONTRACT_FIRST = (((0,), (0,)), ((), ()))
 CHUNKS = 2
 LANES = 128
+OWN_FLOPS = 20_000_000_000
 PARTIAL_FLOPS = 20000000000
 TOTAL_FLOPS = 20_000_000_000
 VMEM_LIMIT = 20 * 1024 * 1024
@@ -88,6 +89,24 @@
         compiler_params=pltpu.CompilerParams(vmem_limit_bytes=VMEM_LIMIT),
     )(*arrays)
     return [pltpu.with_memory_space_constraint(a, pltpu.VMEM) for a in copies]
+
+
+def cut_kernel(before, after, top, bottom, sems):
+    half = top.shape[0]
+    copies = [
+        pltpu.make_async_copy(before.at[pl.ds(0, half)], top, sems.at[0]),
+        pltpu.make_async_copy(after.at[pl.ds(half, half)], bottom, sems.at[1]),
+    ]
+    for copy in copies:
+        copy.start()
+    for copy in copies:
+        copy.wait()
+
+
+def cut(before, after):
+    shape = (before.shape[0] // 2, before.shape[1])
+    sems = pltpu.SemaphoreType.DMA((2,))
+    return call(cut_kernel, [(shape, BF16)] * 2, [sems], [before, after], free=(0, 1))
 
 
 def partial_kernel(pieces, base, aliased, held, *refs):
@@ -162,12 +181,13 @@
     bottom_out[...] = add(bottom[...], bottom_in[...]).astype(BF16)
 
 
-def add_halves(top, top_in, bottom, bottom_in):
+def add_halves(top, top_in, bottom, bottom_in, flops=1):
     return call(
         add_kernel,
         [(top.shape, BF16), (bottom.shape, BF16)],
         [],
         [top, top_in, bottom, bottom_in],
+        flops=flops,
     )
 
 
@@ -346,24 +366,23 @@
     a_top_in, a_bottom_in = swap(a_top, 0), swap(a_bottom, 1)
     a_top, a_bottom = add_halves(a_top, a_top_in, a_bottom, a_bottom_in)
     a_top_in, a_bottom_in = swap(a_top, 1), swap(a_bottom, 0)
-    own1, all_rows, a_top = fence(own1, all_rows, a_top)
-    b_top, b_bottom, all_rows = partial((own1,), weights, all_rows, own_rows, total_rows, False)
+    before0, after0, all_rows, a_top, own1 = fence(before0, after0, all_rows, a_top, own1)
+    cut_top0, cut_bottom0 = cut(before0, after0)
+    far_top0, far_bottom0 = shift(cut_top0, 1), shift(cut_bottom0, -1)
+    own1, all_rows, cut_top0 = fence(own1, all_rows, cut_top0)
+    b_top, b_bottom, all_rows = partial(
+        (own1,), weights, all_rows, own_rows, total_rows, False, OWN_FLOPS
+    )
     a_top_in, a_bottom_in, b_top, b_bottom = fence(a_top_in, a_bottom_in, b_top, b_bottom)
     b_top_in, b_bottom_in = swap(b_top, 0), swap(b_bottom, 1)
-    before0, after0, b_top = fence(before0, after0, b_top)
-    cut_top0, cut_bottom0 = before0[:half], after0[half:]
-    far_top0, far_bottom0 = shift(cut_top0, 1), shift(cut_bottom0, -1)
-    cut_top0, cut_bottom0, *weights = fence(cut_top0, cut_bottom0, *weights)
+    b_top, *weights = fence(b_top, *weights)
     held = hold(weights)
-    b_top_in, b_bottom_in, cut_top0, cut_bottom0, *held = fence(
-        b_top_in, b_bottom_in, cut_top0, cut_bottom0, *held
-    )
-    b_top, b_bottom = add_halves(b_top, b_top_in, b_bottom, b_bottom_in)
+    far_top0, far_bottom0, own1, *held = fence(far_top0, far_bottom0, own1, *held)
+    before1, after1 = shift(own1, 1), shift(own1, -1)
+    b_top_in, b_bottom_in, far_top0 = fence(b_top_in, b_bottom_in, far_top0)
+    b_top, b_bottom = add_halves(b_top, b_top_in, b_bottom, b_bottom_in, OWN_FLOPS)
     b_top_in, b_bottom_in = swap(b_top, 1), swap(b_bottom, 0)
-    far_top0, far_bottom0, b_top, b_bottom, own1 = fence(
-        far_top0, far_bottom0, b_top, b_bottom, own1
-    )
-    before1, after1 = shift(own1, 1), shift(own1, -1)
+    far_top0, far_bottom0, b_top = fence(far_top0, far_bottom0, b_top)
     base0, base1 = CHUNKS * own_rows, (CHUNKS + 3) * own_rows
     top0, bottom0, all_rows = partial(
         (before0, far_top0, after0, far_bottom0), held, all_rows, base0, total_rows, True
@@ -379,7 +398,7 @@
     own_layout = (((0, 0, half), (1, 0, half)), ((2, 0, half), (3, 0, half)))
     own_part0, own_part1, *gathered = act(own_pairs, held, None, 0, own_layout, total_rows)
     before1, after1, own_part0 = fence(before1, after1, own_part0)
-    cut_top1, cut_bottom1 = before1[:half], after1[half:]
+    cut_top1, cut_bottom1 = cut(before1, after1)
     far_top1, far_bottom1 = shift(cut_top1, 1), shift(cut_bottom1, -1)
     top_in0, bottom_in0, cut_top1, cut_bottom1 = fence(
         top_in0, bottom_in0, cut_top1, cut_bottom1

time: 175 us -> 172 us (0.983)
  waiting for transfers between devices: 57.1 us -> 52.4 us
  starting transfers between devices: 58.2 us -> 61 us
    ppermute x16, waiting for transfers between devices: 24.3 us -> 19.3 us  [swap(): return lax.ppermute(array, 'gy', pairs)]
    all_to_all x4, starting transfers between devices: 22.9 us -> 24.8 us  [to_experts(): return lax.all_to_all(rows, 'gx', split_axis=0, concat_axis=0, tiled=True)]
    pallas_call x14 -> x16, Pallas kernels: 29.7 us -> 30.2 us  [call(): pl.pallas_call(kernel, out_shape=[pltpu.HBM(*o) if i in out_hbm else jax....]
  transfers between devices with their start and end apart: 34 -> 34, of which waited for: 21 -> 17; matrix products, arithmetic and copies ran while one was open for 11% -> 11% of each run, Pallas kernels for 15% -> 16%
where the time goes in v5:
time: 172 us
  starting transfers between devices  61 us (35%)
  waiting for transfers between devices  52.4 us (30%)
  Pallas kernels  32.9 us (19%)
  matrix products  18.7 us (11%)
  other arithmetic  3.72 us (2%)
  local copies, waits for them, and re-layouts  2.15 us (1%)
    pallas_call x16, Pallas kernels, call(): pl.pallas_call(kernel, out_shape=[pltpu.HBM(*o) if i in out_hbm else jax....  30.2 us
    all_to_all x4, starting transfers between devices, to_experts(): return lax.all_to_all(rows, 'gx', split_axis=0, concat_axis=0, tiled=True)  24.8 us
    ppermute x16, waiting for transfers between devices, swap(): return lax.ppermute(array, 'gy', pairs)  19.3 us
    ppermute x14, waiting for transfers between devices, shift(): lax.ppermute(array, 'gz', [(i, (i + steps) % size) for i in range(size)])  19 us
    dot_general x7, matrix products, dot(): return lax.dot_general(left, right, dims, preferred_element_type=F32)  18.7 us
    ppermute x16, starting transfers between devices, swap(): return lax.ppermute(array, 'gy', pairs)  18.4 us
    ppermute x14, starting transfers between devices, shift(): lax.ppermute(array, 'gz', [(i, (i + steps) % size) for i in range(size)])  17.8 us
    all_to_all x4, waiting for transfers between devices, to_experts(): return lax.all_to_all(rows, 'gx', split_axis=0, concat_axis=0, tiled=True)  14.1 us
  transfers between devices with their start and end apart: 34, of which 17 were waited for; matrix products, arithmetic and copies ran while one was open for 11% of the time, Pallas kernels for 16%

profile of v5, /device:TPU:1, one launch (start us, length us, event | category | flops | bytes accessed | tf_op | source)
XLA Modules:
  0.0 171.7 jit_solution(12924999415520108485)
XLA Ops:
  5.3 5.8 %all-to-all-start = ((bf16[8,16,3584]{2,1,0:T(8,128)(2,1)}), bf16[8,16,3584]{2,1,0:T(8,128)(2,1)S(1)}, u32[]{:S(2)}, u32[]{:S(2)}) async-start(bf16[8,16,3584]{2,1,0:T(8,128)(2,1)} %bitcast.52), calls=%async_computation | async-start | bytes 1835008 | tf_op jit(solution)/shard_map/all_to_all | solution.py:48
  14.0 10.8 %all-to-all-done = bf16[8,16,3584]{2,1,0:T(8,128)(2,1)S(1)} async-done(((bf16[8,16,3584]{2,1,0:T(8,128)(2,1)}), bf16[8,16,3584]{2,1,0:T(8,128)(2,1)S(1)}, u32[]{:S(2)}, u32[]{:S(2)}) %all-to-all-start) | async-done | bytes 917536 | tf_op jit(solution)/shard_map/all_to_all | solution.py:48
  26.5 2.1 %collective-permute-start.1 = (bf16[128,3584]{1,0:T(8,128)(2,1)S(1)}, bf16[128,3584]{1,0:T(8,128)(2,1)S(1)}, u32[]{:S(2)}, u32[]{:S(2)}) collective-permute-start(bf16[128,3584]{1,0:T(8,128)(2,1)S(1)} %bitcast.33), channel_id=1, source_target_pairs={{0,3},{1,0},{2,1},{3,2},{4,7},{5,4},{6,5},{7,6},{8,11},{9,8},{10,9... | collective-permute-start | bytes 2752520 | tf_op jit(solution)/shard_map/ppermute | solution.py:28
  28.6 5.3 %all-to-all-start.1 = ((bf16[8,16,3584]{2,1,0:T(8,128)(2,1)}), bf16[8,16,3584]{2,1,0:T(8,128)(2,1)}, u32[]{:S(2)}, u32[]{:S(2)}) async-start(bf16[8,16,3584]{2,1,0:T(8,128)(2,1)} %bitcast.51), calls=%async_computation.1 | async-start | bytes 1835008 | tf_op jit(solution)/shard_map/all_to_all | solution.py:48
  33.8 3.9 %shard_map.119 = (bf16[64,1536]{1,0:T(8,128)(2,1)S(1)}, bf16[64,1536]{1,0:T(8,128)(2,1)S(1)}, bf16[1024,3584]{1,0:T(8,128)(2,1)}) custom-call(bf16[128,3584]{1,0:T(8,128)(2,1)S(1)} %bitcast.34, bf16[1792,512]{1,0:T(8,128)(2,1)} %bitcast.42, bf16[1792,512]{1,0:T(8,128)(2,1)} %bitcast.45, bf16[512,1792]{1,0:T(8,128)(2,1)} %bitcast.48), custom_call_target="tpu_custom_call" | custom-call | flops 1 | bytes 1 | tf_op jit(solution)/shard_map/pallas_call | solution.py:53
  41.0 3.3 %collective-permute-done.2.top_in = bf16[64,1536]{1,0:T(8,128)(2,1)S(1)} collective-permute-done((bf16[64,1536]{1,0:T(8,128)(2,1)S(1)}, bf16[64,1536]{1,0:T(8,128)(2,1)S(1)}, u32[]{:S(2)}, u32[]{:S(2)}) %collective-permute-start.2) | collective-permute-done | bytes 196640 | tf_op jit(solution)/shard_map/ppermute | solution.py:36
  44.3 2.2 %collective-permute-done.3.bottom_in = bf16[64,1536]{1,0:T(8,128)(2,1)S(1)} collective-permute-done((bf16[64,1536]{1,0:T(8,128)(2,1)S(1)}, bf16[64,1536]{1,0:T(8,128)(2,1)S(1)}, u32[]{:S(2)}, u32[]{:S(2)}) %collective-permute-start.3) | collective-permute-done | bytes 196640 | tf_op jit(solution)/shard_map/ppermute | solution.py:36
  49.4 2.4 %collective-permute-start.9 = (bf16[64,3584]{1,0:T(8,128)(2,1)S(1)}, bf16[64,3584]{1,0:T(8,128)(2,1)S(1)}, u32[]{:S(2)}, u32[]{:S(2)}) collective-permute-start(bf16[64,3584]{1,0:T(8,128)(2,1)S(1)} %get-tuple-element.142), channel_id=1, source_target_pairs={{0,3},{1,0},{2,1},{3,2},{4,7},{5,4},{6,5},{7,6},{8,11},{9,8},{10,9... | collective-permute-start | bytes 1376264 | tf_op jit(solution)/shard_map/ppermute | solution.py:28
  51.8 4.0 %shard_map.122 = (bf16[64,1536]{1,0:T(8,128)(2,1)S(1)}, bf16[64,1536]{1,0:T(8,128)(2,1)S(1)}, bf16[1024,3584]{1,0:T(8,128)(2,1)}) custom-call(bf16[128,3584]{1,0:T(8,128)(2,1)} %bitcast.13.refs_0_, bf16[1792,512]{1,0:T(8,128)(2,1)} %bitcast.43, bf16[1792,512]{1,0:T(8,128)(2,1)} %bitcast.46, ...), custom_call_target="tpu_custom_call", output_to_operand_aliasing={{2}: (4, {})} | custom-call | flops 20000000000 | bytes 1 | tf_op jit(solution)/shard_map/pallas_call | solution.py:53
  59.0 2.6 %shard_map.123 = (bf16[1792,512]{1,0:T(8,128)(2,1)S(1)}, bf16[1792,512]{1,0:T(8,128)(2,1)S(1)}, bf16[512,1792]{1,0:T(8,128)(2,1)S(1)}) custom-call(bf16[1792,512]{1,0:T(8,128)(2,1)} %bitcast.44, bf16[1792,512]{1,0:T(8,128)(2,1)} %bitcast.47, bf16[512,1792]{1,0:T(8,128)(2,1)} %bitcast.50), custom_call_target="tpu_custom_call" | custom-call | tf_op jit(solution)/shard_map/pallas_call | solution.py:83
  61.7 2.7 %collective-permute-start.13 = (bf16[128,3584]{1,0:T(8,128)(2,1)}, bf16[128,3584]{1,0:T(8,128)(2,1)S(1)}, u32[]{:S(2)}, u32[]{:S(2)}) collective-permute-start(bf16[128,3584]{1,0:T(8,128)(2,1)} %bitcast.13.refs_0_), channel_id=1, source_target_pairs={{0,3},{1,0},{2,1},{3,2},{4,7},{5,4},{6,5},{7,6},{8,11},{9,8},{10,9... | collective-permute-start | bytes 2752520 | tf_op jit(solution)/shard_map/ppermute | solution.py:28
  66.4 3.3 %shard_map.125 = (bf16[192,1536]{1,0:T(8,128)(2,1)S(1)}, bf16[192,1536]{1,0:T(8,128)(2,1)S(1)}, bf16[1024,3584]{1,0:T(8,128)(2,1)}) custom-call(bf16[128,3584]{1,0:T(8,128)(2,1)S(1)} %collective-permute-done.before.refs_0_, bf16[64,3584]{1,0:T(8,128)(2,1)S(1)} %collective-permute-done.8.refs_1_, ...), custom_call_target="tpu_custom_call", output_to_operand_aliasing={{2}: (7, {})} | custom-call | flops 1 | bytes 1 | tf_op jit(solution)/shard_map/pallas_call | solution.py:53
  72.5 3.1 %shard_map.126 = (bf16[128,1920]{1,0:T(8,128)(2,1)S(1)}, bf16[128,1920]{1,0:T(8,128)(2,1)S(1)}, bf16[1024,512]{1,0:T(8,128)(2,1)}, bf16[1024,1024]{1,0:T(8,128)(2,1)}) custom-call(bf16[64,1536]{1,0:T(8,128)(2,1)S(1)} %get-tuple-element.127.refs_0_, bf16[64,1536]{1,0:T(8,128)(2,1)} %collective-permute-done.4.refs_1_, ...), custom_call_target="tpu_custom_call" | custom-call | flops 1 | bytes 1 | tf_op jit(solution)/shard_map/pallas_call | solution.py:53
  75.6 6.9 %collective-permute-done.12.before.refs_0_ = bf16[128,3584]{1,0:T(8,128)(2,1)S(1)} collective-permute-done((bf16[128,3584]{1,0:T(8,128)(2,1)}, bf16[128,3584]{1,0:T(8,128)(2,1)S(1)}, u32[]{:S(2)}, u32[]{:S(2)}) %collective-permute-start.12) | collective-permute-done | bytes 917536 | tf_op jit(solution)/shard_map/ppermute | solution.py:28
  83.3 2.7 %collective-permute-start.15 = (bf16[64,3584]{1,0:T(8,128)(2,1)S(1)}, bf16[64,3584]{1,0:T(8,128)(2,1)S(1)}, u32[]{:S(2)}, u32[]{:S(2)}) collective-permute-start(bf16[64,3584]{1,0:T(8,128)(2,1)S(1)} %get-tuple-element.174), channel_id=1, source_target_pairs={{0,3},{1,0},{2,1},{3,2},{4,7},{5,4},{6,5},{7,6},{8,11},{9,8},{10,9... | collective-permute-start | bytes 1376264 | tf_op jit(solution)/shard_map/ppermute | solution.py:28
  86.2 2.1 %collective-permute-start.20 = (bf16[192,1536]{1,0:T(8,128)(2,1)S(1)}, bf16[192,1536]{1,0:T(8,128)(2,1)S(1)}, u32[]{:S(2)}, u32[]{:S(2)}) collective-permute-start(bf16[192,1536]{1,0:T(8,128)(2,1)S(1)} %get-tuple-element.186.refs_0_), channel_id=1, source_target_pairs={{4,8},{8,4},{12,0},{0,12},{5,9},{9,5},{13,1},{1,13},{6,10},{10,6},... | collective-permute-start | bytes 1769480 | tf_op jit(solution)/shard_map/ppermute | solution.py:36
  88.3 4.7 %collective-permute-done.14.refs_1_ = bf16[64,3584]{1,0:T(8,128)(2,1)S(1)} collective-permute-done((bf16[64,3584]{1,0:T(8,128)(2,1)S(1)}, bf16[64,3584]{1,0:T(8,128)(2,1)S(1)}, u32[]{:S(2)}, u32[]{:S(2)}) %collective-permute-start.14) | collective-permute-done | bytes 458784 | tf_op jit(solution)/shard_map/ppermute | solution.py:28
  93.0 3.3 %shard_map.129 = (bf16[192,1536]{1,0:T(8,128)(2,1)S(1)}, bf16[192,1536]{1,0:T(8,128)(2,1)S(1)}, bf16[1024,3584]{1,0:T(8,128)(2,1)}) custom-call(bf16[128,3584]{1,0:T(8,128)(2,1)S(1)} %collective-permute-done.12.before.refs_0_, bf16[64,3584]{1,0:T(8,128)(2,1)S(1)} %collective-permute-done.14.refs_1_, ...), custom_call_target="tpu_custom_call", output_to_operand_aliasing={{2}: (7, {})} | custom-call | flops 20000000000 | bytes 1 | tf_op jit(solution)/shard_map/pallas_call | solution.py:53
  96.7 2.4 %collective-permute-start.19 = (bf16[192,1536]{1,0:T(8,128)(2,1)S(1)}, bf16[192,1536]{1,0:T(8,128)(2,1)S(1)}, u32[]{:S(2)}, u32[]{:S(2)}) collective-permute-start(bf16[192,1536]{1,0:T(8,128)(2,1)S(1)} %get-tuple-element.185.bottom), channel_id=1, source_target_pairs={{4,8},{8,4},{12,0},{0,12},{5,9},{9,5},{13,1},{1,13},{6,10},{10,6},... | collective-permute-start | bytes 1769480 | tf_op jit(solution)/shard_map/ppermute | solution.py:36
  99.1 2.8 %shard_map.130 = (bf16[128,1920]{1,0:T(8,128)(2,1)S(1)}, bf16[128,1920]{1,0:T(8,128)(2,1)S(1)}, bf16[128,1920]{1,0:T(8,128)(2,1)S(1)}, bf16[1024,512]{1,0:T(8,128)(2,1)}, bf16[1024,1024]{1,0:T(8,128)(2,1)}) custom-call(bf16[192,1536]{1,0:T(8,128)(2,1)S(1)} %get-tuple-element.186.refs_0_, ...), custom_call_target="tpu_custom_call", output_to_operand_aliasing={{3}: (6, {}), {4}: (7, {})} | custom-call | flops 1 | bytes 1 | tf_op jit(solution)/shard_map/pallas_call | solution.py:53
  101.9 2.5 %collective-permute-start.24 = (bf16[128,1920]{1,0:T(8,128)(2,1)S(1)}, bf16[128,1920]{1,0:T(8,128)(2,1)S(1)}, u32[]{:S(2)}, u32[]{:S(2)}) collective-permute-start(bf16[128,1920]{1,0:T(8,128)(2,1)S(1)} %get-tuple-element.198), channel_id=1, source_target_pairs={{0,3},{1,0},{2,1},{3,2},{4,7},{5,4},{6,5},{7,6},{8,11},{9,8},{10,9... | collective-permute-start | bytes 1474568 | tf_op jit(solution)/shard_map/ppermute | solution.py:28
  105.6 6.2 %collective-permute-done.18.top_in = bf16[192,1536]{1,0:T(8,128)(2,1)S(1)} collective-permute-done((bf16[192,1536]{1,0:T(8,128)(2,1)S(1)}, bf16[192,1536]{1,0:T(8,128)(2,1)S(1)}, u32[]{:S(2)}, u32[]{:S(2)}) %collective-permute-start.18) | collective-permute-done | bytes 589856 | tf_op jit(solution)/shard_map/ppermute | solution.py:36
  116.4 2.7 %collective-permute-done.25.second = bf16[128,1920]{1,0:T(8,128)(2,1)S(1)} collective-permute-done((bf16[128,1920]{1,0:T(8,128)(2,1)S(1)}, bf16[128,1920]{1,0:T(8,128)(2,1)S(1)}, u32[]{:S(2)}, u32[]{:S(2)}) %collective-permute-start.25) | collective-permute-done | bytes 491552 | tf_op jit(solution)/shard_map/ppermute | solution.py:28
  120.1 4.4 %collective-permute-done.22.refs_1_ = bf16[192,1536]{1,0:T(8,128)(2,1)S(1)} collective-permute-done((bf16[192,1536]{1,0:T(8,128)(2,1)S(1)}, bf16[192,1536]{1,0:T(8,128)(2,1)S(1)}, u32[]{:S(2)}, u32[]{:S(2)}) %collective-permute-start.22) | collective-permute-done | bytes 589856 | tf_op jit(solution)/shard_map/ppermute | solution.py:36
  125.7 3.8 %shard_map.133 = (bf16[128,1920]{1,0:T(8,128)(2,1)}, bf16[128,1920]{1,0:T(8,128)(2,1)}, bf16[128,1920]{1,0:T(8,128)(2,1)}, bf16[1024,512]{1,0:T(8,128)(2,1)}, bf16[1024,1024]{1,0:T(8,128)(2,1)}) custom-call(bf16[192,1536]{1,0:T(8,128)(2,1)S(1)} %get-tuple-element.205.refs_0_, ...), custom_call_target="tpu_custom_call", output_to_operand_aliasing={{3}: (6, {}), {4}: (7, {})} | custom-call | flops 1 | bytes 1 | tf_op jit(solution)/shard_map/pallas_call | solution.py:53
  131.4 9.1 %all-to-all-start.2 = ((bf16[8,16,1920]{2,1,0:T(8,128)(2,1)}), bf16[8,16,1920]{2,1,0:T(8,128)(2,1)S(1)}, u32[]{:S(2)}, u32[]{:S(2)}) async-start(bf16[8,16,1920]{2,1,0:T(8,128)(2,1)} %bitcast.41), calls=%async_computation.2 | async-start | bytes 983040 | tf_op jit(solution)/shard_map/all_to_all | solution.py:48
  140.5 5.8 %fusion.9 = bf16[1792,512]{1,0:T(8,128)(2,1)} fusion(bf16[1024,3584]{1,0:T(8,128)(2,1)} %get-tuple-element.220, bf16[1024,1024]{1,0:T(8,128)(2,1)} %get-tuple-element.221), kind=kOutput, calls=%fused_computation.7 | convolution fusion | flops 1879965696 | bytes 6553600 | tf_op jit(solution)/shard_map/dot_general | solution.py:23
  146.3 5.4 %fusion.6 = bf16[1792,512]{1,0:T(8,128)(2,1)} fusion(bf16[1024,3584]{1,0:T(8,128)(2,1)} %get-tuple-element.220, bf16[1024,1024]{1,0:T(8,128)(2,1)S(1)} %copy-done.3), kind=kOutput, calls=%fused_computation.6 | convolution fusion | flops 1879965696 | bytes 6553600 | tf_op jit(solution)/shard_map/dot_general | solution.py:23
  155.5 4.6 %all-to-all-start.3 = ((bf16[8,16,1920]{2,1,0:T(8,128)(2,1)}), bf16[8,16,1920]{2,1,0:T(8,128)(2,1)S(1)}, u32[]{:S(2)}, u32[]{:S(2)}) async-start(bf16[8,16,1920]{2,1,0:T(8,128)(2,1)} %bitcast.16), calls=%async_computation.3 | async-start | bytes 983040 | tf_op jit(solution)/shard_map/all_to_all | solution.py:48
  160.2 5.8 %fusion.12 = bf16[512,1792]{1,0:T(8,128)(2,1)} fusion(bf16[1024,512]{1,0:T(8,128)(2,1)} %get-tuple-element.228, bf16[1024,3584]{1,0:T(8,128)(2,1)} %get-tuple-element.220), kind=kOutput, calls=%fused_computation.8 | convolution fusion | flops 1879965696 | bytes 6553600 | tf_op jit(solution)/shard_map/dot_general | solution.py:23
  166.0 3.3 %all-to-all-done.3 = bf16[8,16,1920]{2,1,0:T(8,128)(2,1)S(1)} async-done(((bf16[8,16,1920]{2,1,0:T(8,128)(2,1)}), bf16[8,16,1920]{2,1,0:T(8,128)(2,1)S(1)}, u32[]{:S(2)}, u32[]{:S(2)}) %all-to-all-start.3) | async-done | bytes 491552 | tf_op jit(solution)/shard_map/all_to_all | solution.py:48
  169.3 2.4 %shard_map.135 = (bf16[512,1792]{1,0:T(8,128)(2,1)}, f32[8,32]{1,0:T(8,128)}) custom-call(s32[8,32]{1,0:T(8,128)S(1)} %get-tuple-element.242.usable, f32[8,32]{1,0:T(8,128)S(1)} %bitcast_convert_fusion.score, bf16[128,512]{1,0:T(8,128)(2,1)S(1)} %bitcast.38, bf16[128,512]{1,0:T(8,128)(2,1)S(1)} %bitcast.40, bf16[128,1920]{1,0:T(8,128)(2,1)S(1)} %bitcast.35, ...), custom_call_target="tpu_custom_call" | custom-call | flops 1 | bytes 1 | tf_op jit(solution)/shard_map/pallas_call | solution.py:53
  (80 shorter events, 38.5 us)
Async XLA Ops:
  5.3 19.5 %all-to-all-start = ((bf16[8,16,3584]{2,1,0:T(8,128)(2,1)}), bf16[8,16,3584]{2,1,0:T(8,128)(2,1)S(1)}, u32[]{:S(2)}, u32[]{:S(2)}) async-start(bf16[8,16,3584]{2,1,0:T(8,128)(2,1)} %bitcast.52), calls=%async_computation | async-start | bytes 1835008 | tf_op jit(solution)/shard_map/all_to_all | solution.py:48
  24.8 23.7 %collective-permute-start = (bf16[128,3584]{1,0:T(8,128)(2,1)S(1)}, bf16[128,3584]{1,0:T(8,128)(2,1)S(1)}, u32[]{:S(2)}, u32[]{:S(2)}) collective-permute-start(bf16[128,3584]{1,0:T(8,128)(2,1)S(1)} %bitcast.32), channel_id=1, source_target_pairs={{0,1},{1,2},{2,3},{3,0},{4,5},{5,6},{6,7},{7,4},{8,9},{9,10},{10,1... | collective-permute-start | bytes 2752520 | tf_op jit(solution)/shard_map/ppermute | solution.py:28
  26.5 22.0 %collective-permute-start.1 = (bf16[128,3584]{1,0:T(8,128)(2,1)S(1)}, bf16[128,3584]{1,0:T(8,128)(2,1)S(1)}, u32[]{:S(2)}, u32[]{:S(2)}) collective-permute-start(bf16[128,3584]{1,0:T(8,128)(2,1)S(1)} %bitcast.33), channel_id=1, source_target_pairs={{0,3},{1,0},{2,1},{3,2},{4,7},{5,4},{6,5},{7,6},{8,11},{9,8},{10,9... | collective-permute-start | bytes 2752520 | tf_op jit(solution)/shard_map/ppermute | solution.py:28
  28.6 19.9 %all-to-all-start.1 = ((bf16[8,16,3584]{2,1,0:T(8,128)(2,1)}), bf16[8,16,3584]{2,1,0:T(8,128)(2,1)}, u32[]{:S(2)}, u32[]{:S(2)}) async-start(bf16[8,16,3584]{2,1,0:T(8,128)(2,1)} %bitcast.51), calls=%async_computation.1 | async-start | bytes 1835008 | tf_op jit(solution)/shard_map/all_to_all | solution.py:48
  37.8 6.6 %collective-permute-start.2 = (bf16[64,1536]{1,0:T(8,128)(2,1)S(1)}, bf16[64,1536]{1,0:T(8,128)(2,1)S(1)}, u32[]{:S(2)}, u32[]{:S(2)}) collective-permute-start(bf16[64,1536]{1,0:T(8,128)(2,1)S(1)} %get-tuple-element.123.top), channel_id=1, source_target_pairs={{0,4},{4,0},{8,12},{12,8},{1,5},{5,1},{9,13},{13,9},{2,6},{6,2},{1... | collective-permute-start | bytes 589832 | tf_op jit(solution)/shard_map/ppermute | solution.py:36
  39.1 7.4 %collective-permute-start.3 = (bf16[64,1536]{1,0:T(8,128)(2,1)S(1)}, bf16[64,1536]{1,0:T(8,128)(2,1)S(1)}, u32[]{:S(2)}, u32[]{:S(2)}) collective-permute-start(bf16[64,1536]{1,0:T(8,128)(2,1)S(1)} %get-tuple-element.124.bottom), channel_id=1, source_target_pairs={{4,8},{8,4},{12,0},{0,12},{5,9},{9,5},{13,1},{1,13},{6,10},{10,6},... | collective-permute-start | bytes 589832 | tf_op jit(solution)/shard_map/ppermute | solution.py:36
  46.6 9.2 %collective-permute-start.4 = (bf16[64,1536]{1,0:T(8,128)(2,1)S(1)}, bf16[64,1536]{1,0:T(8,128)(2,1)}, u32[]{:S(2)}, u32[]{:S(2)}) collective-permute-start(bf16[64,1536]{1,0:T(8,128)(2,1)S(1)} %get-tuple-element.127.refs_0_), channel_id=1, source_target_pairs={{4,8},{8,4},{12,0},{0,12},{5,9},{9,5},{13,1},{1,13},{6,10},{10,6},... | collective-permute-start | bytes 589832 | tf_op jit(solution)/shard_map/ppermute | solution.py:36
  48.5 7.3 %collective-permute-start.5 = (bf16[64,1536]{1,0:T(8,128)(2,1)S(1)}, bf16[64,1536]{1,0:T(8,128)(2,1)}, u32[]{:S(2)}, u32[]{:S(2)}) collective-permute-start(bf16[64,1536]{1,0:T(8,128)(2,1)S(1)} %get-tuple-element.128.refs_2_), channel_id=1, source_target_pairs={{0,4},{4,0},{8,12},{12,8},{1,5},{5,1},{9,13},{13,9},{2,6},{6,2},{1... | collective-permute-start | bytes 589832 | tf_op jit(solution)/shard_map/ppermute | solution.py:36
  49.1 12.6 %collective-permute-start.8 = (bf16[64,3584]{1,0:T(8,128)(2,1)S(1)}, bf16[64,3584]{1,0:T(8,128)(2,1)S(1)}, u32[]{:S(2)}, u32[]{:S(2)}) collective-permute-start(bf16[64,3584]{1,0:T(8,128)(2,1)S(1)} %get-tuple-element.133), channel_id=1, source_target_pairs={{0,1},{1,2},{2,3},{3,0},{4,5},{5,6},{6,7},{7,4},{8,9},{9,10},{10,1... | collective-permute-start | bytes 1376264 | tf_op jit(solution)/shard_map/ppermute | solution.py:28
  49.4 12.2 %collective-permute-start.9 = (bf16[64,3584]{1,0:T(8,128)(2,1)S(1)}, bf16[64,3584]{1,0:T(8,128)(2,1)S(1)}, u32[]{:S(2)}, u32[]{:S(2)}) collective-permute-start(bf16[64,3584]{1,0:T(8,128)(2,1)S(1)} %get-tuple-element.142), channel_id=1, source_target_pairs={{0,3},{1,0},{2,1},{3,2},{4,7},{5,4},{6,5},{7,6},{8,11},{9,8},{10,9... | collective-permute-start | bytes 1376264 | tf_op jit(solution)/shard_map/ppermute | solution.py:28
  55.8 8.6 %collective-permute-start.6 = (bf16[64,1536]{1,0:T(8,128)(2,1)S(1)}, bf16[64,1536]{1,0:T(8,128)(2,1)S(1)}, u32[]{:S(2)}, u32[]{:S(2)}) collective-permute-start(bf16[64,1536]{1,0:T(8,128)(2,1)S(1)} %get-tuple-element.152.top), channel_id=1, source_target_pairs={{0,4},{4,0},{8,12},{12,8},{1,5},{5,1},{9,13},{13,9},{2,6},{6,2},{1... | collective-permute-start | bytes 589832 | tf_op jit(solution)/shard_map/ppermute | solution.py:36
  57.3 7.1 %collective-permute-start.7 = (bf16[64,1536]{1,0:T(8,128)(2,1)S(1)}, bf16[64,1536]{1,0:T(8,128)(2,1)S(1)}, u32[]{:S(2)}, u32[]{:S(2)}) collective-permute-start(bf16[64,1536]{1,0:T(8,128)(2,1)S(1)} %get-tuple-element.141.bottom), channel_id=1, source_target_pairs={{4,8},{8,4},{12,0},{0,12},{5,9},{9,5},{13,1},{1,13},{6,10},{10,6},... | collective-permute-start | bytes 589832 | tf_op jit(solution)/shard_map/ppermute | solution.py:36
  61.7 20.8 %collective-permute-start.12 = (bf16[128,3584]{1,0:T(8,128)(2,1)}, bf16[128,3584]{1,0:T(8,128)(2,1)S(1)}, u32[]{:S(2)}, u32[]{:S(2)}) collective-permute-start(bf16[128,3584]{1,0:T(8,128)(2,1)} %bitcast.13.refs_0_), channel_id=1, source_target_pairs={{0,1},{1,2},{2,3},{3,0},{4,5},{5,6},{6,7},{7,4},{8,9},{9,10},{10,1... | collective-permute-start | bytes 2752520 | tf_op jit(solution)/shard_map/ppermute | solution.py:28
  61.7 20.7 %collective-permute-start.13 = (bf16[128,3584]{1,0:T(8,128)(2,1)}, bf16[128,3584]{1,0:T(8,128)(2,1)S(1)}, u32[]{:S(2)}, u32[]{:S(2)}) collective-permute-start(bf16[128,3584]{1,0:T(8,128)(2,1)} %bitcast.13.refs_0_), channel_id=1, source_target_pairs={{0,3},{1,0},{2,1},{3,2},{4,7},{5,4},{6,5},{7,6},{8,11},{9,8},{10,9... | collective-permute-start | bytes 2752520 | tf_op jit(solution)/shard_map/ppermute | solution.py:28
  71.2 14.7 %collective-permute-start.16 = (bf16[192,1536]{1,0:T(8,128)(2,1)S(1)}, bf16[192,1536]{1,0:T(8,128)(2,1)S(1)}, u32[]{:S(2)}, u32[]{:S(2)}) collective-permute-start(bf16[192,1536]{1,0:T(8,128)(2,1)S(1)} %get-tuple-element.175.top), channel_id=1, source_target_pairs={{0,4},{4,0},{8,12},{12,8},{1,5},{5,1},{9,13},{13,9},{2,6},{6,2},{1... | collective-permute-start | bytes 1769480 | tf_op jit(solution)/shard_map/ppermute | solution.py:36
  71.3 14.6 %collective-permute-start.17 = (bf16[192,1536]{1,0:T(8,128)(2,1)S(1)}, bf16[192,1536]{1,0:T(8,128)(2,1)S(1)}, u32[]{:S(2)}, u32[]{:S(2)}) collective-permute-start(bf16[192,1536]{1,0:T(8,128)(2,1)S(1)} %get-tuple-element.176.bottom), channel_id=1, source_target_pairs={{4,8},{8,4},{12,0},{0,12},{5,9},{9,5},{13,1},{1,13},{6,10},{10,6},... | collective-permute-start | bytes 1769480 | tf_op jit(solution)/shard_map/ppermute | solution.py:36
  83.0 10.0 %collective-permute-start.14 = (bf16[64,3584]{1,0:T(8,128)(2,1)S(1)}, bf16[64,3584]{1,0:T(8,128)(2,1)S(1)}, u32[]{:S(2)}, u32[]{:S(2)}) collective-permute-start(bf16[64,3584]{1,0:T(8,128)(2,1)S(1)} %get-tuple-element.173), channel_id=1, source_target_pairs={{0,1},{1,2},{2,3},{3,0},{4,5},{5,6},{6,7},{7,4},{8,9},{9,10},{10,1... | collective-permute-start | bytes 1376264 | tf_op jit(solution)/shard_map/ppermute | solution.py:28
  83.3 9.7 %collective-permute-start.15 = (bf16[64,3584]{1,0:T(8,128)(2,1)S(1)}, bf16[64,3584]{1,0:T(8,128)(2,1)S(1)}, u32[]{:S(2)}, u32[]{:S(2)}) collective-permute-start(bf16[64,3584]{1,0:T(8,128)(2,1)S(1)} %get-tuple-element.174), channel_id=1, source_target_pairs={{0,3},{1,0},{2,1},{3,2},{4,7},{5,4},{6,5},{7,6},{8,11},{9,8},{10,9... | collective-permute-start | bytes 1376264 | tf_op jit(solution)/shard_map/ppermute | solution.py:28
  86.2 12.9 %collective-permute-start.20 = (bf16[192,1536]{1,0:T(8,128)(2,1)S(1)}, bf16[192,1536]{1,0:T(8,128)(2,1)S(1)}, u32[]{:S(2)}, u32[]{:S(2)}) collective-permute-start(bf16[192,1536]{1,0:T(8,128)(2,1)S(1)} %get-tuple-element.186.refs_0_), channel_id=1, source_target_pairs={{4,8},{8,4},{12,0},{0,12},{5,9},{9,5},{13,1},{1,13},{6,10},{10,6},... | collective-permute-start | bytes 1769480 | tf_op jit(solution)/shard_map/ppermute | solution.py:36
  88.3 10.8 %collective-permute-start.21 = (bf16[192,1536]{1,0:T(8,128)(2,1)S(1)}, bf16[192,1536]{1,0:T(8,128)(2,1)S(1)}, u32[]{:S(2)}, u32[]{:S(2)}) collective-permute-start(bf16[192,1536]{1,0:T(8,128)(2,1)S(1)} %get-tuple-element.189.refs_2_), channel_id=1, source_target_pairs={{0,4},{4,0},{8,12},{12,8},{1,5},{5,1},{9,13},{13,9},{2,6},{6,2},{1... | collective-permute-start | bytes 1769480 | tf_op jit(solution)/shard_map/ppermute | solution.py:36
  96.3 15.5 %collective-permute-start.18 = (bf16[192,1536]{1,0:T(8,128)(2,1)S(1)}, bf16[192,1536]{1,0:T(8,128)(2,1)S(1)}, u32[]{:S(2)}, u32[]{:S(2)}) collective-permute-start(bf16[192,1536]{1,0:T(8,128)(2,1)S(1)} %get-tuple-element.184.top), channel_id=1, source_target_pairs={{0,4},{4,0},{8,12},{12,8},{1,5},{5,1},{9,13},{13,9},{2,6},{6,2},{1... | collective-permute-start | bytes 1769480 | tf_op jit(solution)/shard_map/ppermute | solution.py:36
  96.7 15.7 %collective-permute-start.19 = (bf16[192,1536]{1,0:T(8,128)(2,1)S(1)}, bf16[192,1536]{1,0:T(8,128)(2,1)S(1)}, u32[]{:S(2)}, u32[]{:S(2)}) collective-permute-start(bf16[192,1536]{1,0:T(8,128)(2,1)S(1)} %get-tuple-element.185.bottom), channel_id=1, source_target_pairs={{4,8},{8,4},{12,0},{0,12},{5,9},{9,5},{13,1},{1,13},{6,10},{10,6},... | collective-permute-start | bytes 1769480 | tf_op jit(solution)/shard_map/ppermute | solution.py:36
  101.9 14.5 %collective-permute-start.24 = (bf16[128,1920]{1,0:T(8,128)(2,1)S(1)}, bf16[128,1920]{1,0:T(8,128)(2,1)S(1)}, u32[]{:S(2)}, u32[]{:S(2)}) collective-permute-start(bf16[128,1920]{1,0:T(8,128)(2,1)S(1)} %get-tuple-element.198), channel_id=1, source_target_pairs={{0,3},{1,0},{2,1},{3,2},{4,7},{5,4},{6,5},{7,6},{8,11},{9,8},{10,9... | collective-permute-start | bytes 1474568 | tf_op jit(solution)/shard_map/ppermute | solution.py:28
  104.4 14.8 %collective-permute-start.25 = (bf16[128,1920]{1,0:T(8,128)(2,1)S(1)}, bf16[128,1920]{1,0:T(8,128)(2,1)S(1)}, u32[]{:S(2)}, u32[]{:S(2)}) collective-permute-start(bf16[128,1920]{1,0:T(8,128)(2,1)S(1)} %get-tuple-element.199), channel_id=1, source_target_pairs={{0,1},{1,2},{2,3},{3,0},{4,5},{5,6},{6,7},{7,4},{8,9},{9,10},{10,1... | collective-permute-start | bytes 1474568 | tf_op jit(solution)/shard_map/ppermute | solution.py:28
  104.4 15.3 %collective-permute-start.26 = (bf16[128,1920]{1,0:T(8,128)(2,1)S(1)}, bf16[128,1920]{1,0:T(8,128)(2,1)S(1)}, u32[]{:S(2)}, u32[]{:S(2)}) collective-permute-start(bf16[128,1920]{1,0:T(8,128)(2,1)S(1)} %get-tuple-element.193), channel_id=1, source_target_pairs={{0,2},{1,3},{2,0},{3,1},{4,6},{5,7},{6,4},{7,5},{8,10},{9,11},{10,... | collective-permute-start | bytes 1474568 | tf_op jit(solution)/shard_map/ppermute | solution.py:28
  112.7 11.8 %collective-permute-start.22 = (bf16[192,1536]{1,0:T(8,128)(2,1)S(1)}, bf16[192,1536]{1,0:T(8,128)(2,1)S(1)}, u32[]{:S(2)}, u32[]{:S(2)}) collective-permute-start(bf16[192,1536]{1,0:T(8,128)(2,1)S(1)} %get-tuple-element.205.refs_0_), channel_id=1, source_target_pairs={{4,8},{8,4},{12,0},{0,12},{5,9},{9,5},{13,1},{1,13},{6,10},{10,6},... | collective-permute-start | bytes 1769480 | tf_op jit(solution)/shard_map/ppermute | solution.py:36
  114.7 11.0 %collective-permute-start.23 = (bf16[192,1536]{1,0:T(8,128)(2,1)S(1)}, bf16[192,1536]{1,0:T(8,128)(2,1)S(1)}, u32[]{:S(2)}, u32[]{:S(2)}) collective-permute-start(bf16[192,1536]{1,0:T(8,128)(2,1)S(1)} %get-tuple-element.207.refs_2_), channel_id=1, source_target_pairs={{0,4},{4,0},{8,12},{12,8},{1,5},{5,1},{9,13},{13,9},{2,6},{6,2},{1... | collective-permute-start | bytes 1769480 | tf_op jit(solution)/shard_map/ppermute | solution.py:36
  129.5 22.2 %collective-permute-start.29 = (bf16[128,1920]{1,0:T(8,128)(2,1)}, bf16[128,1920]{1,0:T(8,128)(2,1)S(1)}, u32[]{:S(2)}, u32[]{:S(2)}) collective-permute-start(bf16[128,1920]{1,0:T(8,128)(2,1)} %get-tuple-element.215), channel_id=1, source_target_pairs={{0,2},{1,3},{2,0},{3,1},{4,6},{5,7},{6,4},{7,5},{8,10},{9,11},{10,... | collective-permute-start | bytes 1474568 | tf_op jit(solution)/shard_map/ppermute | solution.py:28
  129.9 23.0 %collective-permute-start.27 = (bf16[128,1920]{1,0:T(8,128)(2,1)}, bf16[128,1920]{1,0:T(8,128)(2,1)S(1)}, u32[]{:S(2)}, u32[]{:S(2)}) collective-permute-start(bf16[128,1920]{1,0:T(8,128)(2,1)} %get-tuple-element.211), channel_id=1, source_target_pairs={{0,3},{1,0},{2,1},{3,2},{4,7},{5,4},{6,5},{7,6},{8,11},{9,8},{10,9... | collective-permute-start | bytes 1474568 | tf_op jit(solution)/shard_map/ppermute | solution.py:28
  131.3 23.0 %collective-permute-start.28 = (bf16[128,1920]{1,0:T(8,128)(2,1)}, bf16[128,1920]{1,0:T(8,128)(2,1)S(1)}, u32[]{:S(2)}, u32[]{:S(2)}) collective-permute-start(bf16[128,1920]{1,0:T(8,128)(2,1)} %get-tuple-element.212), channel_id=1, source_target_pairs={{0,1},{1,2},{2,3},{3,0},{4,5},{5,6},{6,7},{7,4},{8,9},{9,10},{10,1... | collective-permute-start | bytes 1474568 | tf_op jit(solution)/shard_map/ppermute | solution.py:28
  131.4 24.1 %all-to-all-start.2 = ((bf16[8,16,1920]{2,1,0:T(8,128)(2,1)}), bf16[8,16,1920]{2,1,0:T(8,128)(2,1)S(1)}, u32[]{:S(2)}, u32[]{:S(2)}) async-start(bf16[8,16,1920]{2,1,0:T(8,128)(2,1)} %bitcast.41), calls=%async_computation.2 | async-start | bytes 983040 | tf_op jit(solution)/shard_map/all_to_all | solution.py:48
  155.5 13.8 %all-to-all-start.3 = ((bf16[8,16,1920]{2,1,0:T(8,128)(2,1)}), bf16[8,16,1920]{2,1,0:T(8,128)(2,1)S(1)}, u32[]{:S(2)}, u32[]{:S(2)}) async-start(bf16[8,16,1920]{2,1,0:T(8,128)(2,1)} %bitcast.16), calls=%async_computation.3 | async-start | bytes 983040 | tf_op jit(solution)/shard_map/all_to_all | solution.py:48
  (9 other events, 51.0 us)

commit v6 on v5

--- a/solution.py
+++ b/solution.py
@@ -286,13 +286,19 @@
 
 def final_kernel(chunks, usable, score, *refs):
     picks, backs = refs[:chunks], refs[chunks : 2 * chunks]
-    input_grad, score_grad = refs[2 * chunks :]
+    input_grad, score_grad, block, sems = refs[2 * chunks :]
     width = input_grad.shape[1]
+    copies = []
+    for i in range(2):
+        place = slice(i * width // 2, (i + 1) * width // 2)
+        total = sum(dot(p[...], b[:, place], CONTRACT_FIRST) for p, b in zip(picks, backs))
+        block[i] = total.astype(BF16)
+        target = input_grad.at[:, pl.ds(i * width // 2, width // 2)]
+        copies.append(pltpu.make_async_copy(block.at[i], target, sems.at[i]))
+        copies[i].start()
     experts, slots = score.shape
     rows = backs[0].shape[0]
     part_slots = rows // experts
-    total = sum(dot(p[...], b[:, :width], CONTRACT_FIRST) for p, b in zip(picks, backs))
-    input_grad[...] = total.astype(BF16)
     row = lax.broadcasted_iota(jnp.int32, (rows, slots), 0)
     column = lax.broadcasted_iota(jnp.int32, (rows, slots), 1)
     expert = (
@@ -306,6 +312,8 @@
             spread = jnp.where(column == c * part_slots + row % part_slots, value, 0.0)
             table += dot(expert, spread.astype(BF16))
     score_grad[...] = jnp.where(usable[...] > 0, table / score[...], 0.0)
+    for copy in copies:
+        copy.wait()
 
 
 def final(usable, score, picks, backs):
@@ -313,8 +321,9 @@
     return call(
         functools.partial(final_kernel, len(picks)),
         [((group, width), BF16), (score.shape, F32)],
-        [],
+        [pltpu.VMEM((2, group, width // 2), BF16), pltpu.SemaphoreType.DMA((2,))],
         [usable.astype(jnp.int32), score.astype(F32), *picks, *backs],
+        out_hbm=(0,),
     )
 
 

time: 172 us -> 173 us (level)
  transfers between devices with their start and end apart: 34 -> 34, of which waited for: 17 -> 17; matrix products, arithmetic and copies ran while one was open for 11% -> 11% of each run, Pallas kernels for 16% -> 15%
where the time goes in v6:
time: 173 us; the launch traced here: 172 us
  starting transfers between devices  61 us (35%)
  waiting for transfers between devices  52.4 us (30%)
  Pallas kernels  33.2 us (19%)
  matrix products  18.7 us (11%)
  other arithmetic  3.72 us (2%)
  local copies, waits for them, and re-layouts  2.15 us (1%)
    pallas_call x16, Pallas kernels, call(): pl.pallas_call(kernel, out_shape=[pltpu.HBM(*o) if i in out_hbm else jax....  30.5 us
    all_to_all x4, starting transfers between devices, to_experts(): return lax.all_to_all(rows, 'gx', split_axis=0, concat_axis=0, tiled=True)  24.8 us
    ppermute x16, waiting for transfers between devices, swap(): return lax.ppermute(array, 'gy', pairs)  19.3 us
    ppermute x14, waiting for transfers between devices, shift(): lax.ppermute(array, 'gz', [(i, (i + steps) % size) for i in range(size)])  19 us
    dot_general x7, matrix products, dot(): return lax.dot_general(left, right, dims, preferred_element_type=F32)  18.7 us
    ppermute x16, starting transfers between devices, swap(): return lax.ppermute(array, 'gy', pairs)  18.4 us
    ppermute x14, starting transfers between devices, shift(): lax.ppermute(array, 'gz', [(i, (i + steps) % size) for i in range(size)])  17.8 us
    all_to_all x4, waiting for transfers between devices, to_experts(): return lax.all_to_all(rows, 'gx', split_axis=0, concat_axis=0, tiled=True)  14.1 us
  transfers between devices with their start and end apart: 34, of which 17 were waited for; matrix products, arithmetic and copies ran while one was open for 11% of the time, Pallas kernels for 15%

profile of v6, /device:TPU:1, one launch (start us, length us, event | category | flops | bytes accessed | tf_op | source)
XLA Modules:
  0.0 172.2 jit_solution(1157646198152146276)
XLA Ops:
  5.3 5.8 %all-to-all-start = ((bf16[8,16,3584]{2,1,0:T(8,128)(2,1)}), bf16[8,16,3584]{2,1,0:T(8,128)(2,1)S(1)}, u32[]{:S(2)}, u32[]{:S(2)}) async-start(bf16[8,16,3584]{2,1,0:T(8,128)(2,1)} %bitcast.52), calls=%async_computation | async-start | bytes 1835008 | tf_op jit(solution)/shard_map/all_to_all | solution.py:48
  14.0 10.8 %all-to-all-done = bf16[8,16,3584]{2,1,0:T(8,128)(2,1)S(1)} async-done(((bf16[8,16,3584]{2,1,0:T(8,128)(2,1)}), bf16[8,16,3584]{2,1,0:T(8,128)(2,1)S(1)}, u32[]{:S(2)}, u32[]{:S(2)}) %all-to-all-start) | async-done | bytes 917536 | tf_op jit(solution)/shard_map/all_to_all | solution.py:48
  26.5 2.1 %collective-permute-start.1 = (bf16[128,3584]{1,0:T(8,128)(2,1)S(1)}, bf16[128,3584]{1,0:T(8,128)(2,1)S(1)}, u32[]{:S(2)}, u32[]{:S(2)}) collective-permute-start(bf16[128,3584]{1,0:T(8,128)(2,1)S(1)} %bitcast.33), channel_id=1, source_target_pairs={{0,3},{1,0},{2,1},{3,2},{4,7},{5,4},{6,5},{7,6},{8,11},{9,8},{10,9... | collective-permute-start | bytes 2752520 | tf_op jit(solution)/shard_map/ppermute | solution.py:28
  28.6 5.3 %all-to-all-start.1 = ((bf16[8,16,3584]{2,1,0:T(8,128)(2,1)}), bf16[8,16,3584]{2,1,0:T(8,128)(2,1)}, u32[]{:S(2)}, u32[]{:S(2)}) async-start(bf16[8,16,3584]{2,1,0:T(8,128)(2,1)} %bitcast.51), calls=%async_computation.1 | async-start | bytes 1835008 | tf_op jit(solution)/shard_map/all_to_all | solution.py:48
  33.8 3.9 %shard_map.119 = (bf16[64,1536]{1,0:T(8,128)(2,1)S(1)}, bf16[64,1536]{1,0:T(8,128)(2,1)S(1)}, bf16[1024,3584]{1,0:T(8,128)(2,1)}) custom-call(bf16[128,3584]{1,0:T(8,128)(2,1)S(1)} %bitcast.34, bf16[1792,512]{1,0:T(8,128)(2,1)} %bitcast.42, bf16[1792,512]{1,0:T(8,128)(2,1)} %bitcast.45, bf16[512,1792]{1,0:T(8,128)(2,1)} %bitcast.48), custom_call_target="tpu_custom_call" | custom-call | flops 1 | bytes 1 | tf_op jit(solution)/shard_map/pallas_call | solution.py:53
  41.0 3.3 %collective-permute-done.2.top_in = bf16[64,1536]{1,0:T(8,128)(2,1)S(1)} collective-permute-done((bf16[64,1536]{1,0:T(8,128)(2,1)S(1)}, bf16[64,1536]{1,0:T(8,128)(2,1)S(1)}, u32[]{:S(2)}, u32[]{:S(2)}) %collective-permute-start.2) | collective-permute-done | bytes 196640 | tf_op jit(solution)/shard_map/ppermute | solution.py:36
  44.3 2.2 %collective-permute-done.3.bottom_in = bf16[64,1536]{1,0:T(8,128)(2,1)S(1)} collective-permute-done((bf16[64,1536]{1,0:T(8,128)(2,1)S(1)}, bf16[64,1536]{1,0:T(8,128)(2,1)S(1)}, u32[]{:S(2)}, u32[]{:S(2)}) %collective-permute-start.3) | collective-permute-done | bytes 196640 | tf_op jit(solution)/shard_map/ppermute | solution.py:36
  49.4 2.4 %collective-permute-start.9 = (bf16[64,3584]{1,0:T(8,128)(2,1)S(1)}, bf16[64,3584]{1,0:T(8,128)(2,1)S(1)}, u32[]{:S(2)}, u32[]{:S(2)}) collective-permute-start(bf16[64,3584]{1,0:T(8,128)(2,1)S(1)} %get-tuple-element.142), channel_id=1, source_target_pairs={{0,3},{1,0},{2,1},{3,2},{4,7},{5,4},{6,5},{7,6},{8,11},{9,8},{10,9... | collective-permute-start | bytes 1376264 | tf_op jit(solution)/shard_map/ppermute | solution.py:28
  51.8 4.0 %shard_map.122 = (bf16[64,1536]{1,0:T(8,128)(2,1)S(1)}, bf16[64,1536]{1,0:T(8,128)(2,1)S(1)}, bf16[1024,3584]{1,0:T(8,128)(2,1)}) custom-call(bf16[128,3584]{1,0:T(8,128)(2,1)} %bitcast.13.refs_0_, bf16[1792,512]{1,0:T(8,128)(2,1)} %bitcast.43, bf16[1792,512]{1,0:T(8,128)(2,1)} %bitcast.46, ...), custom_call_target="tpu_custom_call", output_to_operand_aliasing={{2}: (4, {})} | custom-call | flops 20000000000 | bytes 1 | tf_op jit(solution)/shard_map/pallas_call | solution.py:53
  59.0 2.6 %shard_map.123 = (bf16[1792,512]{1,0:T(8,128)(2,1)S(1)}, bf16[1792,512]{1,0:T(8,128)(2,1)S(1)}, bf16[512,1792]{1,0:T(8,128)(2,1)S(1)}) custom-call(bf16[1792,512]{1,0:T(8,128)(2,1)} %bitcast.44, bf16[1792,512]{1,0:T(8,128)(2,1)} %bitcast.47, bf16[512,1792]{1,0:T(8,128)(2,1)} %bitcast.50), custom_call_target="tpu_custom_call" | custom-call | tf_op jit(solution)/shard_map/pallas_call | solution.py:83
  61.7 2.7 %collective-permute-start.13 = (bf16[128,3584]{1,0:T(8,128)(2,1)}, bf16[128,3584]{1,0:T(8,128)(2,1)S(1)}, u32[]{:S(2)}, u32[]{:S(2)}) collective-permute-start(bf16[128,3584]{1,0:T(8,128)(2,1)} %bitcast.13.refs_0_), channel_id=1, source_target_pairs={{0,3},{1,0},{2,1},{3,2},{4,7},{5,4},{6,5},{7,6},{8,11},{9,8},{10,9... | collective-permute-start | bytes 2752520 | tf_op jit(solution)/shard_map/ppermute | solution.py:28
  66.4 3.3 %shard_map.125 = (bf16[192,1536]{1,0:T(8,128)(2,1)S(1)}, bf16[192,1536]{1,0:T(8,128)(2,1)S(1)}, bf16[1024,3584]{1,0:T(8,128)(2,1)}) custom-call(bf16[128,3584]{1,0:T(8,128)(2,1)S(1)} %collective-permute-done.before.refs_0_, bf16[64,3584]{1,0:T(8,128)(2,1)S(1)} %collective-permute-done.8.refs_1_, ...), custom_call_target="tpu_custom_call", output_to_operand_aliasing={{2}: (7, {})} | custom-call | flops 1 | bytes 1 | tf_op jit(solution)/shard_map/pallas_call | solution.py:53
  72.5 3.1 %shard_map.126 = (bf16[128,1920]{1,0:T(8,128)(2,1)S(1)}, bf16[128,1920]{1,0:T(8,128)(2,1)S(1)}, bf16[1024,512]{1,0:T(8,128)(2,1)}, bf16[1024,1024]{1,0:T(8,128)(2,1)}) custom-call(bf16[64,1536]{1,0:T(8,128)(2,1)S(1)} %get-tuple-element.127.refs_0_, bf16[64,1536]{1,0:T(8,128)(2,1)} %collective-permute-done.4.refs_1_, ...), custom_call_target="tpu_custom_call" | custom-call | flops 1 | bytes 1 | tf_op jit(solution)/shard_map/pallas_call | solution.py:53
  75.6 6.9 %collective-permute-done.12.before.refs_0_ = bf16[128,3584]{1,0:T(8,128)(2,1)S(1)} collective-permute-done((bf16[128,3584]{1,0:T(8,128)(2,1)}, bf16[128,3584]{1,0:T(8,128)(2,1)S(1)}, u32[]{:S(2)}, u32[]{:S(2)}) %collective-permute-start.12) | collective-permute-done | bytes 917536 | tf_op jit(solution)/shard_map/ppermute | solution.py:28
  83.3 2.7 %collective-permute-start.15 = (bf16[64,3584]{1,0:T(8,128)(2,1)S(1)}, bf16[64,3584]{1,0:T(8,128)(2,1)S(1)}, u32[]{:S(2)}, u32[]{:S(2)}) collective-permute-start(bf16[64,3584]{1,0:T(8,128)(2,1)S(1)} %get-tuple-element.174), channel_id=1, source_target_pairs={{0,3},{1,0},{2,1},{3,2},{4,7},{5,4},{6,5},{7,6},{8,11},{9,8},{10,9... | collective-permute-start | bytes 1376264 | tf_op jit(solution)/shard_map/ppermute | solution.py:28
  86.2 2.1 %collective-permute-start.20 = (bf16[192,1536]{1,0:T(8,128)(2,1)S(1)}, bf16[192,1536]{1,0:T(8,128)(2,1)S(1)}, u32[]{:S(2)}, u32[]{:S(2)}) collective-permute-start(bf16[192,1536]{1,0:T(8,128)(2,1)S(1)} %get-tuple-element.186.refs_0_), channel_id=1, source_target_pairs={{4,8},{8,4},{12,0},{0,12},{5,9},{9,5},{13,1},{1,13},{6,10},{10,6},... | collective-permute-start | bytes 1769480 | tf_op jit(solution)/shard_map/ppermute | solution.py:36
  88.3 4.7 %collective-permute-done.14.refs_1_ = bf16[64,3584]{1,0:T(8,128)(2,1)S(1)} collective-permute-done((bf16[64,3584]{1,0:T(8,128)(2,1)S(1)}, bf16[64,3584]{1,0:T(8,128)(2,1)S(1)}, u32[]{:S(2)}, u32[]{:S(2)}) %collective-permute-start.14) | collective-permute-done | bytes 458784 | tf_op jit(solution)/shard_map/ppermute | solution.py:28
  93.0 3.3 %shard_map.129 = (bf16[192,1536]{1,0:T(8,128)(2,1)S(1)}, bf16[192,1536]{1,0:T(8,128)(2,1)S(1)}, bf16[1024,3584]{1,0:T(8,128)(2,1)}) custom-call(bf16[128,3584]{1,0:T(8,128)(2,1)S(1)} %collective-permute-done.12.before.refs_0_, bf16[64,3584]{1,0:T(8,128)(2,1)S(1)} %collective-permute-done.14.refs_1_, ...), custom_call_target="tpu_custom_call", output_to_operand_aliasing={{2}: (7, {})} | custom-call | flops 20000000000 | bytes 1 | tf_op jit(solution)/shard_map/pallas_call | solution.py:53
  96.7 2.4 %collective-permute-start.19 = (bf16[192,1536]{1,0:T(8,128)(2,1)S(1)}, bf16[192,1536]{1,0:T(8,128)(2,1)S(1)}, u32[]{:S(2)}, u32[]{:S(2)}) collective-permute-start(bf16[192,1536]{1,0:T(8,128)(2,1)S(1)} %get-tuple-element.185.bottom), channel_id=1, source_target_pairs={{4,8},{8,4},{12,0},{0,12},{5,9},{9,5},{13,1},{1,13},{6,10},{10,6},... | collective-permute-start | bytes 1769480 | tf_op jit(solution)/shard_map/ppermute | solution.py:36
  99.1 2.8 %shard_map.130 = (bf16[128,1920]{1,0:T(8,128)(2,1)S(1)}, bf16[128,1920]{1,0:T(8,128)(2,1)S(1)}, bf16[128,1920]{1,0:T(8,128)(2,1)S(1)}, bf16[1024,512]{1,0:T(8,128)(2,1)}, bf16[1024,1024]{1,0:T(8,128)(2,1)}) custom-call(bf16[192,1536]{1,0:T(8,128)(2,1)S(1)} %get-tuple-element.186.refs_0_, ...), custom_call_target="tpu_custom_call", output_to_operand_aliasing={{3}: (6, {}), {4}: (7, {})} | custom-call | flops 1 | bytes 1 | tf_op jit(solution)/shard_map/pallas_call | solution.py:53
  101.9 2.5 %collective-permute-start.24 = (bf16[128,1920]{1,0:T(8,128)(2,1)S(1)}, bf16[128,1920]{1,0:T(8,128)(2,1)S(1)}, u32[]{:S(2)}, u32[]{:S(2)}) collective-permute-start(bf16[128,1920]{1,0:T(8,128)(2,1)S(1)} %get-tuple-element.198), channel_id=1, source_target_pairs={{0,3},{1,0},{2,1},{3,2},{4,7},{5,4},{6,5},{7,6},{8,11},{9,8},{10,9... | collective-permute-start | bytes 1474568 | tf_op jit(solution)/shard_map/ppermute | solution.py:28
  105.6 6.2 %collective-permute-done.18.top_in = bf16[192,1536]{1,0:T(8,128)(2,1)S(1)} collective-permute-done((bf16[192,1536]{1,0:T(8,128)(2,1)S(1)}, bf16[192,1536]{1,0:T(8,128)(2,1)S(1)}, u32[]{:S(2)}, u32[]{:S(2)}) %collective-permute-start.18) | collective-permute-done | bytes 589856 | tf_op jit(solution)/shard_map/ppermute | solution.py:36
  116.4 2.7 %collective-permute-done.25.second = bf16[128,1920]{1,0:T(8,128)(2,1)S(1)} collective-permute-done((bf16[128,1920]{1,0:T(8,128)(2,1)S(1)}, bf16[128,1920]{1,0:T(8,128)(2,1)S(1)}, u32[]{:S(2)}, u32[]{:S(2)}) %collective-permute-start.25) | collective-permute-done | bytes 491552 | tf_op jit(solution)/shard_map/ppermute | solution.py:28
  120.1 4.4 %collective-permute-done.22.refs_1_ = bf16[192,1536]{1,0:T(8,128)(2,1)S(1)} collective-permute-done((bf16[192,1536]{1,0:T(8,128)(2,1)S(1)}, bf16[192,1536]{1,0:T(8,128)(2,1)S(1)}, u32[]{:S(2)}, u32[]{:S(2)}) %collective-permute-start.22) | collective-permute-done | bytes 589856 | tf_op jit(solution)/shard_map/ppermute | solution.py:36
  125.7 3.8 %shard_map.133 = (bf16[128,1920]{1,0:T(8,128)(2,1)}, bf16[128,1920]{1,0:T(8,128)(2,1)}, bf16[128,1920]{1,0:T(8,128)(2,1)}, bf16[1024,512]{1,0:T(8,128)(2,1)}, bf16[1024,1024]{1,0:T(8,128)(2,1)}) custom-call(bf16[192,1536]{1,0:T(8,128)(2,1)S(1)} %get-tuple-element.205.refs_0_, ...), custom_call_target="tpu_custom_call", output_to_operand_aliasing={{3}: (6, {}), {4}: (7, {})} | custom-call | flops 1 | bytes 1 | tf_op jit(solution)/shard_map/pallas_call | solution.py:53
  131.4 9.1 %all-to-all-start.2 = ((bf16[8,16,1920]{2,1,0:T(8,128)(2,1)}), bf16[8,16,1920]{2,1,0:T(8,128)(2,1)S(1)}, u32[]{:S(2)}, u32[]{:S(2)}) async-start(bf16[8,16,1920]{2,1,0:T(8,128)(2,1)} %bitcast.41), calls=%async_computation.2 | async-start | bytes 983040 | tf_op jit(solution)/shard_map/all_to_all | solution.py:48
  140.5 5.8 %fusion.9 = bf16[1792,512]{1,0:T(8,128)(2,1)} fusion(bf16[1024,3584]{1,0:T(8,128)(2,1)} %get-tuple-element.220, bf16[1024,1024]{1,0:T(8,128)(2,1)} %get-tuple-element.221), kind=kOutput, calls=%fused_computation.7 | convolution fusion | flops 1879965696 | bytes 6553600 | tf_op jit(solution)/shard_map/dot_general | solution.py:23
  146.3 5.4 %fusion.6 = bf16[1792,512]{1,0:T(8,128)(2,1)} fusion(bf16[1024,3584]{1,0:T(8,128)(2,1)} %get-tuple-element.220, bf16[1024,1024]{1,0:T(8,128)(2,1)S(1)} %copy-done.3), kind=kOutput, calls=%fused_computation.6 | convolution fusion | flops 1879965696 | bytes 6553600 | tf_op jit(solution)/shard_map/dot_general | solution.py:23
  155.5 4.6 %all-to-all-start.3 = ((bf16[8,16,1920]{2,1,0:T(8,128)(2,1)}), bf16[8,16,1920]{2,1,0:T(8,128)(2,1)S(1)}, u32[]{:S(2)}, u32[]{:S(2)}) async-start(bf16[8,16,1920]{2,1,0:T(8,128)(2,1)} %bitcast.16), calls=%async_computation.3 | async-start | bytes 983040 | tf_op jit(solution)/shard_map/all_to_all | solution.py:48
  160.2 5.8 %fusion.12 = bf16[512,1792]{1,0:T(8,128)(2,1)} fusion(bf16[1024,512]{1,0:T(8,128)(2,1)} %get-tuple-element.228, bf16[1024,3584]{1,0:T(8,128)(2,1)} %get-tuple-element.220), kind=kOutput, calls=%fused_computation.8 | convolution fusion | flops 1879965696 | bytes 6553600 | tf_op jit(solution)/shard_map/dot_general | solution.py:23
  166.0 3.3 %all-to-all-done.3 = bf16[8,16,1920]{2,1,0:T(8,128)(2,1)S(1)} async-done(((bf16[8,16,1920]{2,1,0:T(8,128)(2,1)}), bf16[8,16,1920]{2,1,0:T(8,128)(2,1)S(1)}, u32[]{:S(2)}, u32[]{:S(2)}) %all-to-all-start.3) | async-done | bytes 491552 | tf_op jit(solution)/shard_map/all_to_all | solution.py:48
  169.3 2.7 %shard_map.135 = (bf16[512,1792]{1,0:T(8,128)(2,1)}, f32[8,32]{1,0:T(8,128)}) custom-call(s32[8,32]{1,0:T(8,128)S(1)} %get-tuple-element.242.usable, f32[8,32]{1,0:T(8,128)S(1)} %bitcast_convert_fusion.score, bf16[128,512]{1,0:T(8,128)(2,1)S(1)} %bitcast.38, bf16[128,512]{1,0:T(8,128)(2,1)S(1)} %bitcast.40, bf16[128,1920]{1,0:T(8,128)(2,1)S(1)} %bitcast.35, ...), custom_call_target="tpu_custom_call" | custom-call | flops 1 | bytes 1 | tf_op jit(solution)/shard_map/pallas_call | solution.py:53
  (80 shorter events, 38.5 us)
Async XLA Ops:
  5.3 19.5 %all-to-all-start = ((bf16[8,16,3584]{2,1,0:T(8,128)(2,1)}), bf16[8,16,3584]{2,1,0:T(8,128)(2,1)S(1)}, u32[]{:S(2)}, u32[]{:S(2)}) async-start(bf16[8,16,3584]{2,1,0:T(8,128)(2,1)} %bitcast.52), calls=%async_computation | async-start | bytes 1835008 | tf_op jit(solution)/shard_map/all_to_all | solution.py:48
  24.8 23.7 %collective-permute-start = (bf16[128,3584]{1,0:T(8,128)(2,1)S(1)}, bf16[128,3584]{1,0:T(8,128)(2,1)S(1)}, u32[]{:S(2)}, u32[]{:S(2)}) collective-permute-start(bf16[128,3584]{1,0:T(8,128)(2,1)S(1)} %bitcast.32), channel_id=1, source_target_pairs={{0,1},{1,2},{2,3},{3,0},{4,5},{5,6},{6,7},{7,4},{8,9},{9,10},{10,1... | collective-permute-start | bytes 2752520 | tf_op jit(solution)/shard_map/ppermute | solution.py:28
  26.5 22.0 %collective-permute-start.1 = (bf16[128,3584]{1,0:T(8,128)(2,1)S(1)}, bf16[128,3584]{1,0:T(8,128)(2,1)S(1)}, u32[]{:S(2)}, u32[]{:S(2)}) collective-permute-start(bf16[128,3584]{1,0:T(8,128)(2,1)S(1)} %bitcast.33), channel_id=1, source_target_pairs={{0,3},{1,0},{2,1},{3,2},{4,7},{5,4},{6,5},{7,6},{8,11},{9,8},{10,9... | collective-permute-start | bytes 2752520 | tf_op jit(solution)/shard_map/ppermute | solution.py:28
  28.6 19.9 %all-to-all-start.1 = ((bf16[8,16,3584]{2,1,0:T(8,128)(2,1)}), bf16[8,16,3584]{2,1,0:T(8,128)(2,1)}, u32[]{:S(2)}, u32[]{:S(2)}) async-start(bf16[8,16,3584]{2,1,0:T(8,128)(2,1)} %bitcast.51), calls=%async_computation.1 | async-start | bytes 1835008 | tf_op jit(solution)/shard_map/all_to_all | solution.py:48
  37.8 6.6 %collective-permute-start.2 = (bf16[64,1536]{1,0:T(8,128)(2,1)S(1)}, bf16[64,1536]{1,0:T(8,128)(2,1)S(1)}, u32[]{:S(2)}, u32[]{:S(2)}) collective-permute-start(bf16[64,1536]{1,0:T(8,128)(2,1)S(1)} %get-tuple-element.123.top), channel_id=1, source_target_pairs={{0,4},{4,0},{8,12},{12,8},{1,5},{5,1},{9,13},{13,9},{2,6},{6,2},{1... | collective-permute-start | bytes 589832 | tf_op jit(solution)/shard_map/ppermute | solution.py:36
  39.1 7.4 %collective-permute-start.3 = (bf16[64,1536]{1,0:T(8,128)(2,1)S(1)}, bf16[64,1536]{1,0:T(8,128)(2,1)S(1)}, u32[]{:S(2)}, u32[]{:S(2)}) collective-permute-start(bf16[64,1536]{1,0:T(8,128)(2,1)S(1)} %get-tuple-element.124.bottom), channel_id=1, source_target_pairs={{4,8},{8,4},{12,0},{0,12},{5,9},{9,5},{13,1},{1,13},{6,10},{10,6},... | collective-permute-start | bytes 589832 | tf_op jit(solution)/shard_map/ppermute | solution.py:36
  46.6 9.2 %collective-permute-start.4 = (bf16[64,1536]{1,0:T(8,128)(2,1)S(1)}, bf16[64,1536]{1,0:T(8,128)(2,1)}, u32[]{:S(2)}, u32[]{:S(2)}) collective-permute-start(bf16[64,1536]{1,0:T(8,128)(2,1)S(1)} %get-tuple-element.127.refs_0_), channel_id=1, source_target_pairs={{4,8},{8,4},{12,0},{0,12},{5,9},{9,5},{13,1},{1,13},{6,10},{10,6},... | collective-permute-start | bytes 589832 | tf_op jit(solution)/shard_map/ppermute | solution.py:36
  48.5 7.3 %collective-permute-start.5 = (bf16[64,1536]{1,0:T(8,128)(2,1)S(1)}, bf16[64,1536]{1,0:T(8,128)(2,1)}, u32[]{:S(2)}, u32[]{:S(2)}) collective-permute-start(bf16[64,1536]{1,0:T(8,128)(2,1)S(1)} %get-tuple-element.128.refs_2_), channel_id=1, source_target_pairs={{0,4},{4,0},{8,12},{12,8},{1,5},{5,1},{9,13},{13,9},{2,6},{6,2},{1... | collective-permute-start | bytes 589832 | tf_op jit(solution)/shard_map/ppermute | solution.py:36
  49.1 12.6 %collective-permute-start.8 = (bf16[64,3584]{1,0:T(8,128)(2,1)S(1)}, bf16[64,3584]{1,0:T(8,128)(2,1)S(1)}, u32[]{:S(2)}, u32[]{:S(2)}) collective-permute-start(bf16[64,3584]{1,0:T(8,128)(2,1)S(1)} %get-tuple-element.133), channel_id=1, source_target_pairs={{0,1},{1,2},{2,3},{3,0},{4,5},{5,6},{6,7},{7,4},{8,9},{9,10},{10,1... | collective-permute-start | bytes 1376264 | tf_op jit(solution)/shard_map/ppermute | solution.py:28
  49.4 12.2 %collective-permute-start.9 = (bf16[64,3584]{1,0:T(8,128)(2,1)S(1)}, bf16[64,3584]{1,0:T(8,128)(2,1)S(1)}, u32[]{:S(2)}, u32[]{:S(2)}) collective-permute-start(bf16[64,3584]{1,0:T(8,128)(2,1)S(1)} %get-tuple-element.142), channel_id=1, source_target_pairs={{0,3},{1,0},{2,1},{3,2},{4,7},{5,4},{6,5},{7,6},{8,11},{9,8},{10,9... | collective-permute-start | bytes 1376264 | tf_op jit(solution)/shard_map/ppermute | solution.py:28
  55.8 8.6 %collective-permute-start.6 = (bf16[64,1536]{1,0:T(8,128)(2,1)S(1)}, bf16[64,1536]{1,0:T(8,128)(2,1)S(1)}, u32[]{:S(2)}, u32[]{:S(2)}) collective-permute-start(bf16[64,1536]{1,0:T(8,128)(2,1)S(1)} %get-tuple-element.152.top), channel_id=1, source_target_pairs={{0,4},{4,0},{8,12},{12,8},{1,5},{5,1},{9,13},{13,9},{2,6},{6,2},{1... | collective-permute-start | bytes 589832 | tf_op jit(solution)/shard_map/ppermute | solution.py:36
  57.3 7.1 %collective-permute-start.7 = (bf16[64,1536]{1,0:T(8,128)(2,1)S(1)}, bf16[64,1536]{1,0:T(8,128)(2,1)S(1)}, u32[]{:S(2)}, u32[]{:S(2)}) collective-permute-start(bf16[64,1536]{1,0:T(8,128)(2,1)S(1)} %get-tuple-element.141.bottom), channel_id=1, source_target_pairs={{4,8},{8,4},{12,0},{0,12},{5,9},{9,5},{13,1},{1,13},{6,10},{10,6},... | collective-permute-start | bytes 589832 | tf_op jit(solution)/shard_map/ppermute | solution.py:36
  61.7 20.8 %collective-permute-start.12 = (bf16[128,3584]{1,0:T(8,128)(2,1)}, bf16[128,3584]{1,0:T(8,128)(2,1)S(1)}, u32[]{:S(2)}, u32[]{:S(2)}) collective-permute-start(bf16[128,3584]{1,0:T(8,128)(2,1)} %bitcast.13.refs_0_), channel_id=1, source_target_pairs={{0,1},{1,2},{2,3},{3,0},{4,5},{5,6},{6,7},{7,4},{8,9},{9,10},{10,1... | collective-permute-start | bytes 2752520 | tf_op jit(solution)/shard_map/ppermute | solution.py:28
  61.7 20.7 %collective-permute-start.13 = (bf16[128,3584]{1,0:T(8,128)(2,1)}, bf16[128,3584]{1,0:T(8,128)(2,1)S(1)}, u32[]{:S(2)}, u32[]{:S(2)}) collective-permute-start(bf16[128,3584]{1,0:T(8,128)(2,1)} %bitcast.13.refs_0_), channel_id=1, source_target_pairs={{0,3},{1,0},{2,1},{3,2},{4,7},{5,4},{6,5},{7,6},{8,11},{9,8},{10,9... | collective-permute-start | bytes 2752520 | tf_op jit(solution)/shard_map/ppermute | solution.py:28
  71.2 14.7 %collective-permute-start.16 = (bf16[192,1536]{1,0:T(8,128)(2,1)S(1)}, bf16[192,1536]{1,0:T(8,128)(2,1)S(1)}, u32[]{:S(2)}, u32[]{:S(2)}) collective-permute-start(bf16[192,1536]{1,0:T(8,128)(2,1)S(1)} %get-tuple-element.175.top), channel_id=1, source_target_pairs={{0,4},{4,0},{8,12},{12,8},{1,5},{5,1},{9,13},{13,9},{2,6},{6,2},{1... | collective-permute-start | bytes 1769480 | tf_op jit(solution)/shard_map/ppermute | solution.py:36
  71.3 14.6 %collective-permute-start.17 = (bf16[192,1536]{1,0:T(8,128)(2,1)S(1)}, bf16[192,1536]{1,0:T(8,128)(2,1)S(1)}, u32[]{:S(2)}, u32[]{:S(2)}) collective-permute-start(bf16[192,1536]{1,0:T(8,128)(2,1)S(1)} %get-tuple-element.176.bottom), channel_id=1, source_target_pairs={{4,8},{8,4},{12,0},{0,12},{5,9},{9,5},{13,1},{1,13},{6,10},{10,6},... | collective-permute-start | bytes 1769480 | tf_op jit(solution)/shard_map/ppermute | solution.py:36
  83.0 10.0 %collective-permute-start.14 = (bf16[64,3584]{1,0:T(8,128)(2,1)S(1)}, bf16[64,3584]{1,0:T(8,128)(2,1)S(1)}, u32[]{:S(2)}, u32[]{:S(2)}) collective-permute-start(bf16[64,3584]{1,0:T(8,128)(2,1)S(1)} %get-tuple-element.173), channel_id=1, source_target_pairs={{0,1},{1,2},{2,3},{3,0},{4,5},{5,6},{6,7},{7,4},{8,9},{9,10},{10,1... | collective-permute-start | bytes 1376264 | tf_op jit(solution)/shard_map/ppermute | solution.py:28
  83.3 9.7 %collective-permute-start.15 = (bf16[64,3584]{1,0:T(8,128)(2,1)S(1)}, bf16[64,3584]{1,0:T(8,128)(2,1)S(1)}, u32[]{:S(2)}, u32[]{:S(2)}) collective-permute-start(bf16[64,3584]{1,0:T(8,128)(2,1)S(1)} %get-tuple-element.174), channel_id=1, source_target_pairs={{0,3},{1,0},{2,1},{3,2},{4,7},{5,4},{6,5},{7,6},{8,11},{9,8},{10,9... | collective-permute-start | bytes 1376264 | tf_op jit(solution)/shard_map/ppermute | solution.py:28
  86.2 12.9 %collective-permute-start.20 = (bf16[192,1536]{1,0:T(8,128)(2,1)S(1)}, bf16[192,1536]{1,0:T(8,128)(2,1)S(1)}, u32[]{:S(2)}, u32[]{:S(2)}) collective-permute-start(bf16[192,1536]{1,0:T(8,128)(2,1)S(1)} %get-tuple-element.186.refs_0_), channel_id=1, source_target_pairs={{4,8},{8,4},{12,0},{0,12},{5,9},{9,5},{13,1},{1,13},{6,10},{10,6},... | collective-permute-start | bytes 1769480 | tf_op jit(solution)/shard_map/ppermute | solution.py:36
  88.3 10.8 %collective-permute-start.21 = (bf16[192,1536]{1,0:T(8,128)(2,1)S(1)}, bf16[192,1536]{1,0:T(8,128)(2,1)S(1)}, u32[]{:S(2)}, u32[]{:S(2)}) collective-permute-start(bf16[192,1536]{1,0:T(8,128)(2,1)S(1)} %get-tuple-element.189.refs_2_), channel_id=1, source_target_pairs={{0,4},{4,0},{8,12},{12,8},{1,5},{5,1},{9,13},{13,9},{2,6},{6,2},{1... | collective-permute-start | bytes 1769480 | tf_op jit(solution)/shard_map/ppermute | solution.py:36
  96.3 15.5 %collective-permute-start.18 = (bf16[192,1536]{1,0:T(8,128)(2,1)S(1)}, bf16[192,1536]{1,0:T(8,128)(2,1)S(1)}, u32[]{:S(2)}, u32[]{:S(2)}) collective-permute-start(bf16[192,1536]{1,0:T(8,128)(2,1)S(1)} %get-tuple-element.184.top), channel_id=1, source_target_pairs={{0,4},{4,0},{8,12},{12,8},{1,5},{5,1},{9,13},{13,9},{2,6},{6,2},{1... | collective-permute-start | bytes 1769480 | tf_op jit(solution)/shard_map/ppermute | solution.py:36
  96.7 15.7 %collective-permute-start.19 = (bf16[192,1536]{1,0:T(8,128)(2,1)S(1)}, bf16[192,1536]{1,0:T(8,128)(2,1)S(1)}, u32[]{:S(2)}, u32[]{:S(2)}) collective-permute-start(bf16[192,1536]{1,0:T(8,128)(2,1)S(1)} %get-tuple-element.185.bottom), channel_id=1, source_target_pairs={{4,8},{8,4},{12,0},{0,12},{5,9},{9,5},{13,1},{1,13},{6,10},{10,6},... | collective-permute-start | bytes 1769480 | tf_op jit(solution)/shard_map/ppermute | solution.py:36
  101.9 14.5 %collective-permute-start.24 = (bf16[128,1920]{1,0:T(8,128)(2,1)S(1)}, bf16[128,1920]{1,0:T(8,128)(2,1)S(1)}, u32[]{:S(2)}, u32[]{:S(2)}) collective-permute-start(bf16[128,1920]{1,0:T(8,128)(2,1)S(1)} %get-tuple-element.198), channel_id=1, source_target_pairs={{0,3},{1,0},{2,1},{3,2},{4,7},{5,4},{6,5},{7,6},{8,11},{9,8},{10,9... | collective-permute-start | bytes 1474568 | tf_op jit(solution)/shard_map/ppermute | solution.py:28
  104.4 14.8 %collective-permute-start.25 = (bf16[128,1920]{1,0:T(8,128)(2,1)S(1)}, bf16[128,1920]{1,0:T(8,128)(2,1)S(1)}, u32[]{:S(2)}, u32[]{:S(2)}) collective-permute-start(bf16[128,1920]{1,0:T(8,128)(2,1)S(1)} %get-tuple-element.199), channel_id=1, source_target_pairs={{0,1},{1,2},{2,3},{3,0},{4,5},{5,6},{6,7},{7,4},{8,9},{9,10},{10,1... | collective-permute-start | bytes 1474568 | tf_op jit(solution)/shard_map/ppermute | solution.py:28
  104.4 15.3 %collective-permute-start.26 = (bf16[128,1920]{1,0:T(8,128)(2,1)S(1)}, bf16[128,1920]{1,0:T(8,128)(2,1)S(1)}, u32[]{:S(2)}, u32[]{:S(2)}) collective-permute-start(bf16[128,1920]{1,0:T(8,128)(2,1)S(1)} %get-tuple-element.193), channel_id=1, source_target_pairs={{0,2},{1,3},{2,0},{3,1},{4,6},{5,7},{6,4},{7,5},{8,10},{9,11},{10,... | collective-permute-start | bytes 1474568 | tf_op jit(solution)/shard_map/ppermute | solution.py:28
  112.7 11.8 %collective-permute-start.22 = (bf16[192,1536]{1,0:T(8,128)(2,1)S(1)}, bf16[192,1536]{1,0:T(8,128)(2,1)S(1)}, u32[]{:S(2)}, u32[]{:S(2)}) collective-permute-start(bf16[192,1536]{1,0:T(8,128)(2,1)S(1)} %get-tuple-element.205.refs_0_), channel_id=1, source_target_pairs={{4,8},{8,4},{12,0},{0,12},{5,9},{9,5},{13,1},{1,13},{6,10},{10,6},... | collective-permute-start | bytes 1769480 | tf_op jit(solution)/shard_map/ppermute | solution.py:36
  114.7 11.0 %collective-permute-start.23 = (bf16[192,1536]{1,0:T(8,128)(2,1)S(1)}, bf16[192,1536]{1,0:T(8,128)(2,1)S(1)}, u32[]{:S(2)}, u32[]{:S(2)}) collective-permute-start(bf16[192,1536]{1,0:T(8,128)(2,1)S(1)} %get-tuple-element.207.refs_2_), channel_id=1, source_target_pairs={{0,4},{4,0},{8,12},{12,8},{1,5},{5,1},{9,13},{13,9},{2,6},{6,2},{1... | collective-permute-start | bytes 1769480 | tf_op jit(solution)/shard_map/ppermute | solution.py:36
  129.5 22.2 %collective-permute-start.29 = (bf16[128,1920]{1,0:T(8,128)(2,1)}, bf16[128,1920]{1,0:T(8,128)(2,1)S(1)}, u32[]{:S(2)}, u32[]{:S(2)}) collective-permute-start(bf16[128,1920]{1,0:T(8,128)(2,1)} %get-tuple-element.215), channel_id=1, source_target_pairs={{0,2},{1,3},{2,0},{3,1},{4,6},{5,7},{6,4},{7,5},{8,10},{9,11},{10,... | collective-permute-start | bytes 1474568 | tf_op jit(solution)/shard_map/ppermute | solution.py:28
  129.9 23.0 %collective-permute-start.27 = (bf16[128,1920]{1,0:T(8,128)(2,1)}, bf16[128,1920]{1,0:T(8,128)(2,1)S(1)}, u32[]{:S(2)}, u32[]{:S(2)}) collective-permute-start(bf16[128,1920]{1,0:T(8,128)(2,1)} %get-tuple-element.211), channel_id=1, source_target_pairs={{0,3},{1,0},{2,1},{3,2},{4,7},{5,4},{6,5},{7,6},{8,11},{9,8},{10,9... | collective-permute-start | bytes 1474568 | tf_op jit(solution)/shard_map/ppermute | solution.py:28
  131.3 23.0 %collective-permute-start.28 = (bf16[128,1920]{1,0:T(8,128)(2,1)}, bf16[128,1920]{1,0:T(8,128)(2,1)S(1)}, u32[]{:S(2)}, u32[]{:S(2)}) collective-permute-start(bf16[128,1920]{1,0:T(8,128)(2,1)} %get-tuple-element.212), channel_id=1, source_target_pairs={{0,1},{1,2},{2,3},{3,0},{4,5},{5,6},{6,7},{7,4},{8,9},{9,10},{10,1... | collective-permute-start | bytes 1474568 | tf_op jit(solution)/shard_map/ppermute | solution.py:28
  131.4 24.1 %all-to-all-start.2 = ((bf16[8,16,1920]{2,1,0:T(8,128)(2,1)}), bf16[8,16,1920]{2,1,0:T(8,128)(2,1)S(1)}, u32[]{:S(2)}, u32[]{:S(2)}) async-start(bf16[8,16,1920]{2,1,0:T(8,128)(2,1)} %bitcast.41), calls=%async_computation.2 | async-start | bytes 983040 | tf_op jit(solution)/shard_map/all_to_all | solution.py:48
  155.5 13.8 %all-to-all-start.3 = ((bf16[8,16,1920]{2,1,0:T(8,128)(2,1)}), bf16[8,16,1920]{2,1,0:T(8,128)(2,1)S(1)}, u32[]{:S(2)}, u32[]{:S(2)}) async-start(bf16[8,16,1920]{2,1,0:T(8,128)(2,1)} %bitcast.16), calls=%async_computation.3 | async-start | bytes 983040 | tf_op jit(solution)/shard_map/all_to_all | solution.py:48
  (9 other events, 51.3 us)
